TPU v7x, 256 devices: a whole 4x4x8 slice. The times are simulated.
256 devices in a mesh: ctx: 16 (over z_lo, x, core), head: 16 (over y, z_hi).
Axes of the slice: x: 4, y: 4, z: 8 (z_hi: 4, z_lo: 2; z = z_hi * 2 + z_lo), core: 2. Of those that a mesh axis runs over, the one named last changes fastest.
Arguments:
- queries: bfloat16 [4096, 64, 576], P('ctx', 'head'), may hold values from -22 to 22
- latent: bfloat16 [4096, 576], P('ctx'), may hold values from -4 to 4
- grad_out: bfloat16 [4096, 64, 512], P('ctx', 'head'), may hold values from -24 to 24
- advantage: float32 [4096], P('ctx'), may hold values from -4 to 4
- ancestors: int32 [32, 8], P('ctx'), may hold values from -1 to 30, as said below
Outputs:
- query_grad: bfloat16 [4096, 64, 576], P(('ctx', 'head'))
- latent_grad: float32 [4096, 576], P(('ctx', 'head'))
Inputs may be any that keep to these rules, and one draw needn't show every extreme that they name: Row b lists ancestors of block b, nearest first: the first entry is the parent of b, each later entry the parent of the one before; after the chain ends or after 8 entries the row holds -1. Entries are always earlier blocks. Block 30 has as parent the block 16 earlier, and block 31 has block 30 as parent.
All inputs are finite; a program needn't handle non-finite values.
Results may differ from a plain program's by a relative error of at most 0.012.
Values may be sent and summed in bfloat16 or wider, within the bound.
No kernel may reach another device: no remote copies, remote signals or barrier semaphores. Data moves between devices by JAX's collectives and lax.ppermute only.
A program may use at most 128 MiB of HBM per device.

v0:
```python
import jax
import jax.numpy as jnp
from jax import lax
from jax.sharding import PartitionSpec as P

LAT = 512
BLK = 128


SOFTMAX_SCALE = 0.07216878364870322


def block_grads(q_block, g_block, lists, own, key_blocks):
    slots = jnp.concatenate([own[:, None], lists], axis=1)
    present = jnp.concatenate([jnp.ones_like(own[:, None]), (lists >= 0).astype(jnp.int32)], axis=1)
    safe_index = jnp.maximum(slots, 0)
    count_q = slots.shape[0]
    count_s = slots.shape[1]
    width = key_blocks.shape[2]
    keys = key_blocks[safe_index].reshape(count_q, count_s * BLK, width)
    scores = (
        jnp.einsum("qihd,qjd->qhij", q_block, keys, preferred_element_type=jnp.float32)
        * SOFTMAX_SCALE
    )
    column = jnp.arange(count_s * BLK)
    slot_of = column // BLK
    inner = column % BLK
    row_pos = jnp.arange(BLK)
    diagonal = (slot_of[None, :] == 0) & (inner[None, :] <= row_pos[:, None])
    listed = (slot_of[None, :] > 0) & (present[:, slot_of] > 0)
    visible = (diagonal[None, :, :] | listed[:, None, :])[:, None, :, :]
    masked = jnp.where(visible, scores, jnp.float32(-1e30))
    top_score = jnp.max(masked, axis=-1, keepdims=True)
    expo = jnp.where(visible, jnp.exp(masked - top_score), jnp.float32(0.0))
    probs = expo / jnp.sum(expo, axis=-1, keepdims=True)
    probs_low = probs.astype(jnp.bfloat16)
    values = keys[:, :, :LAT]
    dprobs = jnp.einsum("qihc,qjc->qhij", g_block, values, preferred_element_type=jnp.float32)
    delta = jnp.sum(probs * dprobs, axis=-1, keepdims=True)
    dscores = (probs * (dprobs - delta) * SOFTMAX_SCALE).astype(jnp.bfloat16)
    query_part = jnp.einsum(
        "qhij,qjd->qihd", dscores, keys, preferred_element_type=jnp.float32
    ).astype(jnp.bfloat16)
    key_part = jnp.einsum("qhij,qihd->qjd", dscores, q_block, preferred_element_type=jnp.float32)
    value_part = jnp.einsum(
        "qhij,qihc->qjc", probs_low, g_block, preferred_element_type=jnp.float32
    )
    padding = jnp.zeros((count_q, count_s * BLK, width - LAT), jnp.float32)
    contrib = (key_part + jnp.concatenate([value_part, padding], axis=-1)).reshape(
        count_q, count_s, BLK, width
    )
    block_count = key_blocks.shape[0]
    onehot = (
        (safe_index[:, :, None] == jnp.arange(block_count, dtype=jnp.int32)[None, None, :])
        & (present[:, :, None] > 0)
    ).astype(jnp.float32)
    term = jnp.einsum("qsn,qsbd->nbd", onehot, contrib, precision=lax.Precision.HIGHEST)
    return (query_part, term)


def on_device(queries, latent, grad_out, advantage, ancestors):
    gathered = lax.all_gather(latent, "ctx", axis=0, tiled=True)
    token_count, head_count, width = queries.shape
    block_count = gathered.shape[0] // BLK
    local_blocks = token_count // BLK
    key_blocks = gathered.reshape(block_count, BLK, width)
    weighted = (advantage[:, None, None] * grad_out.astype(jnp.float32)).astype(jnp.bfloat16)
    q_blocks = queries.reshape(local_blocks, BLK, head_count, width)
    g_blocks = weighted.reshape(local_blocks, BLK, head_count, LAT)
    own = lax.axis_index("ctx") * local_blocks + jnp.arange(local_blocks, dtype=jnp.int32)
    query_part, term = block_grads(q_blocks, g_blocks, ancestors, own, key_blocks)
    query_rows = query_part.reshape(token_count, head_count, width)
    query_grad = lax.all_to_all(query_rows, "head", split_axis=0, concat_axis=1, tiled=True)
    flat_term = term.reshape(block_count * BLK, width)
    partial_rows = lax.psum_scatter(flat_term, "ctx", scatter_dimension=0, tiled=True)
    latent_grad = lax.psum_scatter(partial_rows, "head", scatter_dimension=0, tiled=True)
    return (query_grad, latent_grad)


def solution(mesh):
    in_specs = (
        P("ctx", "head", None),
        P("ctx", None),
        P("ctx", "head", None),
        P("ctx"),
        P("ctx", None),
    )
    out_specs = (P(("ctx", "head"), None, None), P(("ctx", "head"), None))
    return jax.shard_map(
        on_device, mesh=mesh, in_specs=in_specs, out_specs=out_specs, check_vma=False
    )
```

profile of v0, /device:TPU:40, one launch (start us, length us, event | category | flops | bytes accessed | tf_op | source)
XLA Modules:
  0.0 347.3 jit_solution(3909787384259314358)
XLA Ops:
  7.2 0.0 copy-start
  7.2 0.0 copy-start.2
  7.2 0.0 all-gather.2.cloned.1.call-start
  7.2 0.7 all-gather.2.cloned.1.call-update
  7.9 0.0 reduce-scatter.3.cloned.1.call-start
  8.0 0.8 add_maximum_fusion
  8.7 0.1 reshape.201
  8.8 0.7 broadcast_compare_fusion.1
  9.5 0.1 broadcast_compare_fusion
  9.6 0.1 copy.122
  9.7 2.4 gather_fusion.1
  12.2 0.2 and_bitcast_fusion
  12.4 0.2 copy.123
  12.7 1.7 multiply_convert_fusion
  14.4 1.0 copy.136
  15.4 0.0 copy-done.2
  15.4 0.1 add_maximum_fusion.1
  15.5 0.9 fusion.20
  16.4 0.5 broadcast_or_fusion
  16.9 45.0 %all-gather.2.cloned.1.call-done = bf16[4096,576]{0,1:T(8,128)(2,1)} async-done(((bf16[256,576]{0,1:T(8,128)(2,1)}), bf16[4096,576]{0,1:T(8,128)(2,1)}) %all-gather.2.cloned.1.call-update) | async-done | bytes 4718608 | tf_op jit(solution)/shard_map/all_gather | solution.py:62
  61.9 5.8 %copy_bitcast_fusion = bf16[32,128,576]{1,2,0:T(8,128)(2,1)} fusion(bf16[4096,576]{0,1:T(8,128)(2,1)} %all-gather.2.cloned.1.call-done), kind=kLoop, calls=%fused_computation.10 | loop fusion | bytes 9437184 | tf_op jit(solution)/shard_map/reshape | solution.py:66
  67.7 5.0 %gather_fusion = bf16[18,128,576]{1,2,0:T(8,128)(2,1)} fusion(bf16[32,128,576]{1,2,0:T(8,128)(2,1)} %copy_bitcast_fusion, s32[1024]{0:T(1024)S(1)} %pad_clamp_fusion.1), kind=kCustom, calls=%fused_computation | custom fusion | bytes 5308488 | tf_op jit(solution)/shard_map/gather | solution.py:20
  72.6 4.5 %copy.121 = bf16[18,128,576]{2,1,0:T(8,128)(2,1)} copy(bf16[18,128,576]{1,2,0:T(8,128)(2,1)} %gather_fusion) | data formatting | bytes 5308416 | tf_op jit(solution)/shard_map/gather | solution.py:20
  77.1 5.2 %fusion.9 = f32[2,1152,128,4]{2,1,3,0:T(8,128)} fusion(bf16[2,128,4,512]{1,3,2,0:T(8,128)(2,1)S(1)} %copy.136, bf16[2,1152,576]{2,1,0:T(8,128)(2,1)} %bitcast.104), kind=kOutput, calls=%fused_computation.20 | convolution fusion | flops 1207959552 | bytes 8126464 | tf_op jit(solution)/shard_map/qihc,qjc->qhij/dot_general | solution.py:38
  82.3 0.0 copy-done
  82.3 7.1 %fusion.42 = (f32[2,4,128]{2,1,0:T(4,128)S(1)}, f32[2,4,128,1152]{2,3,1,0:T(8,128)}) fusion(pred[2,128,1152]{1,2,0:T(8,128)(4,1)S(1)} %broadcast_or_fusion, bf16[2,1152,576,1]{2,1,3,0:T(8,128)(2,1)} %bitcast.105, bf16[256,4,576]{0,2,1:T(8,128)(2,1)S(1)} %copy-done), kind=kOutput, calls=%fused_computation.75 | convolution fusion | flops 1364853888 | bytes 8851456 | tf_op jit(solution)/shard_map/sub | solution.py:34
  89.5 6.1 %convolution_bitcast_fusion = f32[2,1152,512]{1,2,0:T(8,128)} fusion(bf16[2,128,4,512]{1,3,2,0:T(8,128)(2,1)S(1)} %copy.136, f32[2,4,128,1152]{2,3,1,0:T(8,128)} %get-tuple-element.13, f32[2,4,128]{2,1,0:T(4,128)S(1)} %get-tuple-element.12), kind=kOutput, calls=%fused_computation.16 | convolution fusion | flops 1210318848 | bytes 10489856 | tf_op jit(solution)/shard_map/qhij,qihc->qjc/dot_general | solution.py:45
  95.6 11.1 %bitcast_add_fusion = f32[2,1152,576]{1,2,0:T(8,128)} fusion(f32[2,1152,512]{1,2,0:T(8,128)} %convolution_bitcast_fusion, f32[2,1152,128,4]{2,1,3,0:T(8,128)} %fusion.9, f32[2,4,128,1152]{2,3,1,0:T(8,128)} %get-tuple-element.13, f32[2,4,128]{2,1,0:T(4,128)S(1)} %get-tuple-element.12, bf16[256,4,576]{0,2,1:T(8,128)(2,1)S(1)} %copy-done), kind=kOutput, calls=%fused_computation.5 | convolution fusion | flops 1368541312 | bytes 20647936 | tf_op jit(solution)/shard_map/qhij,qihd->qjd/dot_general | solution.py:44
  106.7 6.5 %copy.137 = f32[2,1152,576]{2,1,0:T(8,128)} copy(f32[2,1152,576]{1,2,0:T(8,128)} %bitcast_add_fusion) | data formatting | bytes 10616832 | tf_op jit(solution)/shard_map/add | solution.py:49
  113.1 11.2 %copy.138 = f32[2,9,128,576]{2,1,0,3:T(8,128)} copy(f32[2,9,128,576]{3,2,1,0:T(8,128)} %bitcast.103) | data formatting | bytes 10616832 | tf_op jit(solution)/shard_map/reshape | solution.py:49
  124.3 9.4 %convolution_bitcast_fusion.1 = f32[32,128,576]{1,0,2:T(8,128)} fusion(f32[2,9,128,576]{2,1,0,3:T(8,128)} %copy.138, s32[2,9]{1,0:T(2,128)S(1)} %add_maximum_fusion.1, pred[2,9]{1,0:T(4,128)(4,1)S(1)} %get-tuple-element.10), kind=kOutput, calls=%fused_computation.18 | convolution fusion | flops 509609088 | bytes 14745690 | tf_op jit(solution)/shard_map/qsn,qsbd->nbd/dot_general | solution.py:57
  133.7 12.0 %copy.155 = f32[32,128,576]{2,1,0:T(8,128)} copy(f32[32,128,576]{1,0,2:T(8,128)} %convolution_bitcast_fusion.1) | data formatting | bytes 18874368 | tf_op jit(solution)/shard_map/reshape | solution.py:74
  145.7 0.0 reduce-scatter.3.cloned.1.call-update
  145.7 9.6 %fusion.15 = bf16[2,128,4,576]{1,3,2,0:T(8,128)(2,1)S(1)} fusion(bf16[2,1152,576,1]{2,1,3,0:T(8,128)(2,1)} %bitcast.106, f32[2,1152,128,4]{2,1,3,0:T(8,128)} %fusion.9, f32[2,4,128,1152]{2,3,1,0:T(8,128)} %get-tuple-element.13, f32[2,4,128]{2,1,0:T(4,128)S(1)} %get-tuple-element.12), kind=kOutput, calls=%fused_computation.28 | convolution fusion | flops 1367804032 | bytes 13275136 | tf_op jit(solution)/shard_map/qhij,qjd->qihd/dot_general | solution.py:41
  155.3 2.3 copy.154
  157.6 9.2 %all-to-all-start = ((bf16[256,4,576]{2,1,0:T(4,128)(2,1)}), bf16[256,4,576]{2,1,0:T(4,128)(2,1)S(1)}, u32[]{:S(2)}, u32[]{:S(2)}) async-start(bf16[256,4,576]{2,1,0:T(4,128)(2,1)} %bitcast.107), calls=%async_computation | async-start | bytes 2621440 | tf_op jit(solution)/shard_map/all_to_all | solution.py:73
  166.8 0.0 copy-start.1
  166.8 0.0 reduce-scatter.5.cloned.1.call-start
  166.8 84.9 %reduce-scatter.3.cloned.1.call-done = f32[256,576]{1,0:T(8,128)} async-done(((f32[4096,576]{1,0:T(8,128)}), f32[256,576]{1,0:T(8,128)}) %reduce-scatter.3.cloned.1.call-update) | async-done | bytes 589840 | tf_op jit(solution)/shard_map/reduce_scatter | solution.py:75
  251.7 0.0 reduce-scatter.5.cloned.1.call-update
  251.8 0.0 all-to-all-done
  251.8 0.2 copy.131
  251.9 0.2 copy.132
  252.1 1.3 copy.140
  253.5 87.3 %reduce-scatter.5.cloned.1.call-done = f32[16,576]{1,0:T(8,128)} async-done(((f32[256,576]{1,0:T(8,128)}), f32[16,576]{1,0:T(8,128)}) %reduce-scatter.5.cloned.1.call-update) | async-done | bytes 36880 | tf_op jit(solution)/shard_map/reduce_scatter | solution.py:76
  340.8 0.0 copy-done.1
  (8 shorter events, 0.1 us)
Async XLA Ops:
  7.2 75.2 %copy-start = (bf16[256,4,576]{0,2,1:T(8,128)(2,1)S(1)}, bf16[256,4,576]{0,2,1:T(8,128)(2,1)}, u32[]{:S(2)}) copy-start(bf16[256,4,576]{0,2,1:T(8,128)(2,1)} %param.5) | copy-start | bytes 3538948
  7.2 8.2 %copy-start.2 = (s32[2,8]{1,0:T(2,128)S(1)}, s32[2,8]{1,0:T(2,128)}, u32[]{:S(2)}) copy-start(s32[2,8]{1,0:T(2,128)} %param.9) | copy-start | bytes 196
  7.2 54.7 %all-gather.2.cloned.1.call-start = ((), (), s32[]{:S(2)}) async-start(), calls=%async_computation.3 | async-start | bytes 5013504 | tf_op jit(solution)/shard_map/all_gather | solution.py:62
  7.9 243.8 %reduce-scatter.3.cloned.1.call-start = ((), (), s32[]{:S(2)}) async-start(), calls=%async_computation.4 | async-start | bytes 11141120 | tf_op jit(solution)/shard_map/reduce_scatter | solution.py:75
  157.6 94.2 %all-to-all-start = ((bf16[256,4,576]{2,1,0:T(4,128)(2,1)}), bf16[256,4,576]{2,1,0:T(4,128)(2,1)S(1)}, u32[]{:S(2)}, u32[]{:S(2)}) async-start(bf16[256,4,576]{2,1,0:T(4,128)(2,1)} %bitcast.107), calls=%async_computation | async-start | bytes 2621440 | tf_op jit(solution)/shard_map/all_to_all | solution.py:73
  166.8 174.0 %copy-start.1 = (bf16[256,4,576]{0,2,1:T(8,128)(2,1)S(1)}, bf16[256,4,576]{0,2,1:T(8,128)(2,1)}, u32[]{:S(2)}) copy-start(bf16[256,4,576]{0,2,1:T(8,128)(2,1)} %param.5) | copy-start | bytes 3538948
  166.8 174.0 %reduce-scatter.5.cloned.1.call-start = ((), (), s32[]{:S(2)}) async-start(), calls=%async_computation.5 | async-start | bytes 696320 | tf_op jit(solution)/shard_map/reduce_scatter | solution.py:76
Sparse Core Ops, SparseCore 0:
  9.8 52.0 all-gather.1
  145.8 105.8 reduce-scatter.2
  255.8 84.9 reduce-scatter.4
where the time goes:
time: 350 us; the launch traced here: 347 us
  waiting for transfers between devices  218 us (62%)
  local copies, waits for them, and re-layouts  52.7 us (15%)
  matrix products  48.4 us (14%)
  between operations  13.9 us (4%)
  starting transfers between devices  9.29 us (3%)
  other arithmetic  5 us (1%)
    reduce_scatter x1, waiting for transfers between devices, on_device(): lax.psum_scatter(partial_rows, 'head', scatter_dimension=0, tiled=True)  87.3 us
    reduce_scatter x1, waiting for transfers between devices, on_device(): lax.psum_scatter(flat_term, 'ctx', scatter_dimension=0, tiled=True)  84.9 us
    all_gather x1, waiting for transfers between devices, on_device(): gathered = lax.all_gather(latent, 'ctx', axis=0, tiled=True)  45 us
    reshape x1, local copies, waits for them, and re-layouts, on_device(): flat_term = term.reshape(block_count * BLK, width)  12 us
    reshape x1, local copies, waits for them, and re-layouts, block_grads(): (key_part + jnp.concatenate([value_part, padding], axis=-1)).reshape(coun...  11.2 us
    dot_general x1, matrix products, block_grads(): jnp.einsum('qhij,qihd->qjd', dscores, q_block, preferred_element_type=jnp...  11.1 us
    dot_general x1, matrix products, block_grads(): jnp.einsum('qhij,qjd->qihd', dscores, keys, preferred_element_type=jnp.fl...  9.56 us
    gather x2, local copies, waits for them, and re-layouts, block_grads(): keys = key_blocks[safe_index].reshape(count_q, count_s * BLK, width)  9.48 us
  transfers between devices with their start and end apart: 4, of which 3 were waited for; matrix products, arithmetic and copies ran while one was open for 6% of the time, Pallas kernels for 0%

commit v1 on v0

v1 whole, which is shorter than its diff:
```python
import jax
import jax.numpy as jnp
from jax import lax
from jax.experimental import pallas as pl
from jax.experimental.pallas import tpu as pltpu
from jax.sharding import Mesh
from jax.sharding import PartitionSpec as P

LAT = 512
QW = 576
BLK = 128
NSLOT = 9
HALF = 16

SOFTMAX_SCALE = 0.07216878364870322
LOG2E = 1.4426950408889634
MASKED = -1e30

SPLIT = (("z_lo", 2), ("x", 4), ("core", 2), ("y", 4), ("z_hi", 4))
CTX = ("z_lo", "x", "core")
HEAD = ("y", "z_hi")


def kernel(info, qt_ref, g_ref, mine_ref, other_ref, dq_ref, keep_ref, send_ref, keys, acc):
    block, pair = pl.program_id(0), pl.program_id(1)

    @pl.when((block == 0) & (pair == 0))
    def _():
        def clear(i, carry):
            acc[i] = jnp.zeros((BLK, QW), jnp.float32)
            return carry

        lax.fori_loop(0, 2 * HALF, clear, 0)

    @pl.when(pair == 0)
    def _():
        for s in range(NSLOT):
            place = info[block, s]
            rows = pl.ds(s * BLK, BLK)

            @pl.when(place < HALF)
            def _():
                keys[rows, :] = mine_ref[place]

            @pl.when(place >= HALF)
            def _():
                keys[rows, :] = other_ref[place - HALF]

    k = keys[...]
    qt = jnp.concatenate([qt_ref[0], qt_ref[1]], axis=1)
    g = g_ref[...].reshape(2 * BLK, LAT)
    nt = (((1,), (1,)), ((), ()))
    scores = jnp.dot(k, qt, preferred_element_type=jnp.float32)
    dprobs = lax.dot_general(k[:, :LAT], g, nt, preferred_element_type=jnp.float32)

    key_pos = lax.broadcasted_iota(jnp.int32, (BLK, 2 * BLK), 0)
    row_pos = lax.broadcasted_iota(jnp.int32, (BLK, 2 * BLK), 1) % BLK
    parts = []
    for s in range(NSLOT):
        part = scores[s * BLK : (s + 1) * BLK] * (SOFTMAX_SCALE * LOG2E)
        if s == 0:
            part = jnp.where(key_pos <= row_pos, part, MASKED)
        else:
            part = jnp.where(info[block, NSLOT + s] > 0, part, MASKED)
        parts.append(part)
    masked = jnp.concatenate(parts, axis=0)
    top = jnp.max(masked, axis=0, keepdims=True)
    expo = jnp.exp2(masked - top)
    probs = expo * (1.0 / jnp.sum(expo, axis=0, keepdims=True))
    delta = jnp.sum(probs * dprobs, axis=0, keepdims=True)
    dscores = (probs * (dprobs - delta) * SOFTMAX_SCALE).astype(jnp.bfloat16)
    low = probs.astype(jnp.bfloat16)

    dq = lax.dot_general(
        dscores, k, (((0,), (0,)), ((), ())), preferred_element_type=jnp.float32
    ).astype(jnp.bfloat16)
    dq_ref[:, 0] = dq[:BLK].reshape(8, 16, QW)
    dq_ref[:, 1] = dq[BLK:].reshape(8, 16, QW)

    key_part = lax.dot_general(dscores, qt, nt, preferred_element_type=jnp.float32)
    value_part = jnp.dot(low, g, preferred_element_type=jnp.float32)
    for s in range(NSLOT):
        place = info[block, s]
        rows = slice(s * BLK, (s + 1) * BLK)
        acc[place, :, :LAT] += key_part[rows, :LAT] + value_part[rows]
        acc[place, :, LAT:] += key_part[rows, LAT:]

    @pl.when((block == 1) & (pair == 1))
    def _():
        def write(i, carry):
            keep_ref[i] = acc[i].astype(jnp.bfloat16)
            send_ref[i] = acc[HALF + i].astype(jnp.bfloat16)
            return carry

        lax.fori_loop(0, HALF, write, 0)


def local_grads(info, qt, weighted, mine, other):
    whole = lambda b, p, info: (0, 0, 0)
    return pl.pallas_call(
        kernel,
        grid_spec=pltpu.PrefetchScalarGridSpec(
            num_scalar_prefetch=1,
            grid=(2, 2),
            in_specs=[
                pl.BlockSpec((2, QW, BLK), lambda b, p, info: (p, 0, b)),
                pl.BlockSpec((2, BLK, LAT), lambda b, p, info: (p, b, 0)),
                pl.BlockSpec((HALF, BLK, QW), whole, pipeline_mode=pl.Buffered(1)),
                pl.BlockSpec((HALF, BLK, QW), whole, pipeline_mode=pl.Buffered(1)),
            ],
            out_specs=[
                pl.BlockSpec((8, 2, 16, QW), lambda b, p, info: (b, p, 0, 0)),
                pl.BlockSpec((HALF, BLK, QW), whole),
                pl.BlockSpec((HALF, BLK, QW), whole),
            ],
            scratch_shapes=[
                pltpu.VMEM((NSLOT * BLK, QW), jnp.bfloat16),
                pltpu.VMEM((2 * HALF, BLK, QW), jnp.float32),
            ],
        ),
        out_shape=[
            jax.ShapeDtypeStruct((16, 4, 16, QW), jnp.bfloat16),
            jax.ShapeDtypeStruct((HALF, BLK, QW), jnp.bfloat16),
            jax.ShapeDtypeStruct((HALF, BLK, QW), jnp.bfloat16),
        ],
        compiler_params=pltpu.CompilerParams(
            dimension_semantics=("arbitrary", "arbitrary"),
            vmem_limit_bytes=56 * 1024 * 1024,
        ),
    )(info, qt, weighted, mine, other)


def swap_cores(a):
    return lax.ppermute(a, "core", [(0, 1), (1, 0)])


def exchange(a, axes):
    return lax.all_to_all(a, axes, split_axis=0, concat_axis=0, tiled=True)


def on_device(queries, latent, grad_out, advantage, ancestors):
    core = lax.axis_index("core")
    mine = exchange(jnp.broadcast_to(latent[None], (8, 256, QW)), ("x", "z_lo"))
    mine = mine.reshape(HALF, BLK, QW)
    other = swap_cores(mine)

    qt = jnp.transpose(queries, (1, 2, 0))
    weighted = (advantage[:, None, None] * grad_out.astype(jnp.float32)).astype(jnp.bfloat16)
    weighted = jnp.transpose(weighted, (1, 0, 2))

    own = lax.axis_index(CTX) * 2 + jnp.arange(2, dtype=jnp.int32)
    slots = jnp.concatenate([own[:, None], ancestors], axis=1)
    present = (slots >= 0).astype(jnp.int32)
    n = jnp.maximum(slots, 0)
    z_lo, x, owner_core, parity = n // 16, (n // 4) % 4, (n // 2) % 2, n % 2
    place = jnp.where(owner_core == core, 0, HALF) + x * 4 + z_lo * 2 + parity
    info = jnp.concatenate([place, present], axis=1)

    dq, keep, send = local_grads(info, qt, weighted, mine, other)

    total = keep.astype(jnp.float32) + swap_cores(send).astype(jnp.float32)
    rows = exchange(total.astype(jnp.bfloat16).reshape(2048, QW), "x")
    rows = jnp.sum(rows.reshape(4, 512, QW).astype(jnp.float32), axis=0).astype(jnp.bfloat16)
    rows = exchange(rows, ("z_lo",) + HEAD)
    latent_grad = jnp.sum(rows.reshape(32, 16, QW).astype(jnp.float32), axis=0)

    dq = exchange(dq, HEAD)
    query_grad = jnp.transpose(dq.reshape(64, 16, QW), (1, 0, 2))
    return query_grad, latent_grad


def solution(mesh):
    names = tuple(name for name, _ in SPLIT)
    sizes = tuple(size for _, size in SPLIT)
    fine = Mesh(mesh.devices.reshape(sizes), names)
    in_specs = (P(CTX, HEAD, None), P(CTX, None), P(CTX, HEAD, None), P(CTX), P(CTX, None))
    out_specs = (P(CTX + HEAD, None, None), P(CTX + HEAD, None))
    return jax.shard_map(
        on_device, mesh=fine, in_specs=in_specs, out_specs=out_specs, check_vma=False
    )
```

time: 350 us -> 197 us (0.56)
  waiting for transfers between devices: 218 us -> 48.5 us
  blocking collectives: 0 us -> 67.6 us
  matrix products: 48.4 us -> 0 us
  local copies, waits for them, and re-layouts: 52.7 us -> 25.8 us
  Pallas kernels: 0 us -> 21.3 us
  between operations: 13.9 us -> 0.71 us
  starting transfers between devices: 9.29 us -> 22.2 us
  other arithmetic: 5 us -> 8.78 us
    reduce_scatter x2 -> x0, waiting for transfers between devices: 172 us -> none  [the longest x1 87.3 us: on_device(): lax.psum_scatter(partial_rows, 'head', scatter_dimension=0, tiled=True)]
    all_to_all x0 -> x2, blocking collectives: none -> 67.6 us  [exchange(): return lax.all_to_all(a, axes, split_axis=0, concat_axis=0, tiled=True)]
    all_gather x1 -> x0, waiting for transfers between devices: 45 us -> none  [on_device(): gathered = lax.all_gather(latent, 'ctx', axis=0, tiled=True)]
    all_to_all x1 -> x2, waiting for transfers between devices: 0.01 us -> 42.4 us  [exchange(): return lax.all_to_all(a, axes, split_axis=0, concat_axis=0, tiled=True)]
    dot_general x5 -> x0, matrix products: 41.3 us -> none  [the longest x1 11.1 us: block_grads(): jnp.einsum('qhij,qihd->qjd', dscores, q_block, preferred_element_type=jnp...]
    reshape x5 -> x2, local copies, waits for them, and re-layouts: 32.3 us -> 5.54 us  [the longest x1 2.88 us: on_device(): mine = mine.reshape(HALF, BLK, QW)]
    pallas_call x0 -> x1, Pallas kernels: none -> 21.3 us  [local_grads(): pl.pallas_call(kernel, grid_spec=pltpu.PrefetchScalarGridSpec(num_scalar_...]
    all_to_all x1 -> x2, starting transfers between devices: 9.18 us -> 22 us  [exchange(): return lax.all_to_all(a, axes, split_axis=0, concat_axis=0, tiled=True)]
  transfers between devices with their start and end apart: 4 -> 4, of which waited for: 3 -> 4; matrix products, arithmetic and copies ran while one was open for 6% -> 4% of each run, Pallas kernels for 0% -> 0%
where the time goes in v1:
time: 197 us; the launch traced here: 195 us
  blocking collectives  67.6 us (34%)
  waiting for transfers between devices  48.5 us (25%)
  local copies, waits for them, and re-layouts  25.8 us (13%)
  starting transfers between devices  22.2 us (11%)
  Pallas kernels  21.3 us (11%)
  other arithmetic  8.78 us (4%)
    all_to_all x2, blocking collectives, exchange(): return lax.all_to_all(a, axes, split_axis=0, concat_axis=0, tiled=True)  67.6 us
    all_to_all x2, waiting for transfers between devices, exchange(): return lax.all_to_all(a, axes, split_axis=0, concat_axis=0, tiled=True)  42.4 us
    all_to_all x2, starting transfers between devices, exchange(): return lax.all_to_all(a, axes, split_axis=0, concat_axis=0, tiled=True)  22 us
    pallas_call x1, Pallas kernels, local_grads(): pl.pallas_call(kernel, grid_spec=pltpu.PrefetchScalarGridSpec(num_scalar_...  21.3 us
    ppermute x2, local copies, waits for them, and re-layouts, swap_cores(): return lax.ppermute(a, 'core', [(0, 1), (1, 0)])  7.44 us
    all_to_all x2, local copies, waits for them, and re-layouts, exchange(): return lax.all_to_all(a, axes, split_axis=0, concat_axis=0, tiled=True)  7.4 us
    ppermute x2, waiting for transfers between devices, swap_cores(): return lax.ppermute(a, 'core', [(0, 1), (1, 0)])  6.1 us
    convert_element_type x1, other arithmetic, on_device(): rows = exchange(total.astype(jnp.bfloat16).reshape(2048, QW), 'x')  4.02 us
  transfers between devices with their start and end apart: 4, of which 4 were waited for; matrix products, arithmetic and copies ran while one was open for 4% of the time, Pallas kernels for 0%

profile of v1, /device:TPU:40, one launch (start us, length us, event | category | flops | bytes accessed | tf_op | source)
XLA Modules:
  0.0 194.9 jit_solution(7107856237796761796)
XLA Ops:
  0.6 1.1 broadcast_in_dim.7
  1.7 34.2 %all_to_all.28 = bf16[8,256,576]{1,2,0:T(8,128)(2,1)} all-to-all(bf16[8,256,576]{1,2,0:T(8,128)(2,1)S(1)} %broadcast_in_dim.7), channel_id=1, replica_groups=mesh['z_lo'=2,'x'=4,'core'=2,'y'=4,'z_hi'=4] {'x','z_lo'}, dimensions={0} | all-to-all | bytes 4718592 | tf_op jit(solution)/shard_map/all_to_all | solution.py:138
  36.0 3.1 %copy.27 = bf16[8,256,576]{2,1,0:T(8,128)(2,1)S(1)} copy(bf16[8,256,576]{1,2,0:T(8,128)(2,1)} %all_to_all.28) | data formatting | bytes 4718592 | tf_op jit(solution)/shard_map/all_to_all | solution.py:138
  39.1 0.0 copy-start
  39.1 0.0 copy-start.1
  39.1 0.0 copy-start.2
  39.1 2.9 %copy.28 = bf16[16,128,576]{1,2,0:T(8,128)(2,1)} copy(bf16[16,128,576]{2,1,0:T(8,128)(2,1)S(1)} %bitcast.10) | data formatting | bytes 4718592 | tf_op jit(solution)/shard_map/reshape | solution.py:144
  42.0 0.0 copy-done
  42.0 0.0 collective-permute-start
  42.0 0.0 copy-done.1
  42.0 0.1 fusion.5
  42.1 0.1 compare_convert_fusion
  42.2 0.6 pad_add_fusion.1.info
  42.8 0.0 copy-done.2
  42.8 2.5 %fusion.g_ref = bf16[4,256,512]{2,1,0:T(8,128)(2,1)} fusion(bf16[256,4,512]{2,1,0:T(4,128)(2,1)} %param.7, f32[256]{0:T(256)S(1)} %copy-done.2), kind=kLoop, calls=%fused_computation.4 | loop fusion | flops 1572864 | bytes 2098176 | tf_op jit(solution)/shard_map/transpose | solution.py:149
  45.3 1.6 collective-permute-done
  46.9 4.4 %copy.29.other_ref = bf16[16,128,576]{2,1,0:T(8,128)(2,1)} copy(bf16[16,128,576]{1,2,0:T(8,128)(2,1)} %collective-permute-done) | data formatting | bytes 4718592 | tf_op jit(solution)/shard_map/ppermute | solution.py:134
  51.2 21.3 %shard_map.68 = (bf16[16,4,16,576]{3,2,1,0:T(8,128)(2,1)}, bf16[16,128,576]{2,1,0:T(8,128)(2,1)}, bf16[16,128,576]{2,1,0:T(8,128)(2,1)}) custom-call(s32[2,18]{1,0:T(2,128)} %pad_add_fusion.1.info, bf16[4,576,256]{2,1,0:T(8,128)(2,1)} %bitcast.14, bf16[4,256,512]{2,1,0:T(8,128)(2,1)} %fusion.g_ref, bf16[16,128,576]{2,1,0:T(8,128)(2,1)} %bitcast.11, ...), custom_call_target="tpu_custom_call" | custom-call | tf_op jit(solution)/shard_map/pallas_call | solution.py:100
  72.5 3.2 %copy.31 = bf16[16,128,576]{1,2,0:T(8,128)(2,1)S(1)} copy(bf16[16,128,576]{2,1,0:T(8,128)(2,1)} %get-tuple-element.7) | data formatting | bytes 4718592 | tf_op jit(solution)/shard_map/pallas_call | solution.py:100
  75.7 0.2 collective-permute-start.1
  76.0 4.5 %collective-permute-done.1 = bf16[16,128,576]{1,2,0:T(8,128)(2,1)} collective-permute-done((bf16[16,128,576]{1,2,0:T(8,128)(2,1)S(1)}, bf16[16,128,576]{1,2,0:T(8,128)(2,1)}, u32[]{:S(2)}, u32[]{:S(2)}) %collective-permute-start.1) | collective-permute-done | bytes 2359328 | tf_op jit(solution)/shard_map/ppermute | solution.py:134
  80.5 3.1 %copy.32 = bf16[16,128,576]{2,1,0:T(8,128)(2,1)S(1)} copy(bf16[16,128,576]{1,2,0:T(8,128)(2,1)} %collective-permute-done.1) | data formatting | bytes 4718592 | tf_op jit(solution)/shard_map/ppermute | solution.py:134
  83.6 4.0 %add_convert_fusion = bf16[16,128,576]{2,1,0:T(8,128)(2,1)} fusion(bf16[16,128,576]{2,1,0:T(8,128)(2,1)S(1)} %copy.32, bf16[16,128,576]{2,1,0:T(8,128)(2,1)} %get-tuple-element.6), kind=kLoop, calls=%fused_computation | loop fusion | flops 4718592 | bytes 7077888 | tf_op jit(solution)/shard_map/convert_element_type | solution.py:162
  87.6 4.3 %copy.33 = bf16[4,512,576]{1,2,0:T(8,128)(2,1)} copy(bf16[4,512,576]{2,1,0:T(8,128)(2,1)} %bitcast.12) | data formatting | bytes 4718592 | tf_op jit(solution)/shard_map/all_to_all | solution.py:138
  91.9 33.3 %all_to_all.29 = bf16[4,512,576]{1,2,0:T(8,128)(2,1)S(1)} all-to-all(bf16[4,512,576]{1,2,0:T(8,128)(2,1)} %copy.33), channel_id=1, replica_groups=mesh['z_lo'=2,'x'=4,'core'=2,'y'=4,'z_hi'=4] {'x'}, dimensions={0} | all-to-all | bytes 4718592 | tf_op jit(solution)/shard_map/all_to_all | solution.py:138
  125.2 10.7 %all-to-all-start.1 = ((bf16[16,4,16,576]{3,2,1,0:T(8,128)(2,1)}), bf16[16,4,16,576]{3,2,1,0:T(8,128)(2,1)}, u32[]{:S(2)}, u32[]{:S(2)}) async-start(bf16[16,4,16,576]{3,2,1,0:T(8,128)(2,1)} %get-tuple-element.5), calls=%async_computation.1 | async-start | bytes 2621440 | tf_op jit(solution)/shard_map/all_to_all | solution.py:138
  135.9 0.7 reduce_sum.21
  136.6 1.1 copy.34
  137.7 27.0 %all-to-all-done.1 = bf16[16,4,16,576]{3,2,1,0:T(8,128)(2,1)} async-done(((bf16[16,4,16,576]{3,2,1,0:T(8,128)(2,1)}), bf16[16,4,16,576]{3,2,1,0:T(8,128)(2,1)}, u32[]{:S(2)}, u32[]{:S(2)}) %all-to-all-start.1) | async-done | bytes 1179680 | tf_op jit(solution)/shard_map/all_to_all | solution.py:138
  164.7 11.3 %all-to-all-start.3 = ((bf16[32,16,576]{2,1,0:T(8,128)(2,1)}), bf16[32,16,576]{2,1,0:T(8,128)(2,1)S(1)}, u32[]{:S(2)}, u32[]{:S(2)}) async-start(bf16[32,16,576]{2,1,0:T(8,128)(2,1)} %bitcast.6), calls=%async_computation.3 | async-start | bytes 1310720 | tf_op jit(solution)/shard_map/all_to_all | solution.py:138
  176.0 2.7 %copy.37 = bf16[64,16,576]{2,0,1:T(8,128)(2,1)} copy(bf16[64,16,576]{2,1,0:T(8,128)(2,1)} %bitcast.3) | data formatting | bytes 2359296 | tf_op jit(solution)/shard_map/reshape | solution.py:168
  178.7 15.5 %all-to-all-done.3 = bf16[32,16,576]{2,1,0:T(8,128)(2,1)S(1)} async-done(((bf16[32,16,576]{2,1,0:T(8,128)(2,1)}), bf16[32,16,576]{2,1,0:T(8,128)(2,1)S(1)}, u32[]{:S(2)}, u32[]{:S(2)}) %all-to-all-start.3) | async-done | bytes 589856 | tf_op jit(solution)/shard_map/all_to_all | solution.py:138
  194.2 0.7 convert_reduce_fusion
  (1 shorter events, 0.0 us)
Async XLA Ops:
  39.1 2.9 %copy-start = (bf16[8,256,576]{2,1,0:T(8,128)(2,1)}, bf16[8,256,576]{2,1,0:T(8,128)(2,1)S(1)}, u32[]{:S(2)}) copy-start(bf16[8,256,576]{2,1,0:T(8,128)(2,1)S(1)} %copy.27) | copy-start | bytes 7077892
  39.1 2.9 %copy-start.1 = (s32[2,8]{1,0:T(2,128)S(1)}, s32[2,8]{1,0:T(2,128)}, u32[]{:S(2)}) copy-start(s32[2,8]{1,0:T(2,128)} %param.9) | copy-start | bytes 196
  39.1 3.7 %copy-start.2 = (f32[256]{0:T(256)S(1)}, f32[256]{0:T(256)}, u32[]{:S(2)}) copy-start(f32[256]{0:T(256)} %param.8) | copy-start | bytes 3076
  42.0 4.9 %collective-permute-start = (bf16[16,128,576]{1,2,0:T(8,128)(2,1)}, bf16[16,128,576]{1,2,0:T(8,128)(2,1)}, u32[]{:S(2)}, u32[]{:S(2)}) collective-permute-start(bf16[16,128,576]{1,2,0:T(8,128)(2,1)} %copy.28), channel_id=1, source_target_pairs={{0,16},{16,0},{1,17},{17,1},{2,18},{18,2},{3,19},{19,3},{4,20},{20... | collective-permute-start | bytes 7077896 | tf_op jit(solution)/shard_map/ppermute | solution.py:134
  75.7 4.8 %collective-permute-start.1 = (bf16[16,128,576]{1,2,0:T(8,128)(2,1)S(1)}, bf16[16,128,576]{1,2,0:T(8,128)(2,1)}, u32[]{:S(2)}, u32[]{:S(2)}) collective-permute-start(bf16[16,128,576]{1,2,0:T(8,128)(2,1)S(1)} %copy.31), channel_id=1, source_target_pairs={{0,16},{16,0},{1,17},{17,1},{2,18},{18,2},{3,19},{19,3},{4,20},{20... | collective-permute-start | bytes 7077896 | tf_op jit(solution)/shard_map/ppermute | solution.py:134
  125.2 39.5 %all-to-all-start.1 = ((bf16[16,4,16,576]{3,2,1,0:T(8,128)(2,1)}), bf16[16,4,16,576]{3,2,1,0:T(8,128)(2,1)}, u32[]{:S(2)}, u32[]{:S(2)}) async-start(bf16[16,4,16,576]{3,2,1,0:T(8,128)(2,1)} %get-tuple-element.5), calls=%async_computation.1 | async-start | bytes 2621440 | tf_op jit(solution)/shard_map/all_to_all | solution.py:138
  164.7 29.4 %all-to-all-start.3 = ((bf16[32,16,576]{2,1,0:T(8,128)(2,1)}), bf16[32,16,576]{2,1,0:T(8,128)(2,1)S(1)}, u32[]{:S(2)}, u32[]{:S(2)}) async-start(bf16[32,16,576]{2,1,0:T(8,128)(2,1)} %bitcast.6), calls=%async_computation.3 | async-start | bytes 1310720 | tf_op jit(solution)/shard_map/all_to_all | solution.py:138

commit v2 on v1

v2 whole, which is shorter than its diff:
```python
import functools
import math

import jax
import jax.numpy as jnp
from jax import lax
from jax.experimental import pallas as pl
from jax.experimental.pallas import tpu as pltpu
from jax.sharding import Mesh
from jax.sharding import PartitionSpec as P

LAT = 512
QW = 576
BLK = 128
NSLOT = 9
NB = 32
HEADS_HERE = 4
MIB = 1024 * 1024
ROWS = HEADS_HERE * BLK

SOFTMAX_SCALE = 0.07216878364870322
LOG2E = 1.4426950408889634
MASKED = -1e30

SPLIT = (("z_lo", 2), ("x", 4), ("core", 2), ("y", 4), ("z_hi", 4))
AXES = tuple(name for name, _ in SPLIT)
SIZES = tuple(size for _, size in SPLIT)
CTX = AXES[:3]
HEAD = AXES[3:]


def kernel(info, q_ref, qt_ref, g_ref, gt_ref, *rest, npieces, nouts):
    pieces, rest = rest[:npieces], rest[npieces:]
    dq_ref, outs = rest[0], rest[1 : 1 + nouts]
    all_keys, keys, dense, sem, out_sem = rest[1 + nouts :]
    b = pl.program_id(0)
    each = NB // nouts

    def writes():
        return [
            pltpu.make_async_copy(dense.at[pl.ds(i * each, each)], out, out_sem)
            for i, out in enumerate(outs)
        ]

    @pl.when(b == 0)
    def _():
        copies, at = [], 0
        for piece in pieces:
            n = piece.shape[0]
            copies.append(pltpu.make_async_copy(piece, all_keys.at[pl.ds(at, n)], sem))
            at += n
        for copy in copies:
            copy.start()

        def clear(i, carry):
            dense[i] = jnp.zeros((QW, BLK), jnp.bfloat16)
            return carry

        lax.fori_loop(0, NB, clear, 0)
        for copy in copies:
            copy.wait()

    for s in range(NSLOT):
        keys[:, s * BLK : (s + 1) * BLK] = all_keys[info[b, s]]
    k = keys[...]
    q = q_ref[...].reshape(ROWS, QW)
    g = g_ref[...].reshape(ROWS, LAT)
    scores = jnp.dot(q, k, preferred_element_type=jnp.float32)
    dprobs = jnp.dot(g, k[:LAT], preferred_element_type=jnp.float32)

    row_pos = lax.broadcasted_iota(jnp.int32, (ROWS, BLK), 0) % BLK
    key_pos = lax.broadcasted_iota(jnp.int32, (ROWS, BLK), 1)
    parts = []
    for s in range(NSLOT):
        part = scores[:, s * BLK : (s + 1) * BLK] * (SOFTMAX_SCALE * LOG2E)
        if s == 0:
            part = jnp.where(key_pos <= row_pos, part, MASKED)
        else:
            part = jnp.where(info[b, NSLOT + s] > 0, part, MASKED)
        parts.append(part)
    masked = jnp.concatenate(parts, axis=1)
    top = jnp.max(masked, axis=1, keepdims=True)
    expo = jnp.exp2(masked - top)
    probs = expo * (1.0 / jnp.sum(expo, axis=1, keepdims=True))
    delta = jnp.sum(probs * dprobs, axis=1, keepdims=True)
    dscores = (probs * (dprobs - delta) * SOFTMAX_SCALE).astype(jnp.bfloat16)
    low = probs.astype(jnp.bfloat16)

    qt = jnp.concatenate([qt_ref[h] for h in range(HEADS_HERE)], axis=1)
    gt = jnp.concatenate([gt_ref[h] for h in range(HEADS_HERE)], axis=1)
    key_part = jnp.dot(qt, dscores, preferred_element_type=jnp.float32)
    value_part = jnp.dot(gt, low, preferred_element_type=jnp.float32)
    for s in range(NSLOT):
        cols = slice(s * BLK, (s + 1) * BLK)
        dest = info[b, 2 * NSLOT + s]
        head = dense[dest, :LAT].astype(jnp.float32) + key_part[:LAT, cols] + value_part[:, cols]
        tail = dense[dest, LAT:].astype(jnp.float32) + key_part[LAT:, cols]
        dense[dest, :LAT] = head.astype(jnp.bfloat16)
        dense[dest, LAT:] = tail.astype(jnp.bfloat16)

    @pl.when(b == 1)
    def _():
        for copy in writes():
            copy.start()

    dq = lax.dot_general(
        dscores, k, (((1,), (1,)), ((), ())), preferred_element_type=jnp.float32
    ).astype(jnp.bfloat16)
    for h in range(HEADS_HERE):
        dq_ref[:, h] = dq[h * BLK : (h + 1) * BLK].reshape(8, 16, QW)

    @pl.when(b == 1)
    def _():
        for copy in writes():
            copy.wait()


def local_grads(info, q, qt, g, gt, pieces, nouts):
    each = NB // nouts
    return pl.pallas_call(
        functools.partial(kernel, npieces=len(pieces), nouts=nouts),
        grid_spec=pltpu.PrefetchScalarGridSpec(
            num_scalar_prefetch=1,
            grid=(2,),
            in_specs=[
                pl.BlockSpec((HEADS_HERE, BLK, QW), lambda b, info: (0, b, 0)),
                pl.BlockSpec((HEADS_HERE, QW, BLK), lambda b, info: (0, 0, b)),
                pl.BlockSpec((HEADS_HERE, BLK, LAT), lambda b, info: (0, b, 0)),
                pl.BlockSpec((HEADS_HERE, LAT, BLK), lambda b, info: (0, 0, b)),
            ]
            + [pl.BlockSpec(memory_space=pltpu.HBM)] * len(pieces),
            out_specs=[pl.BlockSpec((8, HEADS_HERE, 16, QW), lambda b, info: (b, 0, 0, 0))]
            + [pl.BlockSpec(memory_space=pltpu.HBM)] * nouts,
            scratch_shapes=[
                pltpu.VMEM((NB, QW, BLK), jnp.bfloat16),
                pltpu.VMEM((QW, NSLOT * BLK), jnp.bfloat16),
                pltpu.VMEM((NB, QW, BLK), jnp.bfloat16),
                pltpu.SemaphoreType.DMA,
                pltpu.SemaphoreType.DMA,
            ],
        ),
        out_shape=[jax.ShapeDtypeStruct((16, HEADS_HERE, 16, QW), jnp.bfloat16)]
        + [jax.ShapeDtypeStruct((each, QW, BLK), jnp.bfloat16)] * nouts,
        compiler_params=pltpu.CompilerParams(
            dimension_semantics=("arbitrary",), vmem_limit_bytes=56 * MIB
        ),
    )(info, q, qt, g, gt, *pieces)


def neighbour(x=0, y=0, z=0, core=0):
    pairs = []
    shape = dict(SPLIT)
    strides = {}
    step = 1
    for name in reversed(AXES):
        strides[name] = step
        step *= shape[name]
    for zl in range(shape["z_lo"]):
        for px in range(shape["x"]):
            for pc in range(shape["core"]):
                for py in range(shape["y"]):
                    for zh in range(shape["z_hi"]):

                        def index(zz, xx, cc, yy):
                            zz %= shape["z_lo"] * shape["z_hi"]
                            high, low = zz // shape["z_lo"], zz % shape["z_lo"]
                            return (
                                low * strides["z_lo"]
                                + (xx % shape["x"]) * strides["x"]
                                + (cc % 2) * strides["core"]
                                + (yy % shape["y"]) * strides["y"]
                                + high * strides["z_hi"]
                            )

                        zz = zh * shape["z_lo"] + zl
                        pairs.append((index(zz, px, pc, py), index(zz + z, px + x, pc + core, py + y)))
    return pairs


def other_z():
    shape = tuple(size for _, size in SPLIT)
    step = math.prod(shape[1:])
    return [(i, (i + step) % (2 * step)) for i in range(2 * step)]


ALONG_X = [neighbour(x=d) for d in range(4)]
ALONG_Y = [neighbour(y=d) for d in range(4)]
RIGHT, LEFT = ALONG_X[1], ALONG_X[3]
UP, DOWN = neighbour(z=1), neighbour(z=-1)
SWAP = neighbour(core=1)
OTHER_Z = other_z()


def move(a, pairs):
    return lax.ppermute(a, AXES, pairs)


def pack_kernel(*refs):
    *pieces, out, sem = refs
    copies, at = [], 0
    for piece in pieces:
        n = piece.shape[0]
        copies.append(pltpu.make_async_copy(piece, out.at[pl.ds(at, n)], sem))
        at += n
    for copy in copies:
        copy.start()
    for copy in copies:
        copy.wait()


def pack(pieces):
    n = sum(piece.shape[0] for piece in pieces)
    return pl.pallas_call(
        pack_kernel,
        in_specs=[pl.BlockSpec(memory_space=pl.ANY)] * len(pieces),
        out_specs=pl.BlockSpec(memory_space=pl.ANY),
        out_shape=jax.ShapeDtypeStruct((n, QW, BLK), jnp.bfloat16),
        scratch_shapes=[pltpu.SemaphoreType.DMA],
        compiler_params=pltpu.CompilerParams(vmem_limit_bytes=4 * MIB),
    )(*pieces)


PLACES = (0, 2, 8, 4, 6, 12, 10, 14)


def gather_keys(own, beside):
    across = move(own, ALONG_X[2])
    first = move(own, RIGHT), move(own, LEFT), move(own, OTHER_Z)
    (from_left, from_right, z_own), beside = lax.optimization_barrier((first, beside))
    z_across, z_left, z_right = move(z_own, ALONG_X[2]), move(from_left, UP), move(from_right, DOWN)
    near = pack([own, from_right, from_left, z_own])
    far = pack([across, z_across, z_right, z_left])
    return [near, far, move(near, SWAP), move(far, SWAP)], beside


def add_cores_kernel(keep, got, *rest):
    outs, (ours, theirs, total, in_sems, out_sem) = rest[:4], rest[4:]
    loads, writes = [], []
    for i, d in enumerate((2, 1, 3, 0)):
        part = pl.ds(4 * d, 4)
        loads.append(
            [
                pltpu.make_async_copy(keep.at[part], ours.at[part], in_sems.at[i]),
                pltpu.make_async_copy(got.at[part], theirs.at[part], in_sems.at[4 + i]),
            ]
        )
        for load in loads[-1]:
            load.start()
    for i, d in enumerate((2, 1, 3, 0)):
        for load in loads[i]:
            load.wait()
        part = slice(4 * d, 4 * d + 4)
        added = ours[part].astype(jnp.float32) + theirs[part].astype(jnp.float32)
        total[part] = added.astype(jnp.bfloat16)
        writes.append(pltpu.make_async_copy(total.at[pl.ds(4 * d, 4)], outs[d], out_sem))
        writes[-1].start()
    for write in writes:
        write.wait()


def add_cores(keep, got):
    hbm = pl.BlockSpec(memory_space=pltpu.HBM)
    return pl.pallas_call(
        add_cores_kernel,
        in_specs=[hbm, hbm],
        out_specs=[hbm] * 4,
        scratch_shapes=[pltpu.VMEM((16, QW, BLK), jnp.bfloat16)] * 3
        + [pltpu.SemaphoreType.DMA((8,)), pltpu.SemaphoreType.DMA],
        out_shape=[jax.ShapeDtypeStruct((4, QW, BLK), jnp.bfloat16)] * 4,
        compiler_params=pltpu.CompilerParams(vmem_limit_bytes=24 * MIB),
    )(keep, got)


def total_of(refs, index):
    return sum(ref[index].astype(jnp.float32) for ref in refs)


def add_x_kernel(y_ref, *refs):
    parts, outs, turned = refs[:4], refs[4:8], refs[8]
    for z in range(2):
        for block in range(2):
            rows = total_of(parts, 2 * z + block).T.astype(jnp.bfloat16)
            turned[2 * block, z] = rows[: BLK // 2]
            turned[2 * block + 1, z] = rows[BLK // 2 :]
    for d in range(4):
        outs[d][...] = turned[(y_ref[0] + d) & 3]


def add_x(my_y, parts):
    vmem = pl.BlockSpec(memory_space=pltpu.VMEM)
    shape = (2, BLK // 2, QW)
    return pl.pallas_call(
        add_x_kernel,
        grid_spec=pltpu.PrefetchScalarGridSpec(
            num_scalar_prefetch=1,
            grid=(),
            in_specs=[vmem] * 4,
            out_specs=[vmem] * 4,
            scratch_shapes=[pltpu.VMEM((4, *shape), jnp.bfloat16)],
        ),
        out_shape=[jax.ShapeDtypeStruct(shape, jnp.bfloat16)] * 4,
        compiler_params=pltpu.CompilerParams(vmem_limit_bytes=16 * MIB),
    )(my_y, *parts)


def add_y_kernel(*refs):
    *parts, out = refs
    out[...] = total_of(parts, ...).astype(jnp.bfloat16)


def add_y(parts):
    vmem = pl.BlockSpec(memory_space=pltpu.VMEM)
    return pl.pallas_call(
        add_y_kernel,
        in_specs=[vmem] * 4,
        out_specs=vmem,
        out_shape=jax.ShapeDtypeStruct((2, BLK // 2, QW), jnp.bfloat16),
        compiler_params=pltpu.CompilerParams(vmem_limit_bytes=8 * MIB),
    )(*parts)


def spread(parts, moves):
    return [parts[0]] + [move(parts[d], moves[d]) for d in (1, 2, 3)]


def on_device(queries, latent, grad_out, advantage, ancestors):
    weighted = (advantage[:, None, None] * grad_out.astype(jnp.float32)).astype(jnp.bfloat16)
    beside = (
        jnp.transpose(queries, (1, 0, 2)),
        jnp.transpose(queries, (1, 2, 0)),
        jnp.transpose(weighted, (1, 0, 2)),
        jnp.transpose(weighted, (1, 2, 0)),
    )
    own_keys = jnp.swapaxes(latent.reshape(2, BLK, QW), 1, 2)
    pieces, (q, qt, g, gt) = gather_keys(own_keys, beside)

    my_z, my_x, my_core = (lax.axis_index(name) for name in CTX)
    own = lax.axis_index(CTX) * 2 + jnp.arange(2, dtype=jnp.int32)
    slots = jnp.concatenate([own[:, None], ancestors], axis=1)
    present = (slots >= 0).astype(jnp.int32)
    n = jnp.maximum(slots, 0)
    z, x, c, block = n // 16, (n // 4) % 4, (n // 2) % 2, n % 2
    dz, dx, dc = z ^ my_z, (x - my_x) & 3, c ^ my_core
    offset = dz * 4 + dx
    place = dc * 16 + sum(jnp.where(offset == i, at, 0) for i, at in enumerate(PLACES)) + block
    dest = dc * 16 + dx * 4 + z * 2 + block
    info = jnp.concatenate([place, present, dest], axis=1)

    dq, keep, send = local_grads(info, q, qt, g, gt, pieces, 2)

    parts = spread(add_cores(keep, move(send, SWAP)), ALONG_X)
    parts = spread(add_x(lax.axis_index("y")[None], parts), ALONG_Y)
    rows = add_y(parts).reshape(128, QW)
    rows = lax.all_to_all(rows, ("z_lo", "z_hi"), split_axis=0, concat_axis=0, tiled=True)
    latent_grad = jnp.sum(rows.reshape(8, 16, QW).astype(jnp.float32), axis=0)

    dq = lax.all_to_all(dq, HEAD, split_axis=0, concat_axis=0, tiled=True)
    query_grad = jnp.transpose(dq.reshape(64, 16, QW), (1, 0, 2))
    return query_grad, latent_grad


def solution(mesh):
    fine = Mesh(mesh.devices.reshape(SIZES), AXES)
    in_specs = (P(CTX, HEAD, None), P(CTX, None), P(CTX, HEAD, None), P(CTX), P(CTX, None))
    out_specs = (P(CTX + HEAD, None, None), P(CTX + HEAD, None))
    return jax.shard_map(
        on_device, mesh=fine, in_specs=in_specs, out_specs=out_specs, check_vma=False
    )
```

time: 197 us -> 125 us (0.63)
  blocking collectives: 67.6 us -> 0 us
  starting transfers between devices: 22.2 us -> 39.1 us
  local copies, waits for them, and re-layouts: 25.8 us -> 9.82 us
  other arithmetic: 8.78 us -> 4.21 us
    all_to_all x2 -> x0, blocking collectives: 67.6 us -> none  [exchange(): return lax.all_to_all(a, axes, split_axis=0, concat_axis=0, tiled=True)]
    all_to_all x2, waiting for transfers between devices: 42.4 us -> 5.14 us  [the longest x1 5.14 us: on_device(): lax.all_to_all(rows, ('z_lo', 'z_hi'), split_axis=0, concat_axis=0, tiled...]
    ppermute x2 -> x16, waiting for transfers between devices: 6.1 us -> 42 us  [move(): return lax.ppermute(a, AXES, pairs)]
    ppermute x2 -> x16, starting transfers between devices: 0.23 us -> 21.8 us  [move(): return lax.ppermute(a, AXES, pairs)]
    ppermute x2 -> x0, local copies, waits for them, and re-layouts: 7.44 us -> none  [swap_cores(): return lax.ppermute(a, 'core', [(0, 1), (1, 0)])]
    all_to_all x2 -> x0, local copies, waits for them, and re-layouts: 7.4 us -> none  [exchange(): return lax.all_to_all(a, axes, split_axis=0, concat_axis=0, tiled=True)]
    unnamed x6 -> x16, local copies, waits for them, and re-layouts: 0.02 us -> 4.84 us
    all_to_all x2, starting transfers between devices: 22 us -> 17.4 us  [the longest x1 10.3 us: on_device(): dq = lax.all_to_all(dq, HEAD, split_axis=0, concat_axis=0, tiled=True)]
  transfers between devices with their start and end apart: 4 -> 18, of which waited for: 4 -> 9; matrix products, arithmetic and copies ran while one was open for 4% -> 10% of each run, Pallas kernels for 0% -> 4%
where the time goes in v2:
time: 125 us; the launch traced here: 123 us
  waiting for transfers between devices  47.1 us (38%)
  starting transfers between devices  39.1 us (31%)
  Pallas kernels  22 us (18%)
  local copies, waits for them, and re-layouts  9.82 us (8%)
  other arithmetic  4.21 us (3%)
    ppermute x16, waiting for transfers between devices, move(): return lax.ppermute(a, AXES, pairs)  42 us
    ppermute x16, starting transfers between devices, move(): return lax.ppermute(a, AXES, pairs)  21.8 us
    pallas_call x1, Pallas kernels, local_grads(): pl.pallas_call(functools.partial(kernel, npieces=len(pieces), nouts=nouts...  17.6 us
    all_to_all x1, starting transfers between devices, on_device(): dq = lax.all_to_all(dq, HEAD, split_axis=0, concat_axis=0, tiled=True)  10.3 us
    all_to_all x1, starting transfers between devices, on_device(): lax.all_to_all(rows, ('z_lo', 'z_hi'), split_axis=0, concat_axis=0, tiled...  7.05 us
    all_to_all x1, waiting for transfers between devices, on_device(): lax.all_to_all(rows, ('z_lo', 'z_hi'), split_axis=0, concat_axis=0, tiled...  5.14 us
    unnamed x16, local copies, waits for them, and re-layouts  4.84 us
    transpose x1, other arithmetic, on_device(): jnp.transpose(weighted, (1, 2, 0))  2.77 us
  transfers between devices with their start and end apart: 18, of which 9 were waited for; matrix products, arithmetic and copies ran while one was open for 10% of the time, Pallas kernels for 4%

profile of v2, /device:TPU:40, one launch (start us, length us, event | category | flops | bytes accessed | tf_op | source)
XLA Modules:
  0.0 123.1 jit_solution(10899271619079387309)
XLA Ops:
  0.6 0.0 copy-start
  0.6 0.0 copy-start.4
  0.7 0.9 copy-done
  1.6 3.1 %collective-permute-start.3 = (bf16[2,576,128]{2,1,0:T(8,128)(2,1)S(1)}, bf16[2,576,128]{2,1,0:T(8,128)(2,1)S(1)}, u32[]{:S(2)}, u32[]{:S(2)}) collective-permute-start(bf16[2,576,128]{2,1,0:T(8,128)(2,1)S(1)} %bitcast_bitcast_fusion.refs_0_), channel_id=1, source_target_pairs={{0,64},{1,65},{2,66},{3,67},{4,68},{5,69},{6,70},{7,71},{8,72},{9,... | collective-permute-start | bytes 884744 | tf_op jit(solution)/shard_map/ppermute | solution.py:195
  4.7 0.1 collective-permute-start.2
  4.8 1.1 collective-permute-start.1
  6.0 0.9 collective-permute-start
  6.9 2.4 %copy.13 = bf16[256,4,512]{0,2,1:T(8,128)(2,1)} copy(bf16[256,4,512]{2,1,0:T(4,128)(2,1)} %param.7) | data formatting | bytes 2097152 | tf_op args[2]
  9.3 0.0 copy-done.4
  9.3 0.0 copy-start.5
  9.3 1.4 %copy.12 = bf16[256,4,576]{2,0,1:T(8,128)(2,1)} copy(bf16[256,4,576]{0,2,1:T(8,128)(2,1)S(1)} %copy-done.4) | data formatting | bytes 2359296 | tf_op args[0]
  10.7 0.0 copy-done.5
  10.7 2.8 %fusion = (bf16[4,512,256]{2,1,0:T(8,128)(2,1)}, bf16[4,256,512]{1,2,0:T(8,128)(2,1)}) fusion(bf16[256,4,512]{0,2,1:T(8,128)(2,1)} %copy.13, f32[256]{0:T(256)S(1)} %copy-done.5), kind=kLoop, calls=%fused_computation.2 | loop fusion | flops 1572864 | bytes 3146752 | tf_op jit(solution)/shard_map/transpose | solution.py:332
  13.5 0.0 collective-permute-done.2.refs_3_
  13.5 4.9 %collective-permute-done.1.refs_1_ = bf16[2,576,128]{2,1,0:T(8,128)(2,1)S(1)} collective-permute-done((bf16[2,576,128]{2,1,0:T(8,128)(2,1)S(1)}, bf16[2,576,128]{2,1,0:T(8,128)(2,1)S(1)}, u32[]{:S(2)}, u32[]{:S(2)}) %collective-permute-start.1) | collective-permute-done | bytes 294944 | tf_op jit(solution)/shard_map/ppermute | solution.py:195
  18.4 0.0 collective-permute-done.refs_2_
  18.4 0.1 collective-permute-start.5
  18.5 1.9 %collective-permute-start.6 = (bf16[2,576,128]{2,1,0:T(8,128)(2,1)S(1)}, bf16[2,576,128]{2,1,0:T(8,128)(2,1)S(1)}, u32[]{:S(2)}, u32[]{:S(2)}) collective-permute-start(bf16[2,576,128]{2,1,0:T(8,128)(2,1)S(1)} %collective-permute-done.refs_2_), channel_id=1, source_target_pairs={{0,128},{1,129},{2,130},{3,131},{4,132},{5,133},{6,134},{7,135},{8... | collective-permute-start | bytes 884744 | tf_op jit(solution)/shard_map/ppermute | solution.py:195
  20.4 2.9 %collective-permute-start.4 = (bf16[2,576,128]{2,1,0:T(8,128)(2,1)S(1)}, bf16[2,576,128]{2,1,0:T(8,128)(2,1)S(1)}, u32[]{:S(2)}, u32[]{:S(2)}) collective-permute-start(bf16[2,576,128]{2,1,0:T(8,128)(2,1)S(1)} %collective-permute-done.2.refs_3_), channel_id=1, source_target_pairs={{0,64},{1,65},{2,66},{3,67},{4,68},{5,69},{6,70},{7,71},{8,72},{9,... | collective-permute-start | bytes 884744 | tf_op jit(solution)/shard_map/ppermute | solution.py:195
  23.3 0.2 shard_map.68.rest_0_
  23.6 0.0 copy-start.1
  23.6 0.0 copy-start.6
  23.6 0.1 collective-permute-start.7
  23.7 0.0 collective-permute-done.3.refs_0_
  23.7 3.5 %collective-permute-done.5.refs_2_ = bf16[2,576,128]{2,1,0:T(8,128)(2,1)S(1)} collective-permute-done((bf16[2,576,128]{2,1,0:T(8,128)(2,1)S(1)}, bf16[2,576,128]{2,1,0:T(8,128)(2,1)S(1)}, u32[]{:S(2)}, u32[]{:S(2)}) %collective-permute-start.5) | collective-permute-done | bytes 294944 | tf_op jit(solution)/shard_map/ppermute | solution.py:195
  27.2 3.6 %collective-permute-done.6.refs_3_ = bf16[2,576,128]{2,1,0:T(8,128)(2,1)S(1)} collective-permute-done((bf16[2,576,128]{2,1,0:T(8,128)(2,1)S(1)}, bf16[2,576,128]{2,1,0:T(8,128)(2,1)S(1)}, u32[]{:S(2)}, u32[]{:S(2)}) %collective-permute-start.6) | collective-permute-done | bytes 294944 | tf_op jit(solution)/shard_map/ppermute | solution.py:195
  30.8 0.0 collective-permute-done.4.refs_1_
  30.8 0.2 shard_map.69.rest_1_
  31.0 0.0 copy-start.2
  31.0 0.1 collective-permute-start.8
  31.2 0.0 copy-done.6
  31.2 0.1 fusion.13
  31.3 0.7 pad_add_fusion.1.info
  32.0 2.3 %copy.14.g_ref = bf16[4,256,512]{2,1,0:T(8,128)(2,1)} copy(bf16[4,256,512]{1,2,0:T(8,128)(2,1)} %get-tuple-element.22) | data formatting | bytes 2097152 | tf_op jit(solution)/shard_map/optimization_barrier | solution.py:229
  34.3 0.0 copy-done.1
  34.3 0.0 collective-permute-done.7.rest_2_
  34.3 0.0 collective-permute-done.8.rest_3_
  34.3 0.0 copy-done.2
  34.3 17.6 %shard_map.70 = (bf16[16,4,16,576]{3,2,1,0:T(8,128)(2,1)}, bf16[16,576,128]{2,1,0:T(8,128)(2,1)}, bf16[16,576,128]{2,1,0:T(8,128)(2,1)}) custom-call(s32[2,27]{1,0:T(2,128)} %pad_add_fusion.1.info, bf16[4,256,576]{2,1,0:T(8,128)(2,1)} %bitcast.19, bf16[4,576,256]{2,1,0:T(8,128)(2,1)} %bitcast.20, bf16[4,256,512]{2,1,0:T(8,128)(2,1)} %copy.14.g_ref, ...), custom_call_target="tpu_custom_call" | custom-call | tf_op jit(solution)/shard_map/pallas_call | solution.py:120
  51.9 0.7 collective-permute-start.9
  52.6 0.0 copy-start.3
  52.6 10.3 %all-to-all-start = ((bf16[16,4,16,576]{3,2,1,0:T(8,128)(2,1)}), bf16[16,4,16,576]{3,2,1,0:T(8,128)(2,1)}, u32[]{:S(2)}, u32[]{:S(2)}) async-start(bf16[16,4,16,576]{3,2,1,0:T(8,128)(2,1)} %get-tuple-element.27), calls=%async_computation | async-start | bytes 2621440 | tf_op jit(solution)/shard_map/all_to_all | solution.py:357
  63.0 0.0 collective-permute-done.9.got
  63.0 0.0 copy-done.3
  63.0 2.6 %shard_map.71 = (bf16[4,576,128]{2,1,0:T(8,128)(2,1)S(1)}, bf16[4,576,128]{2,1,0:T(8,128)(2,1)}, bf16[4,576,128]{2,1,0:T(8,128)(2,1)}, bf16[4,576,128]{2,1,0:T(8,128)(2,1)}) custom-call(bf16[16,576,128]{2,1,0:T(8,128)(2,1)S(1)} %copy-done.3, bf16[16,576,128]{2,1,0:T(8,128)(2,1)} %collective-permute-done.9.got), custom_call_target="tpu_custom_call" | custom-call | tf_op jit(solution)/shard_map/pallas_call | solution.py:263
  65.6 1.8 %collective-permute-start.10 = (bf16[4,576,128]{2,1,0:T(8,128)(2,1)}, bf16[4,576,128]{2,1,0:T(8,128)(2,1)S(1)}, u32[]{:S(2)}, u32[]{:S(2)}) collective-permute-start(bf16[4,576,128]{2,1,0:T(8,128)(2,1)} %get-tuple-element.31), channel_id=1, source_target_pairs={{0,32},{1,33},{2,34},{3,35},{4,36},{5,37},{6,38},{7,39},{8,40},{9,... | collective-permute-start | bytes 1769480 | tf_op jit(solution)/shard_map/ppermute | solution.py:195
  67.4 2.7 %collective-permute-start.11 = (bf16[4,576,128]{2,1,0:T(8,128)(2,1)}, bf16[4,576,128]{2,1,0:T(8,128)(2,1)S(1)}, u32[]{:S(2)}, u32[]{:S(2)}) collective-permute-start(bf16[4,576,128]{2,1,0:T(8,128)(2,1)} %get-tuple-element.32), channel_id=1, source_target_pairs={{0,64},{1,65},{2,66},{3,67},{4,68},{5,69},{6,70},{7,71},{8,72},{9,... | collective-permute-start | bytes 1769480 | tf_op jit(solution)/shard_map/ppermute | solution.py:195
  70.1 1.4 %collective-permute-start.12 = (bf16[4,576,128]{2,1,0:T(8,128)(2,1)}, bf16[4,576,128]{2,1,0:T(8,128)(2,1)S(1)}, u32[]{:S(2)}, u32[]{:S(2)}) collective-permute-start(bf16[4,576,128]{2,1,0:T(8,128)(2,1)} %get-tuple-element.33), channel_id=1, source_target_pairs={{0,96},{1,97},{2,98},{3,99},{4,100},{5,101},{6,102},{7,103},{8,104... | collective-permute-start | bytes 1769480 | tf_op jit(solution)/shard_map/ppermute | solution.py:195
  71.6 10.7 %collective-permute-done.10.refs_1_ = bf16[4,576,128]{2,1,0:T(8,128)(2,1)S(1)} collective-permute-done((bf16[4,576,128]{2,1,0:T(8,128)(2,1)}, bf16[4,576,128]{2,1,0:T(8,128)(2,1)S(1)}, u32[]{:S(2)}, u32[]{:S(2)}) %collective-permute-start.10) | collective-permute-done | bytes 589856 | tf_op jit(solution)/shard_map/ppermute | solution.py:195
  82.2 13.5 %collective-permute-done.11.refs_2_ = bf16[4,576,128]{2,1,0:T(8,128)(2,1)S(1)} collective-permute-done((bf16[4,576,128]{2,1,0:T(8,128)(2,1)}, bf16[4,576,128]{2,1,0:T(8,128)(2,1)S(1)}, u32[]{:S(2)}, u32[]{:S(2)}) %collective-permute-start.11) | collective-permute-done | bytes 589856 | tf_op jit(solution)/shard_map/ppermute | solution.py:195
  95.7 0.0 collective-permute-done.12.refs_3_
  95.7 0.5 shard_map.72
  96.2 1.5 %collective-permute-start.13 = (bf16[2,64,576]{2,1,0:T(8,128)(2,1)S(1)}, bf16[2,64,576]{2,1,0:T(8,128)(2,1)S(1)}, u32[]{:S(2)}, u32[]{:S(2)}) collective-permute-start(bf16[2,64,576]{2,1,0:T(8,128)(2,1)S(1)} %get-tuple-element.35), channel_id=1, source_target_pairs={{0,4},{1,5},{2,6},{3,7},{4,8},{5,9},{6,10},{7,11},{8,12},{9,13},{1... | collective-permute-start | bytes 442376 | tf_op jit(solution)/shard_map/ppermute | solution.py:195
  97.8 1.0 collective-permute-start.14
  98.8 2.2 %collective-permute-start.15 = (bf16[2,64,576]{2,1,0:T(8,128)(2,1)S(1)}, bf16[2,64,576]{2,1,0:T(8,128)(2,1)S(1)}, u32[]{:S(2)}, u32[]{:S(2)}) collective-permute-start(bf16[2,64,576]{2,1,0:T(8,128)(2,1)S(1)} %get-tuple-element.37), channel_id=1, source_target_pairs={{0,12},{1,13},{2,14},{3,15},{4,0},{5,1},{6,2},{7,3},{8,4},{9,5},{1... | collective-permute-start | bytes 442376 | tf_op jit(solution)/shard_map/ppermute | solution.py:195
  101.0 2.2 %collective-permute-done.13.refs_1_ = bf16[2,64,576]{2,1,0:T(8,128)(2,1)S(1)} collective-permute-done((bf16[2,64,576]{2,1,0:T(8,128)(2,1)S(1)}, bf16[2,64,576]{2,1,0:T(8,128)(2,1)S(1)}, u32[]{:S(2)}, u32[]{:S(2)}) %collective-permute-start.13) | collective-permute-done | bytes 147488 | tf_op jit(solution)/shard_map/ppermute | solution.py:195
  103.2 2.5 %collective-permute-done.14.refs_2_ = bf16[2,64,576]{2,1,0:T(8,128)(2,1)S(1)} collective-permute-done((bf16[2,64,576]{2,1,0:T(8,128)(2,1)S(1)}, bf16[2,64,576]{2,1,0:T(8,128)(2,1)S(1)}, u32[]{:S(2)}, u32[]{:S(2)}) %collective-permute-start.14) | collective-permute-done | bytes 147488 | tf_op jit(solution)/shard_map/ppermute | solution.py:195
  105.7 1.2 collective-permute-done.15.refs_3_
  106.9 0.7 shard_map.73
  107.6 0.0 all-to-all-done
  107.6 7.0 %all-to-all-start.1 = ((bf16[8,16,576]{2,1,0:T(8,128)(2,1)}), bf16[8,16,576]{2,1,0:T(8,128)(2,1)S(1)}, u32[]{:S(2)}, u32[]{:S(2)}) async-start(bf16[8,16,576]{2,1,0:T(8,128)(2,1)} %bitcast.8), calls=%async_computation.1 | async-start | bytes 327680 | tf_op jit(solution)/shard_map/all_to_all | solution.py:354
  114.7 2.7 %copy.19 = bf16[64,16,576]{2,0,1:T(8,128)(2,1)} copy(bf16[64,16,576]{2,1,0:T(8,128)(2,1)} %bitcast.5) | data formatting | bytes 2359296 | tf_op jit(solution)/shard_map/reshape | solution.py:358
  117.3 5.1 %all-to-all-done.1 = bf16[8,16,576]{2,1,0:T(8,128)(2,1)S(1)} async-done(((bf16[8,16,576]{2,1,0:T(8,128)(2,1)}), bf16[8,16,576]{2,1,0:T(8,128)(2,1)S(1)}, u32[]{:S(2)}, u32[]{:S(2)}) %all-to-all-start.1) | async-done | bytes 147488 | tf_op jit(solution)/shard_map/all_to_all | solution.py:354
  122.5 0.6 convert_reduce_fusion
  (4 shorter events, 0.0 us)
Async XLA Ops:
  0.6 1.0 copy-start
  0.6 8.7 %copy-start.4 = (bf16[256,4,576]{0,2,1:T(8,128)(2,1)S(1)}, bf16[256,4,576]{0,2,1:T(8,128)(2,1)}, u32[]{:S(2)}) copy-start(bf16[256,4,576]{0,2,1:T(8,128)(2,1)} %param.5) | copy-start | bytes 3538948
  1.6 22.1 %collective-permute-start.3 = (bf16[2,576,128]{2,1,0:T(8,128)(2,1)S(1)}, bf16[2,576,128]{2,1,0:T(8,128)(2,1)S(1)}, u32[]{:S(2)}, u32[]{:S(2)}) collective-permute-start(bf16[2,576,128]{2,1,0:T(8,128)(2,1)S(1)} %bitcast_bitcast_fusion.refs_0_), channel_id=1, source_target_pairs={{0,64},{1,65},{2,66},{3,67},{4,68},{5,69},{6,70},{7,71},{8,72},{9,... | collective-permute-start | bytes 884744 | tf_op jit(solution)/shard_map/ppermute | solution.py:195
  4.7 8.8 %collective-permute-start.2 = (bf16[2,576,128]{2,1,0:T(8,128)(2,1)S(1)}, bf16[2,576,128]{2,1,0:T(8,128)(2,1)S(1)}, u32[]{:S(2)}, u32[]{:S(2)}) collective-permute-start(bf16[2,576,128]{2,1,0:T(8,128)(2,1)S(1)} %bitcast_bitcast_fusion.refs_0_), channel_id=1, source_target_pairs={{0,128},{1,129},{2,130},{3,131},{4,132},{5,133},{6,134},{7,135},{8... | collective-permute-start | bytes 884744 | tf_op jit(solution)/shard_map/ppermute | solution.py:195
  4.8 13.6 %collective-permute-start.1 = (bf16[2,576,128]{2,1,0:T(8,128)(2,1)S(1)}, bf16[2,576,128]{2,1,0:T(8,128)(2,1)S(1)}, u32[]{:S(2)}, u32[]{:S(2)}) collective-permute-start(bf16[2,576,128]{2,1,0:T(8,128)(2,1)S(1)} %bitcast_bitcast_fusion.refs_0_), channel_id=1, source_target_pairs={{0,96},{1,97},{2,98},{3,99},{4,100},{5,101},{6,102},{7,103},{8,104... | collective-permute-start | bytes 884744 | tf_op jit(solution)/shard_map/ppermute | solution.py:195
  6.0 12.4 %collective-permute-start = (bf16[2,576,128]{2,1,0:T(8,128)(2,1)S(1)}, bf16[2,576,128]{2,1,0:T(8,128)(2,1)S(1)}, u32[]{:S(2)}, u32[]{:S(2)}) collective-permute-start(bf16[2,576,128]{2,1,0:T(8,128)(2,1)S(1)} %bitcast_bitcast_fusion.refs_0_), channel_id=1, source_target_pairs={{0,32},{1,33},{2,34},{3,35},{4,36},{5,37},{6,38},{7,39},{8,40},{9,... | collective-permute-start | bytes 884744 | tf_op jit(solution)/shard_map/ppermute | solution.py:195
  9.3 1.4 %copy-start.5 = (f32[256]{0:T(256)S(1)}, f32[256]{0:T(256)}, u32[]{:S(2)}) copy-start(f32[256]{0:T(256)} %param.8) | copy-start | bytes 3076
  18.4 8.8 %collective-permute-start.5 = (bf16[2,576,128]{2,1,0:T(8,128)(2,1)S(1)}, bf16[2,576,128]{2,1,0:T(8,128)(2,1)S(1)}, u32[]{:S(2)}, u32[]{:S(2)}) collective-permute-start(bf16[2,576,128]{2,1,0:T(8,128)(2,1)S(1)} %collective-permute-done.1.refs_1_), channel_id=1, source_target_pairs={{0,131},{1,128},{2,129},{3,130},{4,135},{5,132},{6,133},{7,134},{8... | collective-permute-start | bytes 884744 | tf_op jit(solution)/shard_map/ppermute | solution.py:195
  18.5 12.2 %collective-permute-start.6 = (bf16[2,576,128]{2,1,0:T(8,128)(2,1)S(1)}, bf16[2,576,128]{2,1,0:T(8,128)(2,1)S(1)}, u32[]{:S(2)}, u32[]{:S(2)}) collective-permute-start(bf16[2,576,128]{2,1,0:T(8,128)(2,1)S(1)} %collective-permute-done.refs_2_), channel_id=1, source_target_pairs={{0,128},{1,129},{2,130},{3,131},{4,132},{5,133},{6,134},{7,135},{8... | collective-permute-start | bytes 884744 | tf_op jit(solution)/shard_map/ppermute | solution.py:195
  20.4 10.3 %collective-permute-start.4 = (bf16[2,576,128]{2,1,0:T(8,128)(2,1)S(1)}, bf16[2,576,128]{2,1,0:T(8,128)(2,1)S(1)}, u32[]{:S(2)}, u32[]{:S(2)}) collective-permute-start(bf16[2,576,128]{2,1,0:T(8,128)(2,1)S(1)} %collective-permute-done.2.refs_3_), channel_id=1, source_target_pairs={{0,64},{1,65},{2,66},{3,67},{4,68},{5,69},{6,70},{7,71},{8,72},{9,... | collective-permute-start | bytes 884744 | tf_op jit(solution)/shard_map/ppermute | solution.py:195
  23.6 10.7 %copy-start.1 = (bf16[8,576,128]{2,1,0:T(8,128)(2,1)}, bf16[8,576,128]{2,1,0:T(8,128)(2,1)S(1)}, u32[]{:S(2)}) copy-start(bf16[8,576,128]{2,1,0:T(8,128)(2,1)S(1)} %shard_map.68.rest_0_) | copy-start | bytes 3538948
  23.6 7.6 %copy-start.6 = (s32[2,8]{1,0:T(2,128)S(1)}, s32[2,8]{1,0:T(2,128)}, u32[]{:S(2)}) copy-start(s32[2,8]{1,0:T(2,128)} %param.9) | copy-start | bytes 196
  23.6 10.7 %collective-permute-start.7 = (bf16[8,576,128]{2,1,0:T(8,128)(2,1)S(1)}, bf16[8,576,128]{2,1,0:T(8,128)(2,1)}, u32[]{:S(2)}, u32[]{:S(2)}) collective-permute-start(bf16[8,576,128]{2,1,0:T(8,128)(2,1)S(1)} %shard_map.68.rest_0_), channel_id=1, source_target_pairs={{0,16},{1,17},{2,18},{3,19},{4,20},{5,21},{6,22},{7,23},{8,24},{9,... | collective-permute-start | bytes 3538952 | tf_op jit(solution)/shard_map/ppermute | solution.py:195
  31.0 3.3 %copy-start.2 = (bf16[8,576,128]{2,1,0:T(8,128)(2,1)}, bf16[8,576,128]{2,1,0:T(8,128)(2,1)S(1)}, u32[]{:S(2)}) copy-start(bf16[8,576,128]{2,1,0:T(8,128)(2,1)S(1)} %shard_map.69.rest_1_) | copy-start | bytes 3538948
  31.0 3.2 %collective-permute-start.8 = (bf16[8,576,128]{2,1,0:T(8,128)(2,1)S(1)}, bf16[8,576,128]{2,1,0:T(8,128)(2,1)}, u32[]{:S(2)}, u32[]{:S(2)}) collective-permute-start(bf16[8,576,128]{2,1,0:T(8,128)(2,1)S(1)} %shard_map.69.rest_1_), channel_id=1, source_target_pairs={{0,16},{1,17},{2,18},{3,19},{4,20},{5,21},{6,22},{7,23},{8,24},{9,... | collective-permute-start | bytes 3538952 | tf_op jit(solution)/shard_map/ppermute | solution.py:195
  51.9 11.0 %collective-permute-start.9 = (bf16[16,576,128]{2,1,0:T(8,128)(2,1)}, bf16[16,576,128]{2,1,0:T(8,128)(2,1)}, u32[]{:S(2)}, u32[]{:S(2)}) collective-permute-start(bf16[16,576,128]{2,1,0:T(8,128)(2,1)} %get-tuple-element.29), channel_id=1, source_target_pairs={{0,16},{1,17},{2,18},{3,19},{4,20},{5,21},{6,22},{7,23},{8,24},{9,... | collective-permute-start | bytes 7077896 | tf_op jit(solution)/shard_map/ppermute | solution.py:195
  52.6 10.3 %copy-start.3 = (bf16[16,576,128]{2,1,0:T(8,128)(2,1)S(1)}, bf16[16,576,128]{2,1,0:T(8,128)(2,1)}, u32[]{:S(2)}) copy-start(bf16[16,576,128]{2,1,0:T(8,128)(2,1)} %get-tuple-element.28.keep) | copy-start | bytes 7077892
  52.6 55.0 %all-to-all-start = ((bf16[16,4,16,576]{3,2,1,0:T(8,128)(2,1)}), bf16[16,4,16,576]{3,2,1,0:T(8,128)(2,1)}, u32[]{:S(2)}, u32[]{:S(2)}) async-start(bf16[16,4,16,576]{3,2,1,0:T(8,128)(2,1)} %get-tuple-element.27), calls=%async_computation | async-start | bytes 2621440 | tf_op jit(solution)/shard_map/all_to_all | solution.py:357
  65.6 16.6 %collective-permute-start.10 = (bf16[4,576,128]{2,1,0:T(8,128)(2,1)}, bf16[4,576,128]{2,1,0:T(8,128)(2,1)S(1)}, u32[]{:S(2)}, u32[]{:S(2)}) collective-permute-start(bf16[4,576,128]{2,1,0:T(8,128)(2,1)} %get-tuple-element.31), channel_id=1, source_target_pairs={{0,32},{1,33},{2,34},{3,35},{4,36},{5,37},{6,38},{7,39},{8,40},{9,... | collective-permute-start | bytes 1769480 | tf_op jit(solution)/shard_map/ppermute | solution.py:195
  67.4 28.3 %collective-permute-start.11 = (bf16[4,576,128]{2,1,0:T(8,128)(2,1)}, bf16[4,576,128]{2,1,0:T(8,128)(2,1)S(1)}, u32[]{:S(2)}, u32[]{:S(2)}) collective-permute-start(bf16[4,576,128]{2,1,0:T(8,128)(2,1)} %get-tuple-element.32), channel_id=1, source_target_pairs={{0,64},{1,65},{2,66},{3,67},{4,68},{5,69},{6,70},{7,71},{8,72},{9,... | collective-permute-start | bytes 1769480 | tf_op jit(solution)/shard_map/ppermute | solution.py:195
  70.1 25.6 %collective-permute-start.12 = (bf16[4,576,128]{2,1,0:T(8,128)(2,1)}, bf16[4,576,128]{2,1,0:T(8,128)(2,1)S(1)}, u32[]{:S(2)}, u32[]{:S(2)}) collective-permute-start(bf16[4,576,128]{2,1,0:T(8,128)(2,1)} %get-tuple-element.33), channel_id=1, source_target_pairs={{0,96},{1,97},{2,98},{3,99},{4,100},{5,101},{6,102},{7,103},{8,104... | collective-permute-start | bytes 1769480 | tf_op jit(solution)/shard_map/ppermute | solution.py:195
  96.2 7.0 %collective-permute-start.13 = (bf16[2,64,576]{2,1,0:T(8,128)(2,1)S(1)}, bf16[2,64,576]{2,1,0:T(8,128)(2,1)S(1)}, u32[]{:S(2)}, u32[]{:S(2)}) collective-permute-start(bf16[2,64,576]{2,1,0:T(8,128)(2,1)S(1)} %get-tuple-element.35), channel_id=1, source_target_pairs={{0,4},{1,5},{2,6},{3,7},{4,8},{5,9},{6,10},{7,11},{8,12},{9,13},{1... | collective-permute-start | bytes 442376 | tf_op jit(solution)/shard_map/ppermute | solution.py:195
  97.8 7.9 %collective-permute-start.14 = (bf16[2,64,576]{2,1,0:T(8,128)(2,1)S(1)}, bf16[2,64,576]{2,1,0:T(8,128)(2,1)S(1)}, u32[]{:S(2)}, u32[]{:S(2)}) collective-permute-start(bf16[2,64,576]{2,1,0:T(8,128)(2,1)S(1)} %get-tuple-element.36), channel_id=1, source_target_pairs={{0,8},{1,9},{2,10},{3,11},{4,12},{5,13},{6,14},{7,15},{8,0},{9,1},... | collective-permute-start | bytes 442376 | tf_op jit(solution)/shard_map/ppermute | solution.py:195
  98.8 8.1 %collective-permute-start.15 = (bf16[2,64,576]{2,1,0:T(8,128)(2,1)S(1)}, bf16[2,64,576]{2,1,0:T(8,128)(2,1)S(1)}, u32[]{:S(2)}, u32[]{:S(2)}) collective-permute-start(bf16[2,64,576]{2,1,0:T(8,128)(2,1)S(1)} %get-tuple-element.37), channel_id=1, source_target_pairs={{0,12},{1,13},{2,14},{3,15},{4,0},{5,1},{6,2},{7,3},{8,4},{9,5},{1... | collective-permute-start | bytes 442376 | tf_op jit(solution)/shard_map/ppermute | solution.py:195
  107.6 14.8 %all-to-all-start.1 = ((bf16[8,16,576]{2,1,0:T(8,128)(2,1)}), bf16[8,16,576]{2,1,0:T(8,128)(2,1)S(1)}, u32[]{:S(2)}, u32[]{:S(2)}) async-start(bf16[8,16,576]{2,1,0:T(8,128)(2,1)} %bitcast.8), calls=%async_computation.1 | async-start | bytes 327680 | tf_op jit(solution)/shard_map/all_to_all | solution.py:354

commit v3 on v2

v3 whole, which is shorter than its diff:
```python
import functools
import math

import jax
import jax.numpy as jnp
from jax import lax
from jax.experimental import pallas as pl
from jax.experimental.pallas import tpu as pltpu
from jax.sharding import Mesh
from jax.sharding import PartitionSpec as P

LAT = 512
QW = 576
BLK = 128
NSLOT = 9
NB = 32
HEADS_HERE = 4
MIB = 1024 * 1024
ROWS = HEADS_HERE * BLK

SOFTMAX_SCALE = 0.07216878364870322
LOG2E = 1.4426950408889634
MASKED = -1e30

SPLIT = (("z_lo", 2), ("x", 4), ("core", 2), ("y", 4), ("z_hi", 4))
AXES = tuple(name for name, _ in SPLIT)
SIZES = tuple(size for _, size in SPLIT)
CTX = AXES[:3]
HEAD = AXES[3:]


def prepare_kernel(advantage_ref, qt_hbm, grad_hbm, q_hbm, g_hbm, gt_hbm, *scratch):
    qt, grad, q, g, gt, in_sems, out_sem = scratch
    heads = range(HEADS_HERE)
    load_grad = pltpu.make_async_copy(grad_hbm, grad, in_sems.at[HEADS_HERE])
    load_grad.start()
    loads = [pltpu.make_async_copy(qt_hbm.at[h], qt.at[h], in_sems.at[h]) for h in heads]
    for load in loads:
        load.start()
    writes = []

    def write(value, hbm, h):
        writes.append(pltpu.make_async_copy(value.at[h], hbm.at[h], out_sem))
        writes[-1].start()

    load_grad.wait()
    for h in heads:
        weighted = grad[:, h, :].T.astype(jnp.float32) * advantage_ref[...]
        gt[h] = weighted.astype(jnp.bfloat16)
        write(gt, gt_hbm, h)
        g[h] = gt[h].T
        write(g, g_hbm, h)
    for h in heads:
        loads[h].wait()
        q[h] = qt[h].T
        write(q, q_hbm, h)
    for copy in writes:
        copy.wait()


def prepare(qt, grad_out, advantage):
    hbm = pl.BlockSpec(memory_space=pltpu.HBM)
    shapes = (HEADS_HERE, 2 * BLK, QW), (HEADS_HERE, 2 * BLK, LAT), (HEADS_HERE, LAT, 2 * BLK)
    scratch = (qt.shape, grad_out.shape, *shapes)
    return pl.pallas_call(
        prepare_kernel,
        in_specs=[pl.BlockSpec(memory_space=pltpu.VMEM), hbm, hbm],
        out_specs=[hbm] * 3,
        out_shape=[jax.ShapeDtypeStruct(shape, jnp.bfloat16) for shape in shapes],
        scratch_shapes=[pltpu.VMEM(shape, jnp.bfloat16) for shape in scratch]
        + [pltpu.SemaphoreType.DMA((HEADS_HERE + 1,)), pltpu.SemaphoreType.DMA],
        compiler_params=pltpu.CompilerParams(vmem_limit_bytes=14 * MIB),
    )(advantage[None], qt, grad_out)


def kernel(info, q_hbm, qt_hbm, g_hbm, gt_hbm, *rest):
    pieces, rest = rest[:2], rest[2:]
    dq_ref, keep, send = rest[:3]
    q_ref, qt_ref, g_ref, gt_ref, slots, keys, dense, row_sems, slot_sems, out_sem = rest[3:]
    b = pl.program_id(0)

    def loads(block):
        rows = pl.ds(block * BLK, BLK)
        return [
            pltpu.make_async_copy(q_hbm.at[:, rows], q_ref.at[block], row_sems.at[block, 0]),
            pltpu.make_async_copy(g_hbm.at[:, rows], g_ref.at[block], row_sems.at[block, 1]),
            pltpu.make_async_copy(qt_hbm.at[:, :, rows], qt_ref.at[block], row_sems.at[block, 2]),
            pltpu.make_async_copy(gt_hbm.at[:, :, rows], gt_ref.at[block], row_sems.at[block, 3]),
        ]

    def slot_load(block, s, piece, at):
        return pltpu.make_async_copy(
            piece.at[at], slots.at[block, s], slot_sems.at[block, s]
        )

    @pl.when(b == 0)
    def _():
        for block in range(2):
            for s in range(NSLOT):
                place = info[block, s]
                first = 0
                for piece, count in zip(pieces, PIECES):

                    @pl.when((place >= first) & (place < first + count))
                    def _(piece=piece, first=first, s=s, block=block, place=place):
                        slot_load(block, s, piece, place - first).start()

                    first += count

            for load in loads(block):
                load.start()

        def clear(i, carry):
            dense[i] = jnp.zeros((QW, BLK), jnp.bfloat16)
            return carry

        lax.fori_loop(0, NB, clear, 0)

    for s in range(NSLOT):
        slot_load(b, s, pieces[0], 0).wait()
        keys[:, s * BLK : (s + 1) * BLK] = slots[b, s]
    k = keys[...]
    rows = loads(b)
    rows[0].wait()
    rows[1].wait()

    row_pos = lax.broadcasted_iota(jnp.int32, (ROWS // 2, BLK), 0) % BLK
    key_pos = lax.broadcasted_iota(jnp.int32, (ROWS // 2, BLK), 1)
    all_dscores, all_low = [], []
    for half in range(2):
        heads = slice(half * HEADS_HERE // 2, (half + 1) * HEADS_HERE // 2)
        q = q_ref[b, heads].reshape(ROWS // 2, QW)
        g = g_ref[b, heads].reshape(ROWS // 2, LAT)
        scores = jnp.dot(q, k, preferred_element_type=jnp.float32)
        dprobs = jnp.dot(g, k[:LAT], preferred_element_type=jnp.float32)
        parts = []
        for s in range(NSLOT):
            part = scores[:, s * BLK : (s + 1) * BLK] * (SOFTMAX_SCALE * LOG2E)
            if s == 0:
                part = jnp.where(key_pos <= row_pos, part, MASKED)
            else:
                part = jnp.where(info[b, NSLOT + s] > 0, part, MASKED)
            parts.append(part)
        masked = jnp.concatenate(parts, axis=1)
        top = jnp.max(masked, axis=1, keepdims=True)
        expo = jnp.exp2(masked - top)
        probs = expo * (1.0 / jnp.sum(expo, axis=1, keepdims=True))
        delta = jnp.sum(probs * dprobs, axis=1, keepdims=True)
        all_dscores.append((probs * (dprobs - delta) * SOFTMAX_SCALE).astype(jnp.bfloat16))
        all_low.append(probs.astype(jnp.bfloat16))
    dscores = jnp.concatenate(all_dscores, axis=0)
    low = jnp.concatenate(all_low, axis=0)

    rows[2].wait()
    rows[3].wait()
    qt = jnp.concatenate([qt_ref[b, h] for h in range(HEADS_HERE)], axis=1)
    gt = jnp.concatenate([gt_ref[b, h] for h in range(HEADS_HERE)], axis=1)
    key_part = jnp.dot(qt, dscores, preferred_element_type=jnp.float32)
    value_part = jnp.dot(gt, low, preferred_element_type=jnp.float32)
    for s in range(NSLOT):
        cols = slice(s * BLK, (s + 1) * BLK)
        dest = info[b, 2 * NSLOT + s]
        head = dense[dest, :LAT].astype(jnp.float32) + key_part[:LAT, cols] + value_part[:, cols]
        tail = dense[dest, LAT:].astype(jnp.float32) + key_part[LAT:, cols]
        dense[dest, :LAT] = head.astype(jnp.bfloat16)
        dense[dest, LAT:] = tail.astype(jnp.bfloat16)

    def writes():
        each = 4
        return [
            pltpu.make_async_copy(
                dense.at[pl.ds(at, each)], out.at[pl.ds(at % 16, each)], out_sem
            )
            for at, out in ((i, send if i >= 16 else keep) for i in (16, 20, 24, 28, 0, 4, 8, 12))
        ]

    @pl.when(b == 1)
    def _():
        for write in writes():
            write.start()

    dq = lax.dot_general(
        dscores, k, (((1,), (1,)), ((), ())), preferred_element_type=jnp.float32
    ).astype(jnp.bfloat16)
    for h in range(HEADS_HERE):
        dq_ref[:, h] = dq[h * BLK : (h + 1) * BLK].reshape(8, 16, QW)

    @pl.when(b == 1)
    def _():
        for write in writes():
            write.wait()


def local_grads(info, q, qt, g, gt, pieces):
    hbm = pl.BlockSpec(memory_space=pltpu.HBM)
    return pl.pallas_call(
        kernel,
        grid_spec=pltpu.PrefetchScalarGridSpec(
            num_scalar_prefetch=1,
            grid=(2,),
            in_specs=[hbm] * 6,
            out_specs=[pl.BlockSpec((8, HEADS_HERE, 16, QW), lambda b, info: (b, 0, 0, 0))]
            + [hbm] * 2,
            scratch_shapes=[
                pltpu.VMEM((2, HEADS_HERE, BLK, QW), jnp.bfloat16),
                pltpu.VMEM((2, HEADS_HERE, QW, BLK), jnp.bfloat16),
                pltpu.VMEM((2, HEADS_HERE, BLK, LAT), jnp.bfloat16),
                pltpu.VMEM((2, HEADS_HERE, LAT, BLK), jnp.bfloat16),
                pltpu.VMEM((2, NSLOT, QW, BLK), jnp.bfloat16),
                pltpu.VMEM((QW, NSLOT * BLK), jnp.bfloat16),
                pltpu.VMEM((NB, QW, BLK), jnp.bfloat16),
                pltpu.SemaphoreType.DMA((2, 4)),
                pltpu.SemaphoreType.DMA((2, NSLOT)),
                pltpu.SemaphoreType.DMA,
            ],
        ),
        out_shape=[jax.ShapeDtypeStruct((16, HEADS_HERE, 16, QW), jnp.bfloat16)]
        + [jax.ShapeDtypeStruct((NB // 2, QW, BLK), jnp.bfloat16)] * 2,
        compiler_params=pltpu.CompilerParams(
            dimension_semantics=("arbitrary",), vmem_limit_bytes=58 * MIB
        ),
    )(info, q, qt, g, gt, *pieces)


def neighbour(x=0, y=0, z=0, core=0):
    pairs = []
    shape = dict(SPLIT)
    strides = {}
    step = 1
    for name in reversed(AXES):
        strides[name] = step
        step *= shape[name]
    for zl in range(shape["z_lo"]):
        for px in range(shape["x"]):
            for pc in range(shape["core"]):
                for py in range(shape["y"]):
                    for zh in range(shape["z_hi"]):

                        def index(zz, xx, cc, yy):
                            zz %= shape["z_lo"] * shape["z_hi"]
                            high, low = zz // shape["z_lo"], zz % shape["z_lo"]
                            return (
                                low * strides["z_lo"]
                                + (xx % shape["x"]) * strides["x"]
                                + (cc % 2) * strides["core"]
                                + (yy % shape["y"]) * strides["y"]
                                + high * strides["z_hi"]
                            )

                        zz = zh * shape["z_lo"] + zl
                        pairs.append((index(zz, px, pc, py), index(zz + z, px + x, pc + core, py + y)))
    return pairs


def other_z():
    shape = tuple(size for _, size in SPLIT)
    step = math.prod(shape[1:])
    return [(i, (i + step) % (2 * step)) for i in range(2 * step)]


RIGHT, LEFT = neighbour(x=1), neighbour(x=-1)
ALONG_Y = [neighbour(y=d) for d in range(4)]
UP, DOWN = neighbour(z=1), neighbour(z=-1)
SWAP = neighbour(core=1)
OTHER_Z = other_z()


def move(a, pairs):
    return lax.ppermute(a, AXES, pairs)


def pack_kernel(*refs):
    *pieces, out, sem = refs
    copies, at = [], 0
    for piece in pieces:
        n = piece.shape[0]
        copies.append(pltpu.make_async_copy(piece, out.at[pl.ds(at, n)], sem))
        at += n
    for copy in copies:
        copy.start()
    for copy in copies:
        copy.wait()


def pack(pieces):
    n = sum(piece.shape[0] for piece in pieces)
    return pl.pallas_call(
        pack_kernel,
        in_specs=[pl.BlockSpec(memory_space=pl.ANY)] * len(pieces),
        out_specs=pl.BlockSpec(memory_space=pl.ANY),
        out_shape=jax.ShapeDtypeStruct((n, QW, BLK), jnp.bfloat16),
        scratch_shapes=[pltpu.SemaphoreType.DMA],
        compiler_params=pltpu.CompilerParams(vmem_limit_bytes=4 * MIB),
    )(*pieces)


PLACES = (0, 2, 8, 4, 6, 10, 14, 12)
PIECES = (16, 16)


def copies_kernel(*refs):
    left, right, _, *outs, sem = refs
    parts = left, right, left.at[pl.ds(0, 1)], right.at[pl.ds(1, 1)]
    copies = [pltpu.make_async_copy(part, out, sem) for part, out in zip(parts, outs)]
    for copy in copies:
        copy.start()
    for copy in copies:
        copy.wait()


def copies_after(left, right, after):
    anywhere = pl.BlockSpec(memory_space=pl.ANY)
    return pl.pallas_call(
        copies_kernel,
        in_specs=[anywhere] * 3,
        out_specs=[anywhere] * 4,
        out_shape=[jax.ShapeDtypeStruct((n, QW, BLK), jnp.bfloat16) for n in (2, 2, 1, 1)],
        scratch_shapes=[pltpu.SemaphoreType.DMA],
        compiler_params=pltpu.CompilerParams(vmem_limit_bytes=4 * MIB),
    )(left, right, after)


def gather_keys(own, after):
    from_left, from_right, z_own = move(own, RIGHT), move(own, LEFT), move(own, OTHER_Z)
    from_left, from_right, to_right, to_left = copies_after(from_left, from_right, after)
    far = move(to_right, RIGHT), move(to_left, LEFT)
    z_left, z_right = move(from_left, UP), move(from_right, DOWN)
    z_far = move(far[0], UP), move(far[1], DOWN)
    mine = pack([own, from_right, from_left, z_own, *far, z_right, z_left, *z_far])
    return [mine, move(mine, SWAP)]


SUMS = ((8, 2), (10, 2), (6, 2), (12, 2), (4, 2), (14, 2), (0, 4))


def add_cores_kernel(keep, got, *rest):
    n = len(SUMS)
    outs, (ours, theirs, total, in_sems, out_sem) = rest[:n], rest[n:]
    loads, writes = [], []
    for i, (at, count) in enumerate(SUMS):
        part = pl.ds(at, count)
        loads.append(
            [
                pltpu.make_async_copy(keep.at[part], ours.at[part], in_sems.at[i]),
                pltpu.make_async_copy(got.at[part], theirs.at[part], in_sems.at[n + i]),
            ]
        )
        for load in loads[-1]:
            load.start()
    for i, (at, count) in enumerate(SUMS):
        for load in loads[i]:
            load.wait()
        part = slice(at, at + count)
        added = ours[part].astype(jnp.float32) + theirs[part].astype(jnp.float32)
        total[part] = added.astype(jnp.bfloat16)
        writes.append(pltpu.make_async_copy(total.at[pl.ds(at, count)], outs[i], out_sem))
        writes[-1].start()
    for write in writes:
        write.wait()


def add_cores(keep, got):
    hbm = pl.BlockSpec(memory_space=pltpu.HBM)
    return pl.pallas_call(
        add_cores_kernel,
        in_specs=[hbm, hbm],
        out_specs=[hbm] * len(SUMS),
        scratch_shapes=[pltpu.VMEM((16, QW, BLK), jnp.bfloat16)] * 3
        + [pltpu.SemaphoreType.DMA((2 * len(SUMS),)), pltpu.SemaphoreType.DMA],
        out_shape=[jax.ShapeDtypeStruct((count, QW, BLK), jnp.bfloat16) for _, count in SUMS],
        compiler_params=pltpu.CompilerParams(vmem_limit_bytes=24 * MIB),
    )(keep, got)


def total_of(refs, index):
    return sum(ref[index].astype(jnp.float32) for ref in refs)


def pass_on_kernel(right, from_left, left, from_right, right_out, left_out):
    right_out[...] = total_of((right, from_left), ...).astype(jnp.bfloat16)
    left_out[...] = total_of((left, from_right), ...).astype(jnp.bfloat16)


def pass_on(*parts):
    vmem = pl.BlockSpec(memory_space=pltpu.VMEM)
    return pl.pallas_call(
        pass_on_kernel,
        in_specs=[vmem] * 4,
        out_specs=[vmem] * 2,
        out_shape=[jax.ShapeDtypeStruct((2, QW, BLK), jnp.bfloat16)] * 2,
        compiler_params=pltpu.CompilerParams(vmem_limit_bytes=8 * MIB),
    )(*parts)


def add_x_kernel(y_ref, own, *refs):
    parts, outs, turned = (refs[:2], refs[2:4]), refs[4:8], refs[8]
    for z in range(2):
        for block in range(2):
            total = total_of(parts[z], block) + own[2 * z + block].astype(jnp.float32)
            rows = total.T.astype(jnp.bfloat16)
            turned[2 * block, z] = rows[: BLK // 2]
            turned[2 * block + 1, z] = rows[BLK // 2 :]
    for d in range(4):
        outs[d][...] = turned[(y_ref[0] + d) & 3]


def add_x(my_y, parts):
    vmem = pl.BlockSpec(memory_space=pltpu.VMEM)
    shape = (2, BLK // 2, QW)
    return pl.pallas_call(
        add_x_kernel,
        grid_spec=pltpu.PrefetchScalarGridSpec(
            num_scalar_prefetch=1,
            grid=(),
            in_specs=[vmem] * 5,
            out_specs=[vmem] * 4,
            scratch_shapes=[pltpu.VMEM((4, *shape), jnp.bfloat16)],
        ),
        out_shape=[jax.ShapeDtypeStruct(shape, jnp.bfloat16)] * 4,
        compiler_params=pltpu.CompilerParams(vmem_limit_bytes=16 * MIB),
    )(my_y, *parts)


def add_y_kernel(*refs):
    *parts, out = refs
    out[...] = total_of(parts, ...).astype(jnp.bfloat16)


def add_y(parts):
    vmem = pl.BlockSpec(memory_space=pltpu.VMEM)
    return pl.pallas_call(
        add_y_kernel,
        in_specs=[vmem] * 4,
        out_specs=vmem,
        out_shape=jax.ShapeDtypeStruct((2, BLK // 2, QW), jnp.bfloat16),
        compiler_params=pltpu.CompilerParams(vmem_limit_bytes=8 * MIB),
    )(*parts)


def spread(parts, moves):
    return [parts[0]] + [move(parts[d], moves[d]) for d in (1, 2, 3)]


def on_device(queries, latent, grad_out, advantage, ancestors):
    qt = jnp.transpose(queries, (1, 2, 0))
    own_keys = jnp.swapaxes(latent.reshape(2, BLK, QW), 1, 2)
    q, g, gt = prepare(qt, grad_out, advantage)
    pieces = gather_keys(own_keys, gt)

    my_z, my_x, my_core = (lax.axis_index(name) for name in CTX)
    own = lax.axis_index(CTX) * 2 + jnp.arange(2, dtype=jnp.int32)
    slots = jnp.concatenate([own[:, None], ancestors], axis=1)
    present = (slots >= 0).astype(jnp.int32)
    n = jnp.maximum(slots, 0)
    z, x, c, block = n // 16, (n // 4) % 4, (n // 2) % 2, n % 2
    dz, dx, dc = z ^ my_z, (x - my_x) & 3, c ^ my_core
    offset = dz * 4 + dx
    place = dc * 16 + sum(jnp.where(offset == i, at, 0) for i, at in enumerate(PLACES)) + block
    dest = dc * 16 + dx * 4 + z * 2 + block
    info = jnp.concatenate([place, present, dest], axis=1)

    dq, keep, send = local_grads(info, q, qt, g, gt, pieces)

    far_right, far_left, right, left, right_late, left_late, own = add_cores(keep, move(send, SWAP))
    from_left, from_right = move(far_right, RIGHT), move(far_left, LEFT)
    near = move(right, RIGHT), move(left, LEFT)
    on_right, on_left = pass_on(right_late, from_left, left_late, from_right)
    late = move(on_right, RIGHT), move(on_left, LEFT)
    parts = [own, late[0], near[1], near[0], late[1]]
    parts = spread(add_x(lax.axis_index("y")[None], parts), ALONG_Y)
    rows = add_y(parts).reshape(128, QW)
    rows = lax.all_to_all(rows, ("z_lo", "z_hi"), split_axis=0, concat_axis=0, tiled=True)
    latent_grad = jnp.sum(rows.reshape(8, 16, QW).astype(jnp.float32), axis=0)

    dq = lax.all_to_all(dq, HEAD, split_axis=0, concat_axis=0, tiled=True)
    query_grad = jnp.transpose(dq.reshape(64, 16, QW), (1, 0, 2))
    return query_grad, latent_grad


def solution(mesh):
    fine = Mesh(mesh.devices.reshape(SIZES), AXES)
    in_specs = (P(CTX, HEAD, None), P(CTX, None), P(CTX, HEAD, None), P(CTX), P(CTX, None))
    out_specs = (P(CTX + HEAD, None, None), P(CTX + HEAD, None))
    return jax.shard_map(
        on_device, mesh=fine, in_specs=in_specs, out_specs=out_specs, check_vma=False
    )
```

time: 125 us -> 118 us (0.944); the launches traced: 123 us -> 118 us
  waiting for transfers between devices: 47.1 us -> 40 us
  Pallas kernels: 22 us -> 25.5 us
  starting transfers between devices: 39.1 us -> 42.6 us
  local copies, waits for them, and re-layouts: 9.82 us -> 6.84 us
  other arithmetic: 4.21 us -> 1.65 us
    ppermute x16 -> x20, waiting for transfers between devices: 42 us -> 34.2 us  [move(): return lax.ppermute(a, AXES, pairs)]
    ppermute x16 -> x20, starting transfers between devices: 21.8 us -> 26.1 us  [move(): return lax.ppermute(a, AXES, pairs)]
    pallas_call x2 -> x5, Pallas kernels: 20.3 us -> 23.2 us  [the longest x1 16.1 us: local_grads(): pl.pallas_call(kernel, grid_spec=pltpu.PrefetchScalarGridSpec(num_scalar_...]
    all_to_all x1, starting transfers between devices: 10.3 us -> 7.45 us  [on_device(): dq = lax.all_to_all(dq, HEAD, split_axis=0, concat_axis=0, tiled=True)]
    transpose x1 -> x0, other arithmetic: 2.77 us -> none  [on_device(): jnp.transpose(weighted, (1, 2, 0))]
    optimization_barrier x1 -> x0, local copies, waits for them, and re-layouts: 2.3 us -> none  [gather_keys(): lax.optimization_barrier((first, beside))]
    all_to_all x1, starting transfers between devices: 7.05 us -> 9.06 us  [on_device(): lax.all_to_all(rows, ('z_lo', 'z_hi'), split_axis=0, concat_axis=0, tiled...]
    unnamed x16 -> x20, local copies, waits for them, and re-layouts: 4.84 us -> 4.16 us
  transfers between devices with their start and end apart: 18 -> 22, of which waited for: 9 -> 12; matrix products, arithmetic and copies ran while one was open for 10% -> 3% of each run, Pallas kernels for 4% -> 7%
where the time goes in v3:
time: 118 us
  starting transfers between devices  42.6 us (36%)
  waiting for transfers between devices  40 us (34%)
  Pallas kernels  25.5 us (22%)
  local copies, waits for them, and re-layouts  6.84 us (6%)
  other arithmetic  1.65 us (1%)
    ppermute x20, waiting for transfers between devices, move(): return lax.ppermute(a, AXES, pairs)  34.2 us
    ppermute x20, starting transfers between devices, move(): return lax.ppermute(a, AXES, pairs)  26.1 us
    pallas_call x1, Pallas kernels, local_grads(): pl.pallas_call(kernel, grid_spec=pltpu.PrefetchScalarGridSpec(num_scalar_...  16.1 us
    all_to_all x1, starting transfers between devices, on_device(): lax.all_to_all(rows, ('z_lo', 'z_hi'), split_axis=0, concat_axis=0, tiled...  9.06 us
    all_to_all x1, starting transfers between devices, on_device(): dq = lax.all_to_all(dq, HEAD, split_axis=0, concat_axis=0, tiled=True)  7.45 us
    all_to_all x1, waiting for transfers between devices, on_device(): lax.all_to_all(rows, ('z_lo', 'z_hi'), split_axis=0, concat_axis=0, tiled...  5.81 us
    unnamed x20, local copies, waits for them, and re-layouts  4.16 us
    pallas_call x1, Pallas kernels, prepare(): pl.pallas_call(prepare_kernel, in_specs=[pl.BlockSpec(memory_space=pltpu....  4.15 us
  transfers between devices with their start and end apart: 22, of which 12 were waited for; matrix products, arithmetic and copies ran while one was open for 3% of the time, Pallas kernels for 7%

profile of v3, /device:TPU:40, one launch (start us, length us, event | category | flops | bytes accessed | tf_op | source)
XLA Modules:
  0.0 117.6 jit_solution(2261554991801559957)
XLA Ops:
  0.6 0.0 copy-start
  0.6 1.0 copy-done
  1.6 2.8 %collective-permute-start.1 = (bf16[2,576,128]{2,1,0:T(8,128)(2,1)S(1)}, bf16[2,576,128]{2,1,0:T(8,128)(2,1)S(1)}, u32[]{:S(2)}, u32[]{:S(2)}) collective-permute-start(bf16[2,576,128]{2,1,0:T(8,128)(2,1)S(1)} %bitcast_bitcast_fusion.refs_0_), channel_id=1, source_target_pairs={{0,96},{1,97},{2,98},{3,99},{4,100},{5,101},{6,102},{7,103},{8,104... | collective-permute-start | bytes 884744 | tf_op jit(solution)/shard_map/ppermute | solution.py:269
  4.5 0.0 collective-permute-start
  4.5 0.1 collective-permute-start.2
  4.6 1.3 %copy-done.2 = bf16[256,4,576]{0,2,1:T(8,128)(2,1)S(1)} copy-done((bf16[256,4,576]{0,2,1:T(8,128)(2,1)S(1)}, bf16[256,4,576]{0,2,1:T(8,128)(2,1)}, u32[]{:S(2)}) %copy-start.2) | copy-done | bytes 1179672
  5.8 1.2 %copy-done.7 = bf16[256,4,512]{2,1,0:T(4,128)(2,1)S(1)} copy-done((bf16[256,4,512]{2,1,0:T(4,128)(2,1)S(1)}, bf16[256,4,512]{2,1,0:T(4,128)(2,1)}, u32[]{:S(2)}) %copy-start.7) | copy-done | bytes 1048600
  7.1 0.7 copy-done.8
  7.7 4.1 %shard_map.68 = (bf16[4,256,576]{2,1,0:T(8,128)(2,1)S(1)}, bf16[4,256,512]{2,1,0:T(8,128)(2,1)S(1)}, bf16[4,512,256]{2,1,0:T(8,128)(2,1)S(1)}) custom-call(f32[1,256]{1,0:T(1,128)S(1)} %bitcast.17, bf16[4,576,256]{2,1,0:T(8,128)(2,1)S(1)} %bitcast.16, bf16[256,4,512]{2,1,0:T(4,128)(2,1)S(1)} %copy-done.7), custom_call_target="tpu_custom_call" | custom-call | tf_op jit(solution)/shard_map/pallas_call | solution.py:65
  11.9 0.0 copy-start.3
  11.9 0.0 copy-start.5
  11.9 0.0 collective-permute-done.1.refs_1_
  11.9 2.2 %collective-permute-done.refs_0_ = bf16[2,576,128]{2,1,0:T(8,128)(2,1)S(1)} collective-permute-done((bf16[2,576,128]{2,1,0:T(8,128)(2,1)S(1)}, bf16[2,576,128]{2,1,0:T(8,128)(2,1)S(1)}, u32[]{:S(2)}, u32[]{:S(2)}) %collective-permute-start) | collective-permute-done | bytes 294944 | tf_op jit(solution)/shard_map/ppermute | solution.py:269
  14.1 0.5 shard_map.69
  14.6 0.1 collective-permute-start.3
  14.7 3.2 %collective-permute-start.4 = (bf16[1,576,128]{2,1,0:T(8,128)(2,1)S(1)}, bf16[1,576,128]{2,1,0:T(8,128)(2,1)S(1)}, u32[]{:S(2)}, u32[]{:S(2)}) collective-permute-start(bf16[1,576,128]{2,1,0:T(8,128)(2,1)S(1)} %get-tuple-element.31), channel_id=1, source_target_pairs={{0,96},{1,97},{2,98},{3,99},{4,100},{5,101},{6,102},{7,103},{8,104... | collective-permute-start | bytes 442376 | tf_op jit(solution)/shard_map/ppermute | solution.py:269
  18.0 0.1 collective-permute-start.5
  18.1 1.9 %collective-permute-start.6 = (bf16[2,576,128]{2,1,0:T(8,128)(2,1)S(1)}, bf16[2,576,128]{2,1,0:T(8,128)(2,1)S(1)}, u32[]{:S(2)}, u32[]{:S(2)}) collective-permute-start(bf16[2,576,128]{2,1,0:T(8,128)(2,1)S(1)} %get-tuple-element.29.refs_2_), channel_id=1, source_target_pairs={{0,128},{1,129},{2,130},{3,131},{4,132},{5,133},{6,134},{7,135},{8... | collective-permute-start | bytes 884744 | tf_op jit(solution)/shard_map/ppermute | solution.py:269
  20.0 1.1 collective-permute-done.3.refs_4_
  21.1 1.9 %collective-permute-start.7 = (bf16[1,576,128]{2,1,0:T(8,128)(2,1)S(1)}, bf16[1,576,128]{2,1,0:T(8,128)(2,1)S(1)}, u32[]{:S(2)}, u32[]{:S(2)}) collective-permute-start(bf16[1,576,128]{2,1,0:T(8,128)(2,1)S(1)} %collective-permute-done.3.refs_4_), channel_id=1, source_target_pairs={{0,128},{1,129},{2,130},{3,131},{4,132},{5,133},{6,134},{7,135},{8... | collective-permute-start | bytes 442376 | tf_op jit(solution)/shard_map/ppermute | solution.py:269
  23.0 0.0 collective-permute-done.4.refs_5_
  23.0 1.1 collective-permute-start.8
  24.1 0.0 collective-permute-done.2.refs_3_
  24.1 7.9 %collective-permute-done.7.refs_8_ = bf16[1,576,128]{2,1,0:T(8,128)(2,1)S(1)} collective-permute-done((bf16[1,576,128]{2,1,0:T(8,128)(2,1)S(1)}, bf16[1,576,128]{2,1,0:T(8,128)(2,1)S(1)}, u32[]{:S(2)}, u32[]{:S(2)}) %collective-permute-start.7) | collective-permute-done | bytes 147488 | tf_op jit(solution)/shard_map/ppermute | solution.py:269
  32.1 0.0 collective-permute-done.8.refs_9_
  32.1 0.0 collective-permute-done.5.refs_6_
  32.1 0.0 collective-permute-done.6.refs_7_
  32.1 1.1 shard_map.70.rest_0_
  33.2 0.0 copy-done.3
  33.3 0.3 collective-permute-start.9
  33.6 0.1 fusion.11
  33.7 0.9 pad_add_fusion.1.info
  34.6 3.6 %collective-permute-done.9.rest_1_ = bf16[16,576,128]{2,1,0:T(8,128)(2,1)} collective-permute-done((bf16[16,576,128]{2,1,0:T(8,128)(2,1)S(1)}, bf16[16,576,128]{2,1,0:T(8,128)(2,1)}, u32[]{:S(2)}, u32[]{:S(2)}) %collective-permute-start.9) | collective-permute-done | bytes 2359328 | tf_op jit(solution)/shard_map/ppermute | solution.py:269
  38.2 16.1 %shard_map.71 = (bf16[16,4,16,576]{3,2,1,0:T(8,128)(2,1)}, bf16[16,576,128]{2,1,0:T(8,128)(2,1)}, bf16[16,576,128]{2,1,0:T(8,128)(2,1)}) custom-call(s32[2,27]{1,0:T(2,128)} %pad_add_fusion.1.info, bf16[4,256,576]{2,1,0:T(8,128)(2,1)} %copy-done.5, bf16[4,576,256]{2,1,0:T(8,128)(2,1)} %bitcast.15, bf16[4,256,512]{2,1,0:T(8,128)(2,1)} %copy-done.6, ...), custom_call_target="tpu_custom_call" | custom-call | tf_op jit(solution)/shard_map/pallas_call | solution.py:196
  54.3 1.0 collective-permute-start.10
  55.3 7.4 %all-to-all-start = ((bf16[16,4,16,576]{3,2,1,0:T(8,128)(2,1)}), bf16[16,4,16,576]{3,2,1,0:T(8,128)(2,1)}, u32[]{:S(2)}, u32[]{:S(2)}) async-start(bf16[16,4,16,576]{3,2,1,0:T(8,128)(2,1)} %get-tuple-element.32), calls=%async_computation | async-start | bytes 2621440 | tf_op jit(solution)/shard_map/all_to_all | solution.py:475
  62.8 0.0 collective-permute-done.10.got
  62.8 2.3 %shard_map.72 = (bf16[2,576,128]{2,1,0:T(8,128)(2,1)S(1)}, bf16[2,576,128]{2,1,0:T(8,128)(2,1)S(1)}, bf16[2,576,128]{2,1,0:T(8,128)(2,1)S(1)}, bf16[2,576,128]{2...) custom-call(bf16[16,576,128]{2,1,0:T(8,128)(2,1)S(1)} %copy-done.4, ...), custom_call_target="tpu_custom_call" | custom-call | tf_op jit(solution)/shard_map/pallas_call | solution.py:364
  65.1 0.1 collective-permute-start.11
  65.2 3.2 %collective-permute-start.12 = (bf16[2,576,128]{2,1,0:T(8,128)(2,1)S(1)}, bf16[2,576,128]{2,1,0:T(8,128)(2,1)S(1)}, u32[]{:S(2)}, u32[]{:S(2)}) collective-permute-start(bf16[2,576,128]{2,1,0:T(8,128)(2,1)S(1)} %get-tuple-element.39), channel_id=1, source_target_pairs={{0,96},{1,97},{2,98},{3,99},{4,100},{5,101},{6,102},{7,103},{8,104... | collective-permute-start | bytes 884744 | tf_op jit(solution)/shard_map/ppermute | solution.py:269
  68.4 0.0 collective-permute-start.14
  68.5 2.0 %collective-permute-start.15 = (bf16[2,576,128]{2,1,0:T(8,128)(2,1)S(1)}, bf16[2,576,128]{2,1,0:T(8,128)(2,1)S(1)}, u32[]{:S(2)}, u32[]{:S(2)}) collective-permute-start(bf16[2,576,128]{2,1,0:T(8,128)(2,1)S(1)} %get-tuple-element.42), channel_id=1, source_target_pairs={{0,32},{1,33},{2,34},{3,35},{4,36},{5,37},{6,38},{7,39},{8,40},{9,... | collective-permute-start | bytes 884744 | tf_op jit(solution)/shard_map/ppermute | solution.py:269
  70.5 5.9 %collective-permute-done.11.from_left = bf16[2,576,128]{2,1,0:T(8,128)(2,1)S(1)} collective-permute-done((bf16[2,576,128]{2,1,0:T(8,128)(2,1)S(1)}, bf16[2,576,128]{2,1,0:T(8,128)(2,1)S(1)}, u32[]{:S(2)}, u32[]{:S(2)}) %collective-permute-start.11) | collective-permute-done | bytes 294944 | tf_op jit(solution)/shard_map/ppermute | solution.py:269
  76.3 0.0 collective-permute-done.12.from_right
  76.3 0.1 shard_map.73
  76.5 0.1 collective-permute-start.13
  76.6 3.3 %collective-permute-start.16 = (bf16[2,576,128]{2,1,0:T(8,128)(2,1)S(1)}, bf16[2,576,128]{2,1,0:T(8,128)(2,1)S(1)}, u32[]{:S(2)}, u32[]{:S(2)}) collective-permute-start(bf16[2,576,128]{2,1,0:T(8,128)(2,1)S(1)} %get-tuple-element.43), channel_id=1, source_target_pairs={{0,96},{1,97},{2,98},{3,99},{4,100},{5,101},{6,102},{7,103},{8,104... | collective-permute-start | bytes 884744 | tf_op jit(solution)/shard_map/ppermute | solution.py:269
  79.9 2.4 %collective-permute-done.14.refs_1_ = bf16[2,576,128]{2,1,0:T(8,128)(2,1)S(1)} collective-permute-done((bf16[2,576,128]{2,1,0:T(8,128)(2,1)}, bf16[2,576,128]{2,1,0:T(8,128)(2,1)S(1)}, u32[]{:S(2)}, u32[]{:S(2)}) %collective-permute-start.14) | collective-permute-done | bytes 294944 | tf_op jit(solution)/shard_map/ppermute | solution.py:269
  82.3 0.3 collective-permute-done.15.refs_2_
  82.7 4.9 %collective-permute-done.13.refs_0_ = bf16[2,576,128]{2,1,0:T(8,128)(2,1)S(1)} collective-permute-done((bf16[2,576,128]{2,1,0:T(8,128)(2,1)S(1)}, bf16[2,576,128]{2,1,0:T(8,128)(2,1)S(1)}, u32[]{:S(2)}, u32[]{:S(2)}) %collective-permute-start.13) | collective-permute-done | bytes 294944 | tf_op jit(solution)/shard_map/ppermute | solution.py:269
  87.6 0.0 collective-permute-done.16.refs_3_
  87.6 0.4 shard_map.74
  88.0 1.5 %collective-permute-start.17 = (bf16[2,64,576]{2,1,0:T(8,128)(2,1)S(1)}, bf16[2,64,576]{2,1,0:T(8,128)(2,1)S(1)}, u32[]{:S(2)}, u32[]{:S(2)}) collective-permute-start(bf16[2,64,576]{2,1,0:T(8,128)(2,1)S(1)} %get-tuple-element.45), channel_id=1, source_target_pairs={{0,4},{1,5},{2,6},{3,7},{4,8},{5,9},{6,10},{7,11},{8,12},{9,13},{1... | collective-permute-start | bytes 442376 | tf_op jit(solution)/shard_map/ppermute | solution.py:269
  89.5 1.0 collective-permute-start.18
  90.6 2.2 %collective-permute-start.19 = (bf16[2,64,576]{2,1,0:T(8,128)(2,1)S(1)}, bf16[2,64,576]{2,1,0:T(8,128)(2,1)S(1)}, u32[]{:S(2)}, u32[]{:S(2)}) collective-permute-start(bf16[2,64,576]{2,1,0:T(8,128)(2,1)S(1)} %get-tuple-element.47), channel_id=1, source_target_pairs={{0,12},{1,13},{2,14},{3,15},{4,0},{5,1},{6,2},{7,3},{8,4},{9,5},{1... | collective-permute-start | bytes 442376 | tf_op jit(solution)/shard_map/ppermute | solution.py:269
  92.8 3.9 %collective-permute-done.17.refs_1_ = bf16[2,64,576]{2,1,0:T(8,128)(2,1)S(1)} collective-permute-done((bf16[2,64,576]{2,1,0:T(8,128)(2,1)S(1)}, bf16[2,64,576]{2,1,0:T(8,128)(2,1)S(1)}, u32[]{:S(2)}, u32[]{:S(2)}) %collective-permute-start.17) | collective-permute-done | bytes 147488 | tf_op jit(solution)/shard_map/ppermute | solution.py:269
  96.7 0.8 collective-permute-done.18.refs_2_
  97.5 1.2 collective-permute-done.19.refs_3_
  98.6 0.7 shard_map.75
  99.4 0.0 all-to-all-done
  99.4 9.1 %all-to-all-start.1 = ((bf16[8,16,576]{2,1,0:T(8,128)(2,1)}), bf16[8,16,576]{2,1,0:T(8,128)(2,1)S(1)}, u32[]{:S(2)}, u32[]{:S(2)}) async-start(bf16[8,16,576]{2,1,0:T(8,128)(2,1)} %bitcast.6), calls=%async_computation.1 | async-start | bytes 327680 | tf_op jit(solution)/shard_map/all_to_all | solution.py:472
  108.4 2.7 %copy.13 = bf16[64,16,576]{2,0,1:T(8,128)(2,1)} copy(bf16[64,16,576]{2,1,0:T(8,128)(2,1)} %bitcast.3) | data formatting | bytes 2359296 | tf_op jit(solution)/shard_map/reshape | solution.py:476
  111.1 5.8 %all-to-all-done.1 = bf16[8,16,576]{2,1,0:T(8,128)(2,1)S(1)} async-done(((bf16[8,16,576]{2,1,0:T(8,128)(2,1)}), bf16[8,16,576]{2,1,0:T(8,128)(2,1)S(1)}, u32[]{:S(2)}, u32[]{:S(2)}) %all-to-all-start.1) | async-done | bytes 147488 | tf_op jit(solution)/shard_map/all_to_all | solution.py:472
  116.9 0.6 convert_reduce_fusion
  (16 shorter events, 0.1 us)
Async XLA Ops:
  0.6 1.0 copy-start
  1.6 10.3 %collective-permute-start.1 = (bf16[2,576,128]{2,1,0:T(8,128)(2,1)S(1)}, bf16[2,576,128]{2,1,0:T(8,128)(2,1)S(1)}, u32[]{:S(2)}, u32[]{:S(2)}) collective-permute-start(bf16[2,576,128]{2,1,0:T(8,128)(2,1)S(1)} %bitcast_bitcast_fusion.refs_0_), channel_id=1, source_target_pairs={{0,96},{1,97},{2,98},{3,99},{4,100},{5,101},{6,102},{7,103},{8,104... | collective-permute-start | bytes 884744 | tf_op jit(solution)/shard_map/ppermute | solution.py:269
  4.5 9.7 %collective-permute-start = (bf16[2,576,128]{2,1,0:T(8,128)(2,1)S(1)}, bf16[2,576,128]{2,1,0:T(8,128)(2,1)S(1)}, u32[]{:S(2)}, u32[]{:S(2)}) collective-permute-start(bf16[2,576,128]{2,1,0:T(8,128)(2,1)S(1)} %bitcast_bitcast_fusion.refs_0_), channel_id=1, source_target_pairs={{0,32},{1,33},{2,34},{3,35},{4,36},{5,37},{6,38},{7,39},{8,40},{9,... | collective-permute-start | bytes 884744 | tf_op jit(solution)/shard_map/ppermute | solution.py:269
  4.5 19.7 %collective-permute-start.2 = (bf16[2,576,128]{2,1,0:T(8,128)(2,1)S(1)}, bf16[2,576,128]{2,1,0:T(8,128)(2,1)S(1)}, u32[]{:S(2)}, u32[]{:S(2)}) collective-permute-start(bf16[2,576,128]{2,1,0:T(8,128)(2,1)S(1)} %bitcast_bitcast_fusion.refs_0_), channel_id=1, source_target_pairs={{0,128},{1,129},{2,130},{3,131},{4,132},{5,133},{6,134},{7,135},{8... | collective-permute-start | bytes 884744 | tf_op jit(solution)/shard_map/ppermute | solution.py:269
  4.6 1.3 %copy-start.2 = (bf16[256,4,576]{0,2,1:T(8,128)(2,1)S(1)}, bf16[256,4,576]{0,2,1:T(8,128)(2,1)}, u32[]{:S(2)}) copy-start(bf16[256,4,576]{0,2,1:T(8,128)(2,1)} %param.5) | copy-start | bytes 3538948
  5.8 1.2 %copy-start.7 = (bf16[256,4,512]{2,1,0:T(4,128)(2,1)S(1)}, bf16[256,4,512]{2,1,0:T(4,128)(2,1)}, u32[]{:S(2)}) copy-start(bf16[256,4,512]{2,1,0:T(4,128)(2,1)} %grad_hbm.1) | copy-start | bytes 3145732
  7.1 0.7 copy-start.8
  11.9 21.3 %copy-start.3 = (bf16[4,512,256]{2,1,0:T(8,128)(2,1)}, bf16[4,512,256]{2,1,0:T(8,128)(2,1)S(1)}, u32[]{:S(2)}) copy-start(bf16[4,512,256]{2,1,0:T(8,128)(2,1)S(1)} %get-tuple-element.27.refs_2_.gt_hbm) | copy-start | bytes 3145732
  11.9 21.3 %copy-start.5 = (bf16[4,256,576]{2,1,0:T(8,128)(2,1)}, bf16[4,256,576]{2,1,0:T(8,128)(2,1)S(1)}, u32[]{:S(2)}) copy-start(bf16[4,256,576]{2,1,0:T(8,128)(2,1)S(1)} %get-tuple-element.25.q_hbm) | copy-start | bytes 3538948
  11.9 21.3 %copy-start.6 = (bf16[4,256,512]{2,1,0:T(8,128)(2,1)}, bf16[4,256,512]{2,1,0:T(8,128)(2,1)S(1)}, u32[]{:S(2)}) copy-start(bf16[4,256,512]{2,1,0:T(8,128)(2,1)S(1)} %get-tuple-element.26.g_hbm) | copy-start | bytes 3145732
  14.6 6.4 %collective-permute-start.3 = (bf16[1,576,128]{2,1,0:T(8,128)(2,1)S(1)}, bf16[1,576,128]{2,1,0:T(8,128)(2,1)S(1)}, u32[]{:S(2)}, u32[]{:S(2)}) collective-permute-start(bf16[1,576,128]{2,1,0:T(8,128)(2,1)S(1)} %get-tuple-element.30), channel_id=1, source_target_pairs={{0,32},{1,33},{2,34},{3,35},{4,36},{5,37},{6,38},{7,39},{8,40},{9,... | collective-permute-start | bytes 442376 | tf_op jit(solution)/shard_map/ppermute | solution.py:269
  14.7 8.3 %collective-permute-start.4 = (bf16[1,576,128]{2,1,0:T(8,128)(2,1)S(1)}, bf16[1,576,128]{2,1,0:T(8,128)(2,1)S(1)}, u32[]{:S(2)}, u32[]{:S(2)}) collective-permute-start(bf16[1,576,128]{2,1,0:T(8,128)(2,1)S(1)} %get-tuple-element.31), channel_id=1, source_target_pairs={{0,96},{1,97},{2,98},{3,99},{4,100},{5,101},{6,102},{7,103},{8,104... | collective-permute-start | bytes 442376 | tf_op jit(solution)/shard_map/ppermute | solution.py:269
  18.0 14.1 %collective-permute-start.5 = (bf16[2,576,128]{2,1,0:T(8,128)(2,1)S(1)}, bf16[2,576,128]{2,1,0:T(8,128)(2,1)S(1)}, u32[]{:S(2)}, u32[]{:S(2)}) collective-permute-start(bf16[2,576,128]{2,1,0:T(8,128)(2,1)S(1)} %get-tuple-element.28.refs_1_), channel_id=1, source_target_pairs={{0,131},{1,128},{2,129},{3,130},{4,135},{5,132},{6,133},{7,134},{8... | collective-permute-start | bytes 884744 | tf_op jit(solution)/shard_map/ppermute | solution.py:269
  18.1 15.5 %copy-start.9 = (s32[2,8]{1,0:T(2,128)S(1)}, s32[2,8]{1,0:T(2,128)}, u32[]{:S(2)}) copy-start(s32[2,8]{1,0:T(2,128)} %param.9) | copy-start | bytes 196
  18.1 14.0 %collective-permute-start.6 = (bf16[2,576,128]{2,1,0:T(8,128)(2,1)S(1)}, bf16[2,576,128]{2,1,0:T(8,128)(2,1)S(1)}, u32[]{:S(2)}, u32[]{:S(2)}) collective-permute-start(bf16[2,576,128]{2,1,0:T(8,128)(2,1)S(1)} %get-tuple-element.29.refs_2_), channel_id=1, source_target_pairs={{0,128},{1,129},{2,130},{3,131},{4,132},{5,133},{6,134},{7,135},{8... | collective-permute-start | bytes 884744 | tf_op jit(solution)/shard_map/ppermute | solution.py:269
  21.1 11.0 %collective-permute-start.7 = (bf16[1,576,128]{2,1,0:T(8,128)(2,1)S(1)}, bf16[1,576,128]{2,1,0:T(8,128)(2,1)S(1)}, u32[]{:S(2)}, u32[]{:S(2)}) collective-permute-start(bf16[1,576,128]{2,1,0:T(8,128)(2,1)S(1)} %collective-permute-done.3.refs_4_), channel_id=1, source_target_pairs={{0,128},{1,129},{2,130},{3,131},{4,132},{5,133},{6,134},{7,135},{8... | collective-permute-start | bytes 442376 | tf_op jit(solution)/shard_map/ppermute | solution.py:269
  23.0 9.1 %collective-permute-start.8 = (bf16[1,576,128]{2,1,0:T(8,128)(2,1)S(1)}, bf16[1,576,128]{2,1,0:T(8,128)(2,1)S(1)}, u32[]{:S(2)}, u32[]{:S(2)}) collective-permute-start(bf16[1,576,128]{2,1,0:T(8,128)(2,1)S(1)} %collective-permute-done.4.refs_5_), channel_id=1, source_target_pairs={{0,131},{1,128},{2,129},{3,130},{4,135},{5,132},{6,133},{7,134},{8... | collective-permute-start | bytes 442376 | tf_op jit(solution)/shard_map/ppermute | solution.py:269
  33.3 4.9 %copy-start.1 = (bf16[16,576,128]{2,1,0:T(8,128)(2,1)}, bf16[16,576,128]{2,1,0:T(8,128)(2,1)S(1)}, u32[]{:S(2)}) copy-start(bf16[16,576,128]{2,1,0:T(8,128)(2,1)S(1)} %shard_map.70.rest_0_) | copy-start | bytes 7077892
  33.3 4.9 %collective-permute-start.9 = (bf16[16,576,128]{2,1,0:T(8,128)(2,1)S(1)}, bf16[16,576,128]{2,1,0:T(8,128)(2,1)}, u32[]{:S(2)}, u32[]{:S(2)}) collective-permute-start(bf16[16,576,128]{2,1,0:T(8,128)(2,1)S(1)} %shard_map.70.rest_0_), channel_id=1, source_target_pairs={{0,16},{1,17},{2,18},{3,19},{4,20},{5,21},{6,22},{7,23},{8,24},{9,... | collective-permute-start | bytes 7077896 | tf_op jit(solution)/shard_map/ppermute | solution.py:269
  54.3 8.5 %copy-start.4 = (bf16[16,576,128]{2,1,0:T(8,128)(2,1)S(1)}, bf16[16,576,128]{2,1,0:T(8,128)(2,1)}, u32[]{:S(2)}) copy-start(bf16[16,576,128]{2,1,0:T(8,128)(2,1)} %get-tuple-element.33.keep) | copy-start | bytes 7077892
  54.3 8.5 %collective-permute-start.10 = (bf16[16,576,128]{2,1,0:T(8,128)(2,1)}, bf16[16,576,128]{2,1,0:T(8,128)(2,1)}, u32[]{:S(2)}, u32[]{:S(2)}) collective-permute-start(bf16[16,576,128]{2,1,0:T(8,128)(2,1)} %get-tuple-element.34), channel_id=1, source_target_pairs={{0,16},{1,17},{2,18},{3,19},{4,20},{5,21},{6,22},{7,23},{8,24},{9,... | collective-permute-start | bytes 7077896 | tf_op jit(solution)/shard_map/ppermute | solution.py:269
  55.3 44.1 %all-to-all-start = ((bf16[16,4,16,576]{3,2,1,0:T(8,128)(2,1)}), bf16[16,4,16,576]{3,2,1,0:T(8,128)(2,1)}, u32[]{:S(2)}, u32[]{:S(2)}) async-start(bf16[16,4,16,576]{3,2,1,0:T(8,128)(2,1)} %get-tuple-element.32), calls=%async_computation | async-start | bytes 2621440 | tf_op jit(solution)/shard_map/all_to_all | solution.py:475
  65.1 11.2 %collective-permute-start.11 = (bf16[2,576,128]{2,1,0:T(8,128)(2,1)S(1)}, bf16[2,576,128]{2,1,0:T(8,128)(2,1)S(1)}, u32[]{:S(2)}, u32[]{:S(2)}) collective-permute-start(bf16[2,576,128]{2,1,0:T(8,128)(2,1)S(1)} %get-tuple-element.37), channel_id=1, source_target_pairs={{0,32},{1,33},{2,34},{3,35},{4,36},{5,37},{6,38},{7,39},{8,40},{9,... | collective-permute-start | bytes 884744 | tf_op jit(solution)/shard_map/ppermute | solution.py:269
  65.2 11.1 %collective-permute-start.12 = (bf16[2,576,128]{2,1,0:T(8,128)(2,1)S(1)}, bf16[2,576,128]{2,1,0:T(8,128)(2,1)S(1)}, u32[]{:S(2)}, u32[]{:S(2)}) collective-permute-start(bf16[2,576,128]{2,1,0:T(8,128)(2,1)S(1)} %get-tuple-element.39), channel_id=1, source_target_pairs={{0,96},{1,97},{2,98},{3,99},{4,100},{5,101},{6,102},{7,103},{8,104... | collective-permute-start | bytes 884744 | tf_op jit(solution)/shard_map/ppermute | solution.py:269
  68.4 13.9 %collective-permute-start.14 = (bf16[2,576,128]{2,1,0:T(8,128)(2,1)}, bf16[2,576,128]{2,1,0:T(8,128)(2,1)S(1)}, u32[]{:S(2)}, u32[]{:S(2)}) collective-permute-start(bf16[2,576,128]{2,1,0:T(8,128)(2,1)} %get-tuple-element.41), channel_id=1, source_target_pairs={{0,96},{1,97},{2,98},{3,99},{4,100},{5,101},{6,102},{7,103},{8,104... | collective-permute-start | bytes 884744 | tf_op jit(solution)/shard_map/ppermute | solution.py:269
  68.5 14.2 %collective-permute-start.15 = (bf16[2,576,128]{2,1,0:T(8,128)(2,1)S(1)}, bf16[2,576,128]{2,1,0:T(8,128)(2,1)S(1)}, u32[]{:S(2)}, u32[]{:S(2)}) collective-permute-start(bf16[2,576,128]{2,1,0:T(8,128)(2,1)S(1)} %get-tuple-element.42), channel_id=1, source_target_pairs={{0,32},{1,33},{2,34},{3,35},{4,36},{5,37},{6,38},{7,39},{8,40},{9,... | collective-permute-start | bytes 884744 | tf_op jit(solution)/shard_map/ppermute | solution.py:269
  76.5 11.1 %collective-permute-start.13 = (bf16[2,576,128]{2,1,0:T(8,128)(2,1)S(1)}, bf16[2,576,128]{2,1,0:T(8,128)(2,1)S(1)}, u32[]{:S(2)}, u32[]{:S(2)}) collective-permute-start(bf16[2,576,128]{2,1,0:T(8,128)(2,1)S(1)} %get-tuple-element.40), channel_id=1, source_target_pairs={{0,32},{1,33},{2,34},{3,35},{4,36},{5,37},{6,38},{7,39},{8,40},{9,... | collective-permute-start | bytes 884744 | tf_op jit(solution)/shard_map/ppermute | solution.py:269
  76.6 11.0 %collective-permute-start.16 = (bf16[2,576,128]{2,1,0:T(8,128)(2,1)S(1)}, bf16[2,576,128]{2,1,0:T(8,128)(2,1)S(1)}, u32[]{:S(2)}, u32[]{:S(2)}) collective-permute-start(bf16[2,576,128]{2,1,0:T(8,128)(2,1)S(1)} %get-tuple-element.43), channel_id=1, source_target_pairs={{0,96},{1,97},{2,98},{3,99},{4,100},{5,101},{6,102},{7,103},{8,104... | collective-permute-start | bytes 884744 | tf_op jit(solution)/shard_map/ppermute | solution.py:269
  88.0 8.7 %collective-permute-start.17 = (bf16[2,64,576]{2,1,0:T(8,128)(2,1)S(1)}, bf16[2,64,576]{2,1,0:T(8,128)(2,1)S(1)}, u32[]{:S(2)}, u32[]{:S(2)}) collective-permute-start(bf16[2,64,576]{2,1,0:T(8,128)(2,1)S(1)} %get-tuple-element.45), channel_id=1, source_target_pairs={{0,4},{1,5},{2,6},{3,7},{4,8},{5,9},{6,10},{7,11},{8,12},{9,13},{1... | collective-permute-start | bytes 442376 | tf_op jit(solution)/shard_map/ppermute | solution.py:269
  89.5 7.9 %collective-permute-start.18 = (bf16[2,64,576]{2,1,0:T(8,128)(2,1)S(1)}, bf16[2,64,576]{2,1,0:T(8,128)(2,1)S(1)}, u32[]{:S(2)}, u32[]{:S(2)}) collective-permute-start(bf16[2,64,576]{2,1,0:T(8,128)(2,1)S(1)} %get-tuple-element.46), channel_id=1, source_target_pairs={{0,8},{1,9},{2,10},{3,11},{4,12},{5,13},{6,14},{7,15},{8,0},{9,1},... | collective-permute-start | bytes 442376 | tf_op jit(solution)/shard_map/ppermute | solution.py:269
  90.6 8.1 %collective-permute-start.19 = (bf16[2,64,576]{2,1,0:T(8,128)(2,1)S(1)}, bf16[2,64,576]{2,1,0:T(8,128)(2,1)S(1)}, u32[]{:S(2)}, u32[]{:S(2)}) collective-permute-start(bf16[2,64,576]{2,1,0:T(8,128)(2,1)S(1)} %get-tuple-element.47), channel_id=1, source_target_pairs={{0,12},{1,13},{2,14},{3,15},{4,0},{5,1},{6,2},{7,3},{8,4},{9,5},{1... | collective-permute-start | bytes 442376 | tf_op jit(solution)/shard_map/ppermute | solution.py:269
  99.4 17.5 %all-to-all-start.1 = ((bf16[8,16,576]{2,1,0:T(8,128)(2,1)}), bf16[8,16,576]{2,1,0:T(8,128)(2,1)S(1)}, u32[]{:S(2)}, u32[]{:S(2)}) async-start(bf16[8,16,576]{2,1,0:T(8,128)(2,1)} %bitcast.6), calls=%async_computation.1 | async-start | bytes 327680 | tf_op jit(solution)/shard_map/all_to_all | solution.py:472

commit v4 on v3

--- a/solution.py
+++ b/solution.py
@@ -29,7 +29,8 @@
 HEAD = AXES[3:]
 
 
-def prepare_kernel(advantage_ref, qt_hbm, grad_hbm, q_hbm, g_hbm, gt_hbm, *scratch):
+def prepare_kernel(advantage_ref, qt_hbm, grad_hbm, q_hbm, g_hbm, gt_hbm, done, *scratch):
+    done[...] = jnp.zeros_like(done)
     qt, grad, q, g, gt, in_sems, out_sem = scratch
     heads = range(HEADS_HERE)
     load_grad = pltpu.make_async_copy(grad_hbm, grad, in_sems.at[HEADS_HERE])
@@ -65,11 +66,11 @@
     return pl.pallas_call(
         prepare_kernel,
         in_specs=[pl.BlockSpec(memory_space=pltpu.VMEM), hbm, hbm],
-        out_specs=[hbm] * 3,
-        out_shape=[jax.ShapeDtypeStruct(shape, jnp.bfloat16) for shape in shapes],
+        out_specs=[hbm] * 3 + [pl.BlockSpec(memory_space=pltpu.VMEM)],
+        out_shape=[jax.ShapeDtypeStruct(shape, jnp.bfloat16) for shape in (*shapes, (16, 128))],
         scratch_shapes=[pltpu.VMEM(shape, jnp.bfloat16) for shape in scratch]
         + [pltpu.SemaphoreType.DMA((HEADS_HERE + 1,)), pltpu.SemaphoreType.DMA],
-        compiler_params=pltpu.CompilerParams(vmem_limit_bytes=14 * MIB),
+        compiler_params=pltpu.CompilerParams(vmem_limit_bytes=58 * MIB),
     )(advantage[None], qt, grad_out)
 
 
@@ -261,6 +262,7 @@
 RIGHT, LEFT = neighbour(x=1), neighbour(x=-1)
 ALONG_Y = [neighbour(y=d) for d in range(4)]
 UP, DOWN = neighbour(z=1), neighbour(z=-1)
+RIGHT_UP, LEFT_DOWN = neighbour(x=1, z=1), neighbour(x=-1, z=-1)
 SWAP = neighbour(core=1)
 OTHER_Z = other_z()
 
@@ -269,13 +271,14 @@
     return lax.ppermute(a, AXES, pairs)
 
 
+def key_blocks(piece):
+    return [piece.at[:, pl.ds(at, BLK)] for at in range(0, piece.shape[1], BLK)]
+
+
 def pack_kernel(*refs):
     *pieces, out, sem = refs
-    copies, at = [], 0
-    for piece in pieces:
-        n = piece.shape[0]
-        copies.append(pltpu.make_async_copy(piece, out.at[pl.ds(at, n)], sem))
-        at += n
+    views = [view for piece in pieces for view in key_blocks(piece)]
+    copies = [pltpu.make_async_copy(view, out.at[at], sem) for at, view in enumerate(views)]
     for copy in copies:
         copy.start()
     for copy in copies:
@@ -283,7 +286,7 @@
 
 
 def pack(pieces):
-    n = sum(piece.shape[0] for piece in pieces)
+    n = sum(piece.shape[1] // BLK for piece in pieces)
     return pl.pallas_call(
         pack_kernel,
         in_specs=[pl.BlockSpec(memory_space=pl.ANY)] * len(pieces),
@@ -300,7 +303,7 @@
 
 def copies_kernel(*refs):
     left, right, _, *outs, sem = refs
-    parts = left, right, left.at[pl.ds(0, 1)], right.at[pl.ds(1, 1)]
+    parts = left, right, key_blocks(left)[0], key_blocks(right)[1]
     copies = [pltpu.make_async_copy(part, out, sem) for part, out in zip(parts, outs)]
     for copy in copies:
         copy.start()
@@ -314,7 +317,7 @@
         copies_kernel,
         in_specs=[anywhere] * 3,
         out_specs=[anywhere] * 4,
-        out_shape=[jax.ShapeDtypeStruct((n, QW, BLK), jnp.bfloat16) for n in (2, 2, 1, 1)],
+        out_shape=[jax.ShapeDtypeStruct((QW, n * BLK), jnp.bfloat16) for n in (2, 2, 1, 1)],
         scratch_shapes=[pltpu.SemaphoreType.DMA],
         compiler_params=pltpu.CompilerParams(vmem_limit_bytes=4 * MIB),
     )(left, right, after)
@@ -325,7 +328,7 @@
     from_left, from_right, to_right, to_left = copies_after(from_left, from_right, after)
     far = move(to_right, RIGHT), move(to_left, LEFT)
     z_left, z_right = move(from_left, UP), move(from_right, DOWN)
-    z_far = move(far[0], UP), move(far[1], DOWN)
+    z_far = move(to_right, RIGHT_UP), move(to_left, LEFT_DOWN)
     mine = pack([own, from_right, from_left, z_own, *far, z_right, z_left, *z_far])
     return [mine, move(mine, SWAP)]
 
@@ -398,15 +401,16 @@
         for block in range(2):
             total = total_of(parts[z], block) + own[2 * z + block].astype(jnp.float32)
             rows = total.T.astype(jnp.bfloat16)
-            turned[2 * block, z] = rows[: BLK // 2]
-            turned[2 * block + 1, z] = rows[BLK // 2 :]
+            cols = slice(z * QW, (z + 1) * QW)
+            turned[2 * block, :, cols] = rows[: BLK // 2]
+            turned[2 * block + 1, :, cols] = rows[BLK // 2 :]
     for d in range(4):
         outs[d][...] = turned[(y_ref[0] + d) & 3]
 
 
 def add_x(my_y, parts):
     vmem = pl.BlockSpec(memory_space=pltpu.VMEM)
-    shape = (2, BLK // 2, QW)
+    shape = (BLK // 2, 2 * QW)
     return pl.pallas_call(
         add_x_kernel,
         grid_spec=pltpu.PrefetchScalarGridSpec(
@@ -423,7 +427,9 @@
 
 def add_y_kernel(*refs):
     *parts, out = refs
-    out[...] = total_of(parts, ...).astype(jnp.bfloat16)
+    total = total_of(parts, ...).astype(jnp.bfloat16)
+    out[0] = total[:, :QW]
+    out[1] = total[:, QW:]
 
 
 def add_y(parts):
@@ -443,9 +449,8 @@
 
 def on_device(queries, latent, grad_out, advantage, ancestors):
     qt = jnp.transpose(queries, (1, 2, 0))
-    own_keys = jnp.swapaxes(latent.reshape(2, BLK, QW), 1, 2)
-    q, g, gt = prepare(qt, grad_out, advantage)
-    pieces = gather_keys(own_keys, gt)
+    q, g, gt, done = prepare(qt, grad_out, advantage)
+    pieces = gather_keys(latent.T, done)
 
     my_z, my_x, my_core = (lax.axis_index(name) for name in CTX)
     own = lax.axis_index(CTX) * 2 + jnp.arange(2, dtype=jnp.int32)

time: 118 us -> 117 us (level)
  local copies, waits for them, and re-layouts: 6.84 us -> 3.36 us
  starting transfers between devices: 42.6 us -> 45 us
  Pallas kernels: 25.5 us -> 27.8 us
  waiting for transfers between devices: 40 us -> 38 us
    unnamed x20 -> x10, local copies, waits for them, and re-layouts: 4.16 us -> 0.7 us
    all_to_all x1, starting transfers between devices: 7.45 us -> 10.4 us  [on_device(): dq = lax.all_to_all(dq, HEAD, split_axis=0, concat_axis=0, tiled=True)]
    ppermute x20, waiting for transfers between devices: 34.2 us -> 32.2 us  [move(): return lax.ppermute(a, AXES, pairs)]
    pallas_call x1, Pallas kernels: 4.15 us -> 6.08 us  [prepare(): pl.pallas_call(prepare_kernel, in_specs=[pl.BlockSpec(memory_space=pltpu....]
  transfers between devices with their start and end apart: 22 -> 22, of which waited for: 12 -> 15; matrix products, arithmetic and copies ran while one was open for 3% -> 3% of each run, Pallas kernels for 7% -> 8%
where the time goes in v4:
time: 117 us
  starting transfers between devices  45 us (38%)
  waiting for transfers between devices  38 us (32%)
  Pallas kernels  27.8 us (24%)
  local copies, waits for them, and re-layouts  3.36 us (3%)
  other arithmetic  1.65 us (1%)
    ppermute x20, waiting for transfers between devices, move(): return lax.ppermute(a, AXES, pairs)  32.2 us
    ppermute x20, starting transfers between devices, move(): return lax.ppermute(a, AXES, pairs)  25.7 us
    pallas_call x1, Pallas kernels, local_grads(): pl.pallas_call(kernel, grid_spec=pltpu.PrefetchScalarGridSpec(num_scalar_...  16.8 us
    all_to_all x1, starting transfers between devices, on_device(): dq = lax.all_to_all(dq, HEAD, split_axis=0, concat_axis=0, tiled=True)  10.4 us
    all_to_all x1, starting transfers between devices, on_device(): lax.all_to_all(rows, ('z_lo', 'z_hi'), split_axis=0, concat_axis=0, tiled...  8.91 us
    pallas_call x1, Pallas kernels, prepare(): pl.pallas_call(prepare_kernel, in_specs=[pl.BlockSpec(memory_space=pltpu....  6.08 us
    all_to_all x1, waiting for transfers between devices, on_device(): lax.all_to_all(rows, ('z_lo', 'z_hi'), split_axis=0, concat_axis=0, tiled...  5.83 us
    reshape x1, local copies, waits for them, and re-layouts, on_device(): query_grad = jnp.transpose(dq.reshape(64, 16, QW), (1, 0, 2))  2.66 us
  transfers between devices with their start and end apart: 22, of which 15 were waited for; matrix products, arithmetic and copies ran while one was open for 3% of the time, Pallas kernels for 8%

profile of v4, /device:TPU:40, one launch (start us, length us, event | category | flops | bytes accessed | tf_op | source)
XLA Modules:
  0.0 116.6 jit_solution(10443236574119291594)
XLA Ops:
  0.6 0.0 copy-start.2
  0.6 2.8 %collective-permute-start.1 = (bf16[576,256]{1,0:T(8,128)(2,1)}, bf16[576,256]{1,0:T(8,128)(2,1)S(1)}, u32[]{:S(2)}, u32[]{:S(2)}) collective-permute-start(bf16[576,256]{1,0:T(8,128)(2,1)} %bitcast.9), channel_id=1, source_target_pairs={{0,96},{1,97},{2,98},{3,99},{4,100},{5,101},{6,102},{7,103},{8,104... | collective-permute-start | bytes 884744 | tf_op jit(solution)/shard_map/ppermute | solution.py:271
  3.5 0.0 collective-permute-start
  3.5 0.1 collective-permute-start.2
  3.6 6.1 %shard_map.68 = (bf16[4,256,576]{2,1,0:T(8,128)(2,1)}, bf16[4,256,512]{2,1,0:T(8,128)(2,1)}, bf16[4,512,256]{2,1,0:T(8,128)(2,1)}, bf16[16,128]{1,0:T(8,128)(2,1)}) custom-call(f32[1,256]{1,0:T(1,128)} %bitcast.16, bf16[4,576,256]{2,1,0:T(8,128)(2,1)} %bitcast.13, bf16[256,4,512]{2,1,0:T(4,128)(2,1)} %grad_hbm.1), custom_call_target="tpu_custom_call" | custom-call | tf_op jit(solution)/shard_map/pallas_call | solution.py:66
  9.7 0.4 collective-permute-done.1.refs_1_
  10.1 3.3 %collective-permute-done.refs_0_ = bf16[576,256]{1,0:T(8,128)(2,1)S(1)} collective-permute-done((bf16[576,256]{1,0:T(8,128)(2,1)}, bf16[576,256]{1,0:T(8,128)(2,1)S(1)}, u32[]{:S(2)}, u32[]{:S(2)}) %collective-permute-start) | collective-permute-done | bytes 294944 | tf_op jit(solution)/shard_map/ppermute | solution.py:271
  13.4 0.7 copy-done.3
  14.1 0.2 shard_map.69
  14.2 0.5 collective-permute-start.7
  14.8 0.1 collective-permute-start.5
  14.9 1.9 %collective-permute-start.6 = (bf16[576,256]{1,0:T(8,128)(2,1)S(1)}, bf16[576,256]{1,0:T(8,128)(2,1)S(1)}, u32[]{:S(2)}, u32[]{:S(2)}) collective-permute-start(bf16[576,256]{1,0:T(8,128)(2,1)S(1)} %get-tuple-element.31.refs_2_), channel_id=1, source_target_pairs={{0,128},{1,129},{2,130},{3,131},{4,132},{5,133},{6,134},{7,135},{8... | collective-permute-start | bytes 884744 | tf_op jit(solution)/shard_map/ppermute | solution.py:271
  16.8 1.3 %collective-permute-start.3 = (bf16[576,128]{1,0:T(8,128)(2,1)S(1)}, bf16[576,128]{1,0:T(8,128)(2,1)S(1)}, u32[]{:S(2)}, u32[]{:S(2)}) collective-permute-start(bf16[576,128]{1,0:T(8,128)(2,1)S(1)} %get-tuple-element.32), channel_id=1, source_target_pairs={{0,32},{1,33},{2,34},{3,35},{4,36},{5,37},{6,38},{7,39},{8,40},{9,... | collective-permute-start | bytes 442376 | tf_op jit(solution)/shard_map/ppermute | solution.py:271
  18.1 0.0 collective-permute-done.2.refs_3_
  18.1 5.0 %collective-permute-start.8 = (bf16[576,128]{1,0:T(8,128)(2,1)S(1)}, bf16[576,128]{1,0:T(8,128)(2,1)S(1)}, u32[]{:S(2)}, u32[]{:S(2)}) collective-permute-start(bf16[576,128]{1,0:T(8,128)(2,1)S(1)} %get-tuple-element.33), channel_id=1, source_target_pairs={{0,227},{1,224},{2,225},{3,226},{4,231},{5,228},{6,229},{7,230},{8... | collective-permute-start | bytes 442376 | tf_op jit(solution)/shard_map/ppermute | solution.py:271
  23.1 0.1 collective-permute-done.7.refs_8_
  23.1 0.0 collective-permute-start.4
  23.1 1.4 %collective-permute-done.3.refs_4_ = bf16[576,128]{1,0:T(8,128)(2,1)S(1)} collective-permute-done((bf16[576,128]{1,0:T(8,128)(2,1)S(1)}, bf16[576,128]{1,0:T(8,128)(2,1)S(1)}, u32[]{:S(2)}, u32[]{:S(2)}) %collective-permute-start.3) | collective-permute-done | bytes 147488 | tf_op jit(solution)/shard_map/ppermute | solution.py:271
  24.5 1.9 %collective-permute-done.8.refs_9_ = bf16[576,128]{1,0:T(8,128)(2,1)S(1)} collective-permute-done((bf16[576,128]{1,0:T(8,128)(2,1)S(1)}, bf16[576,128]{1,0:T(8,128)(2,1)S(1)}, u32[]{:S(2)}, u32[]{:S(2)}) %collective-permute-start.8) | collective-permute-done | bytes 147488 | tf_op jit(solution)/shard_map/ppermute | solution.py:271
  26.4 2.2 %collective-permute-done.4.refs_5_ = bf16[576,128]{1,0:T(8,128)(2,1)S(1)} collective-permute-done((bf16[576,128]{1,0:T(8,128)(2,1)S(1)}, bf16[576,128]{1,0:T(8,128)(2,1)S(1)}, u32[]{:S(2)}, u32[]{:S(2)}) %collective-permute-start.4) | collective-permute-done | bytes 147488 | tf_op jit(solution)/shard_map/ppermute | solution.py:271
  28.6 0.0 collective-permute-done.5.refs_6_
  28.6 0.0 collective-permute-done.6.refs_7_
  28.6 0.0 copy-done.2
  28.6 1.1 shard_map.70.rest_0_
  29.7 0.0 copy-start
  29.7 0.3 collective-permute-start.9
  30.0 0.0 copy-done.4
  30.0 0.1 fusion.11
  30.2 0.9 pad_add_fusion.1.info
  31.1 3.6 %collective-permute-done.9.rest_1_ = bf16[16,576,128]{2,1,0:T(8,128)(2,1)} collective-permute-done((bf16[16,576,128]{2,1,0:T(8,128)(2,1)S(1)}, bf16[16,576,128]{2,1,0:T(8,128)(2,1)}, u32[]{:S(2)}, u32[]{:S(2)}) %collective-permute-start.9) | collective-permute-done | bytes 2359328 | tf_op jit(solution)/shard_map/ppermute | solution.py:271
  34.7 0.0 copy-done
  34.7 16.8 %shard_map.71 = (bf16[16,4,16,576]{3,2,1,0:T(8,128)(2,1)}, bf16[16,576,128]{2,1,0:T(8,128)(2,1)}, bf16[16,576,128]{2,1,0:T(8,128)(2,1)}) custom-call(s32[2,27]{1,0:T(2,128)} %pad_add_fusion.1.info, bf16[4,256,576]{2,1,0:T(8,128)(2,1)} %get-tuple-element.26.q_hbm, bf16[4,576,256]{2,1,0:T(8,128)(2,1)} %bitcast.14, ...), custom_call_target="tpu_custom_call" | custom-call | tf_op jit(solution)/shard_map/pallas_call | solution.py:197
  51.5 0.0 copy-start.1
  51.5 0.1 collective-permute-start.10
  51.6 10.4 %all-to-all-start = ((bf16[16,4,16,576]{3,2,1,0:T(8,128)(2,1)}), bf16[16,4,16,576]{3,2,1,0:T(8,128)(2,1)}, u32[]{:S(2)}, u32[]{:S(2)}) async-start(bf16[16,4,16,576]{3,2,1,0:T(8,128)(2,1)} %get-tuple-element.34), calls=%async_computation | async-start | bytes 2621440 | tf_op jit(solution)/shard_map/all_to_all | solution.py:480
  62.0 0.0 collective-permute-done.10.got
  62.0 0.0 copy-done.1
  62.0 2.2 %shard_map.72 = (bf16[2,576,128]{2,1,0:T(8,128)(2,1)S(1)}, bf16[2,576,128]{2,1,0:T(8,128)(2,1)S(1)}, bf16[2,576,128]{2,1,0:T(8,128)(2,1)S(1)}, bf16[2,576,128]{2...) custom-call(bf16[16,576,128]{2,1,0:T(8,128)(2,1)S(1)} %copy-done.1, ...), custom_call_target="tpu_custom_call" | custom-call | tf_op jit(solution)/shard_map/pallas_call | solution.py:367
  64.2 0.1 collective-permute-start.11
  64.3 3.2 %collective-permute-start.12 = (bf16[2,576,128]{2,1,0:T(8,128)(2,1)S(1)}, bf16[2,576,128]{2,1,0:T(8,128)(2,1)S(1)}, u32[]{:S(2)}, u32[]{:S(2)}) collective-permute-start(bf16[2,576,128]{2,1,0:T(8,128)(2,1)S(1)} %get-tuple-element.41), channel_id=1, source_target_pairs={{0,96},{1,97},{2,98},{3,99},{4,100},{5,101},{6,102},{7,103},{8,104... | collective-permute-start | bytes 884744 | tf_op jit(solution)/shard_map/ppermute | solution.py:271
  67.5 0.4 collective-permute-start.14
  67.9 1.6 %collective-permute-start.15 = (bf16[2,576,128]{2,1,0:T(8,128)(2,1)S(1)}, bf16[2,576,128]{2,1,0:T(8,128)(2,1)S(1)}, u32[]{:S(2)}, u32[]{:S(2)}) collective-permute-start(bf16[2,576,128]{2,1,0:T(8,128)(2,1)S(1)} %get-tuple-element.44), channel_id=1, source_target_pairs={{0,32},{1,33},{2,34},{3,35},{4,36},{5,37},{6,38},{7,39},{8,40},{9,... | collective-permute-start | bytes 884744 | tf_op jit(solution)/shard_map/ppermute | solution.py:271
  69.5 5.8 %collective-permute-done.11.from_left = bf16[2,576,128]{2,1,0:T(8,128)(2,1)S(1)} collective-permute-done((bf16[2,576,128]{2,1,0:T(8,128)(2,1)S(1)}, bf16[2,576,128]{2,1,0:T(8,128)(2,1)S(1)}, u32[]{:S(2)}, u32[]{:S(2)}) %collective-permute-start.11) | collective-permute-done | bytes 294944 | tf_op jit(solution)/shard_map/ppermute | solution.py:271
  75.4 0.0 collective-permute-done.12.from_right
  75.4 0.1 shard_map.73
  75.5 0.1 collective-permute-start.13
  75.6 3.3 %collective-permute-start.16 = (bf16[2,576,128]{2,1,0:T(8,128)(2,1)S(1)}, bf16[2,576,128]{2,1,0:T(8,128)(2,1)S(1)}, u32[]{:S(2)}, u32[]{:S(2)}) collective-permute-start(bf16[2,576,128]{2,1,0:T(8,128)(2,1)S(1)} %get-tuple-element.45), channel_id=1, source_target_pairs={{0,96},{1,97},{2,98},{3,99},{4,100},{5,101},{6,102},{7,103},{8,104... | collective-permute-start | bytes 884744 | tf_op jit(solution)/shard_map/ppermute | solution.py:271
  79.0 2.3 %collective-permute-done.14.refs_1_ = bf16[2,576,128]{2,1,0:T(8,128)(2,1)S(1)} collective-permute-done((bf16[2,576,128]{2,1,0:T(8,128)(2,1)S(1)}, bf16[2,576,128]{2,1,0:T(8,128)(2,1)S(1)}, u32[]{:S(2)}, u32[]{:S(2)}) %collective-permute-start.14) | collective-permute-done | bytes 294944 | tf_op jit(solution)/shard_map/ppermute | solution.py:271
  81.3 0.4 collective-permute-done.15.refs_2_
  81.7 5.3 %collective-permute-done.13.refs_0_ = bf16[2,576,128]{2,1,0:T(8,128)(2,1)S(1)} collective-permute-done((bf16[2,576,128]{2,1,0:T(8,128)(2,1)S(1)}, bf16[2,576,128]{2,1,0:T(8,128)(2,1)S(1)}, u32[]{:S(2)}, u32[]{:S(2)}) %collective-permute-start.13) | collective-permute-done | bytes 294944 | tf_op jit(solution)/shard_map/ppermute | solution.py:271
  87.0 0.0 collective-permute-done.16.refs_3_
  87.0 0.5 shard_map.74
  87.5 1.5 %collective-permute-start.17 = (bf16[64,1152]{1,0:T(8,128)(2,1)S(1)}, bf16[64,1152]{1,0:T(8,128)(2,1)S(1)}, u32[]{:S(2)}, u32[]{:S(2)}) collective-permute-start(bf16[64,1152]{1,0:T(8,128)(2,1)S(1)} %get-tuple-element.47), channel_id=1, source_target_pairs={{0,4},{1,5},{2,6},{3,7},{4,8},{5,9},{6,10},{7,11},{8,12},{9,13},{1... | collective-permute-start | bytes 442376 | tf_op jit(solution)/shard_map/ppermute | solution.py:271
  89.0 1.0 collective-permute-start.18
  90.1 2.2 %collective-permute-start.19 = (bf16[64,1152]{1,0:T(8,128)(2,1)S(1)}, bf16[64,1152]{1,0:T(8,128)(2,1)S(1)}, u32[]{:S(2)}, u32[]{:S(2)}) collective-permute-start(bf16[64,1152]{1,0:T(8,128)(2,1)S(1)} %get-tuple-element.49), channel_id=1, source_target_pairs={{0,12},{1,13},{2,14},{3,15},{4,0},{5,1},{6,2},{7,3},{8,4},{9,5},{1... | collective-permute-start | bytes 442376 | tf_op jit(solution)/shard_map/ppermute | solution.py:271
  92.3 1.8 %collective-permute-done.17.refs_1_ = bf16[64,1152]{1,0:T(8,128)(2,1)S(1)} collective-permute-done((bf16[64,1152]{1,0:T(8,128)(2,1)S(1)}, bf16[64,1152]{1,0:T(8,128)(2,1)S(1)}, u32[]{:S(2)}, u32[]{:S(2)}) %collective-permute-start.17) | collective-permute-done | bytes 147488 | tf_op jit(solution)/shard_map/ppermute | solution.py:271
  94.0 2.8 %collective-permute-done.18.refs_2_ = bf16[64,1152]{1,0:T(8,128)(2,1)S(1)} collective-permute-done((bf16[64,1152]{1,0:T(8,128)(2,1)S(1)}, bf16[64,1152]{1,0:T(8,128)(2,1)S(1)}, u32[]{:S(2)}, u32[]{:S(2)}) %collective-permute-start.18) | collective-permute-done | bytes 147488 | tf_op jit(solution)/shard_map/ppermute | solution.py:271
  96.8 1.0 collective-permute-done.19.refs_3_
  97.8 0.8 shard_map.75
  98.6 0.0 all-to-all-done
  98.6 8.9 %all-to-all-start.1 = ((bf16[8,16,576]{2,1,0:T(8,128)(2,1)}), bf16[8,16,576]{2,1,0:T(8,128)(2,1)S(1)}, u32[]{:S(2)}, u32[]{:S(2)}) async-start(bf16[8,16,576]{2,1,0:T(8,128)(2,1)} %bitcast.6), calls=%async_computation.1 | async-start | bytes 327680 | tf_op jit(solution)/shard_map/all_to_all | solution.py:477
  107.5 2.7 %copy.9 = bf16[64,16,576]{2,0,1:T(8,128)(2,1)} copy(bf16[64,16,576]{2,1,0:T(8,128)(2,1)} %bitcast.3) | data formatting | bytes 2359296 | tf_op jit(solution)/shard_map/reshape | solution.py:481
  110.1 5.8 %all-to-all-done.1 = bf16[8,16,576]{2,1,0:T(8,128)(2,1)S(1)} async-done(((bf16[8,16,576]{2,1,0:T(8,128)(2,1)}), bf16[8,16,576]{2,1,0:T(8,128)(2,1)S(1)}, u32[]{:S(2)}, u32[]{:S(2)}) %all-to-all-start.1) | async-done | bytes 147488 | tf_op jit(solution)/shard_map/all_to_all | solution.py:477
  116.0 0.6 convert_reduce_fusion
  (5 shorter events, 0.0 us)
Async XLA Ops:
  0.6 28.0 %copy-start.2 = (bf16[256,576]{0,1:T(8,128)(2,1)S(1)}, bf16[256,576]{0,1:T(8,128)(2,1)}, u32[]{:S(2)}) copy-start(bf16[256,576]{0,1:T(8,128)(2,1)} %param.6) | copy-start | bytes 884740
  0.6 9.4 %collective-permute-start.1 = (bf16[576,256]{1,0:T(8,128)(2,1)}, bf16[576,256]{1,0:T(8,128)(2,1)S(1)}, u32[]{:S(2)}, u32[]{:S(2)}) collective-permute-start(bf16[576,256]{1,0:T(8,128)(2,1)} %bitcast.9), channel_id=1, source_target_pairs={{0,96},{1,97},{2,98},{3,99},{4,100},{5,101},{6,102},{7,103},{8,104... | collective-permute-start | bytes 884744 | tf_op jit(solution)/shard_map/ppermute | solution.py:271
  3.5 9.9 %collective-permute-start = (bf16[576,256]{1,0:T(8,128)(2,1)}, bf16[576,256]{1,0:T(8,128)(2,1)S(1)}, u32[]{:S(2)}, u32[]{:S(2)}) collective-permute-start(bf16[576,256]{1,0:T(8,128)(2,1)} %bitcast.10), channel_id=1, source_target_pairs={{0,32},{1,33},{2,34},{3,35},{4,36},{5,37},{6,38},{7,39},{8,40},{9,... | collective-permute-start | bytes 884744 | tf_op jit(solution)/shard_map/ppermute | solution.py:271
  3.5 14.6 %collective-permute-start.2 = (bf16[576,256]{1,0:T(8,128)(2,1)}, bf16[576,256]{1,0:T(8,128)(2,1)S(1)}, u32[]{:S(2)}, u32[]{:S(2)}) collective-permute-start(bf16[576,256]{1,0:T(8,128)(2,1)} %bitcast.11), channel_id=1, source_target_pairs={{0,128},{1,129},{2,130},{3,131},{4,132},{5,133},{6,134},{7,135},{8... | collective-permute-start | bytes 884744 | tf_op jit(solution)/shard_map/ppermute | solution.py:271
  13.4 0.7 copy-start.3
  14.2 8.9 %collective-permute-start.7 = (bf16[576,128]{1,0:T(8,128)(2,1)S(1)}, bf16[576,128]{1,0:T(8,128)(2,1)S(1)}, u32[]{:S(2)}, u32[]{:S(2)}) collective-permute-start(bf16[576,128]{1,0:T(8,128)(2,1)S(1)} %get-tuple-element.32), channel_id=1, source_target_pairs={{0,160},{1,161},{2,162},{3,163},{4,164},{5,165},{6,166},{7,167},{8... | collective-permute-start | bytes 442376 | tf_op jit(solution)/shard_map/ppermute | solution.py:271
  14.8 13.8 %collective-permute-start.5 = (bf16[576,256]{1,0:T(8,128)(2,1)S(1)}, bf16[576,256]{1,0:T(8,128)(2,1)S(1)}, u32[]{:S(2)}, u32[]{:S(2)}) collective-permute-start(bf16[576,256]{1,0:T(8,128)(2,1)S(1)} %get-tuple-element.30.refs_1_), channel_id=1, source_target_pairs={{0,131},{1,128},{2,129},{3,130},{4,135},{5,132},{6,133},{7,134},{8... | collective-permute-start | bytes 884744 | tf_op jit(solution)/shard_map/ppermute | solution.py:271
  14.9 13.7 %collective-permute-start.6 = (bf16[576,256]{1,0:T(8,128)(2,1)S(1)}, bf16[576,256]{1,0:T(8,128)(2,1)S(1)}, u32[]{:S(2)}, u32[]{:S(2)}) collective-permute-start(bf16[576,256]{1,0:T(8,128)(2,1)S(1)} %get-tuple-element.31.refs_2_), channel_id=1, source_target_pairs={{0,128},{1,129},{2,130},{3,131},{4,132},{5,133},{6,134},{7,135},{8... | collective-permute-start | bytes 884744 | tf_op jit(solution)/shard_map/ppermute | solution.py:271
  16.8 7.7 %collective-permute-start.3 = (bf16[576,128]{1,0:T(8,128)(2,1)S(1)}, bf16[576,128]{1,0:T(8,128)(2,1)S(1)}, u32[]{:S(2)}, u32[]{:S(2)}) collective-permute-start(bf16[576,128]{1,0:T(8,128)(2,1)S(1)} %get-tuple-element.32), channel_id=1, source_target_pairs={{0,32},{1,33},{2,34},{3,35},{4,36},{5,37},{6,38},{7,39},{8,40},{9,... | collective-permute-start | bytes 442376 | tf_op jit(solution)/shard_map/ppermute | solution.py:271
  18.1 11.9 %copy-start.4 = (s32[2,8]{1,0:T(2,128)S(1)}, s32[2,8]{1,0:T(2,128)}, u32[]{:S(2)}) copy-start(s32[2,8]{1,0:T(2,128)} %param.9) | copy-start | bytes 196
  18.1 8.3 %collective-permute-start.8 = (bf16[576,128]{1,0:T(8,128)(2,1)S(1)}, bf16[576,128]{1,0:T(8,128)(2,1)S(1)}, u32[]{:S(2)}, u32[]{:S(2)}) collective-permute-start(bf16[576,128]{1,0:T(8,128)(2,1)S(1)} %get-tuple-element.33), channel_id=1, source_target_pairs={{0,227},{1,224},{2,225},{3,226},{4,231},{5,228},{6,229},{7,230},{8... | collective-permute-start | bytes 442376 | tf_op jit(solution)/shard_map/ppermute | solution.py:271
  23.1 5.5 %collective-permute-start.4 = (bf16[576,128]{1,0:T(8,128)(2,1)S(1)}, bf16[576,128]{1,0:T(8,128)(2,1)S(1)}, u32[]{:S(2)}, u32[]{:S(2)}) collective-permute-start(bf16[576,128]{1,0:T(8,128)(2,1)S(1)} %get-tuple-element.33), channel_id=1, source_target_pairs={{0,96},{1,97},{2,98},{3,99},{4,100},{5,101},{6,102},{7,103},{8,104... | collective-permute-start | bytes 442376 | tf_op jit(solution)/shard_map/ppermute | solution.py:271
  29.7 4.9 %copy-start = (bf16[16,576,128]{2,1,0:T(8,128)(2,1)}, bf16[16,576,128]{2,1,0:T(8,128)(2,1)S(1)}, u32[]{:S(2)}) copy-start(bf16[16,576,128]{2,1,0:T(8,128)(2,1)S(1)} %shard_map.70.rest_0_) | copy-start | bytes 7077892
  29.7 4.9 %collective-permute-start.9 = (bf16[16,576,128]{2,1,0:T(8,128)(2,1)S(1)}, bf16[16,576,128]{2,1,0:T(8,128)(2,1)}, u32[]{:S(2)}, u32[]{:S(2)}) collective-permute-start(bf16[16,576,128]{2,1,0:T(8,128)(2,1)S(1)} %shard_map.70.rest_0_), channel_id=1, source_target_pairs={{0,16},{1,17},{2,18},{3,19},{4,20},{5,21},{6,22},{7,23},{8,24},{9,... | collective-permute-start | bytes 7077896 | tf_op jit(solution)/shard_map/ppermute | solution.py:271
  51.5 10.5 %copy-start.1 = (bf16[16,576,128]{2,1,0:T(8,128)(2,1)S(1)}, bf16[16,576,128]{2,1,0:T(8,128)(2,1)}, u32[]{:S(2)}) copy-start(bf16[16,576,128]{2,1,0:T(8,128)(2,1)} %get-tuple-element.35.keep) | copy-start | bytes 7077892
  51.5 10.5 %collective-permute-start.10 = (bf16[16,576,128]{2,1,0:T(8,128)(2,1)}, bf16[16,576,128]{2,1,0:T(8,128)(2,1)}, u32[]{:S(2)}, u32[]{:S(2)}) collective-permute-start(bf16[16,576,128]{2,1,0:T(8,128)(2,1)} %get-tuple-element.36), channel_id=1, source_target_pairs={{0,16},{1,17},{2,18},{3,19},{4,20},{5,21},{6,22},{7,23},{8,24},{9,... | collective-permute-start | bytes 7077896 | tf_op jit(solution)/shard_map/ppermute | solution.py:271
  51.6 47.0 %all-to-all-start = ((bf16[16,4,16,576]{3,2,1,0:T(8,128)(2,1)}), bf16[16,4,16,576]{3,2,1,0:T(8,128)(2,1)}, u32[]{:S(2)}, u32[]{:S(2)}) async-start(bf16[16,4,16,576]{3,2,1,0:T(8,128)(2,1)} %get-tuple-element.34), calls=%async_computation | async-start | bytes 2621440 | tf_op jit(solution)/shard_map/all_to_all | solution.py:480
  64.2 11.2 %collective-permute-start.11 = (bf16[2,576,128]{2,1,0:T(8,128)(2,1)S(1)}, bf16[2,576,128]{2,1,0:T(8,128)(2,1)S(1)}, u32[]{:S(2)}, u32[]{:S(2)}) collective-permute-start(bf16[2,576,128]{2,1,0:T(8,128)(2,1)S(1)} %get-tuple-element.39), channel_id=1, source_target_pairs={{0,32},{1,33},{2,34},{3,35},{4,36},{5,37},{6,38},{7,39},{8,40},{9,... | collective-permute-start | bytes 884744 | tf_op jit(solution)/shard_map/ppermute | solution.py:271
  64.3 11.1 %collective-permute-start.12 = (bf16[2,576,128]{2,1,0:T(8,128)(2,1)S(1)}, bf16[2,576,128]{2,1,0:T(8,128)(2,1)S(1)}, u32[]{:S(2)}, u32[]{:S(2)}) collective-permute-start(bf16[2,576,128]{2,1,0:T(8,128)(2,1)S(1)} %get-tuple-element.41), channel_id=1, source_target_pairs={{0,96},{1,97},{2,98},{3,99},{4,100},{5,101},{6,102},{7,103},{8,104... | collective-permute-start | bytes 884744 | tf_op jit(solution)/shard_map/ppermute | solution.py:271
  67.5 13.8 %collective-permute-start.14 = (bf16[2,576,128]{2,1,0:T(8,128)(2,1)S(1)}, bf16[2,576,128]{2,1,0:T(8,128)(2,1)S(1)}, u32[]{:S(2)}, u32[]{:S(2)}) collective-permute-start(bf16[2,576,128]{2,1,0:T(8,128)(2,1)S(1)} %get-tuple-element.43), channel_id=1, source_target_pairs={{0,96},{1,97},{2,98},{3,99},{4,100},{5,101},{6,102},{7,103},{8,104... | collective-permute-start | bytes 884744 | tf_op jit(solution)/shard_map/ppermute | solution.py:271
  67.9 13.7 %collective-permute-start.15 = (bf16[2,576,128]{2,1,0:T(8,128)(2,1)S(1)}, bf16[2,576,128]{2,1,0:T(8,128)(2,1)S(1)}, u32[]{:S(2)}, u32[]{:S(2)}) collective-permute-start(bf16[2,576,128]{2,1,0:T(8,128)(2,1)S(1)} %get-tuple-element.44), channel_id=1, source_target_pairs={{0,32},{1,33},{2,34},{3,35},{4,36},{5,37},{6,38},{7,39},{8,40},{9,... | collective-permute-start | bytes 884744 | tf_op jit(solution)/shard_map/ppermute | solution.py:271
  75.5 11.4 %collective-permute-start.13 = (bf16[2,576,128]{2,1,0:T(8,128)(2,1)S(1)}, bf16[2,576,128]{2,1,0:T(8,128)(2,1)S(1)}, u32[]{:S(2)}, u32[]{:S(2)}) collective-permute-start(bf16[2,576,128]{2,1,0:T(8,128)(2,1)S(1)} %get-tuple-element.42), channel_id=1, source_target_pairs={{0,32},{1,33},{2,34},{3,35},{4,36},{5,37},{6,38},{7,39},{8,40},{9,... | collective-permute-start | bytes 884744 | tf_op jit(solution)/shard_map/ppermute | solution.py:271
  75.6 11.4 %collective-permute-start.16 = (bf16[2,576,128]{2,1,0:T(8,128)(2,1)S(1)}, bf16[2,576,128]{2,1,0:T(8,128)(2,1)S(1)}, u32[]{:S(2)}, u32[]{:S(2)}) collective-permute-start(bf16[2,576,128]{2,1,0:T(8,128)(2,1)S(1)} %get-tuple-element.45), channel_id=1, source_target_pairs={{0,96},{1,97},{2,98},{3,99},{4,100},{5,101},{6,102},{7,103},{8,104... | collective-permute-start | bytes 884744 | tf_op jit(solution)/shard_map/ppermute | solution.py:271
  87.5 6.5 %collective-permute-start.17 = (bf16[64,1152]{1,0:T(8,128)(2,1)S(1)}, bf16[64,1152]{1,0:T(8,128)(2,1)S(1)}, u32[]{:S(2)}, u32[]{:S(2)}) collective-permute-start(bf16[64,1152]{1,0:T(8,128)(2,1)S(1)} %get-tuple-element.47), channel_id=1, source_target_pairs={{0,4},{1,5},{2,6},{3,7},{4,8},{5,9},{6,10},{7,11},{8,12},{9,13},{1... | collective-permute-start | bytes 442376 | tf_op jit(solution)/shard_map/ppermute | solution.py:271
  89.0 7.8 %collective-permute-start.18 = (bf16[64,1152]{1,0:T(8,128)(2,1)S(1)}, bf16[64,1152]{1,0:T(8,128)(2,1)S(1)}, u32[]{:S(2)}, u32[]{:S(2)}) collective-permute-start(bf16[64,1152]{1,0:T(8,128)(2,1)S(1)} %get-tuple-element.48), channel_id=1, source_target_pairs={{0,8},{1,9},{2,10},{3,11},{4,12},{5,13},{6,14},{7,15},{8,0},{9,1},... | collective-permute-start | bytes 442376 | tf_op jit(solution)/shard_map/ppermute | solution.py:271
  90.1 7.7 %collective-permute-start.19 = (bf16[64,1152]{1,0:T(8,128)(2,1)S(1)}, bf16[64,1152]{1,0:T(8,128)(2,1)S(1)}, u32[]{:S(2)}, u32[]{:S(2)}) collective-permute-start(bf16[64,1152]{1,0:T(8,128)(2,1)S(1)} %get-tuple-element.49), channel_id=1, source_target_pairs={{0,12},{1,13},{2,14},{3,15},{4,0},{5,1},{6,2},{7,3},{8,4},{9,5},{1... | collective-permute-start | bytes 442376 | tf_op jit(solution)/shard_map/ppermute | solution.py:271
  98.6 17.4 %all-to-all-start.1 = ((bf16[8,16,576]{2,1,0:T(8,128)(2,1)}), bf16[8,16,576]{2,1,0:T(8,128)(2,1)S(1)}, u32[]{:S(2)}, u32[]{:S(2)}) async-start(bf16[8,16,576]{2,1,0:T(8,128)(2,1)} %bitcast.6), calls=%async_computation.1 | async-start | bytes 327680 | tf_op jit(solution)/shard_map/all_to_all | solution.py:477

commit v5 on v4

--- a/solution.py
+++ b/solution.py
@@ -125,8 +125,9 @@
     rows[0].wait()
     rows[1].wait()
 
-    row_pos = lax.broadcasted_iota(jnp.int32, (ROWS // 2, BLK), 0) % BLK
-    key_pos = lax.broadcasted_iota(jnp.int32, (ROWS // 2, BLK), 1)
+    key_pos = lax.broadcasted_iota(jnp.int32, (32, BLK), 1)
+    row_pos = lax.broadcasted_iota(jnp.int32, (32, BLK), 0)
+    shown = [info[b, NSLOT + s] > 0 for s in range(NSLOT)]
     all_dscores, all_low = [], []
     for half in range(2):
         heads = slice(half * HEADS_HERE // 2, (half + 1) * HEADS_HERE // 2)
@@ -134,21 +135,26 @@
         g = g_ref[b, heads].reshape(ROWS // 2, LAT)
         scores = jnp.dot(q, k, preferred_element_type=jnp.float32)
         dprobs = jnp.dot(g, k[:LAT], preferred_element_type=jnp.float32)
-        parts = []
-        for s in range(NSLOT):
-            part = scores[:, s * BLK : (s + 1) * BLK] * (SOFTMAX_SCALE * LOG2E)
-            if s == 0:
-                part = jnp.where(key_pos <= row_pos, part, MASKED)
-            else:
-                part = jnp.where(info[b, NSLOT + s] > 0, part, MASKED)
-            parts.append(part)
-        masked = jnp.concatenate(parts, axis=1)
-        top = jnp.max(masked, axis=1, keepdims=True)
-        expo = jnp.exp2(masked - top)
-        probs = expo * (1.0 / jnp.sum(expo, axis=1, keepdims=True))
-        delta = jnp.sum(probs * dprobs, axis=1, keepdims=True)
-        all_dscores.append((probs * (dprobs - delta) * SOFTMAX_SCALE).astype(jnp.bfloat16))
-        all_low.append(probs.astype(jnp.bfloat16))
+        for at in range(0, ROWS // 2, 32):
+            parts = []
+            for s in range(NSLOT):
+                part = scores[at : at + 32, s * BLK : (s + 1) * BLK] * (SOFTMAX_SCALE * LOG2E)
+                if s == 0:
+                    part = jnp.where(key_pos <= row_pos + at % BLK, part, MASKED)
+                else:
+                    part = jnp.where(shown[s], part, MASKED)
+                parts.append(part)
+            top = jnp.max(functools.reduce(jnp.maximum, parts), axis=1, keepdims=True)
+            expo = [jnp.exp2(part - top) for part in parts]
+            inverse = 1.0 / jnp.sum(sum(expo), axis=1, keepdims=True)
+            grads = [dprobs[at : at + 32, s * BLK : (s + 1) * BLK] for s in range(NSLOT)]
+            delta = jnp.sum(sum(e * d for e, d in zip(expo, grads)), axis=1, keepdims=True)
+            delta = delta * inverse
+            probs = [e * inverse for e in expo]
+            low = [p.astype(jnp.bfloat16) for p in probs]
+            ds = [(p * (d - delta) * SOFTMAX_SCALE).astype(jnp.bfloat16) for p, d in zip(probs, grads)]
+            all_low.append(jnp.concatenate(low, axis=1))
+            all_dscores.append(jnp.concatenate(ds, axis=1))
     dscores = jnp.concatenate(all_dscores, axis=0)
     low = jnp.concatenate(all_low, axis=0)
 
@@ -444,7 +450,8 @@
 
 
 def spread(parts, moves):
-    return [parts[0]] + [move(parts[d], moves[d]) for d in (1, 2, 3)]
+    far = move(parts[2], moves[2])
+    return [parts[0], move(parts[1], moves[1]), far, move(parts[3], moves[3])]
 
 
 def on_device(queries, latent, grad_out, advantage, ancestors):

time: 117 us -> 116 us (level)
  transfers between devices with their start and end apart: 22 -> 22, of which waited for: 15 -> 15; matrix products, arithmetic and copies ran while one was open for 3% -> 3% of each run, Pallas kernels for 8% -> 9%
where the time goes in v5:
time: 116 us
  starting transfers between devices  46 us (40%)
  waiting for transfers between devices  37 us (32%)
  Pallas kernels  26.8 us (23%)
  local copies, waits for them, and re-layouts  3.36 us (3%)
  other arithmetic  1.65 us (1%)
    ppermute x20, waiting for transfers between devices, move(): return lax.ppermute(a, AXES, pairs)  31.4 us
    ppermute x20, starting transfers between devices, move(): return lax.ppermute(a, AXES, pairs)  26.1 us
    pallas_call x1, Pallas kernels, local_grads(): pl.pallas_call(kernel, grid_spec=pltpu.PrefetchScalarGridSpec(num_scalar_...  15.8 us
    all_to_all x1, starting transfers between devices, on_device(): dq = lax.all_to_all(dq, HEAD, split_axis=0, concat_axis=0, tiled=True)  10.4 us
    all_to_all x1, starting transfers between devices, on_device(): lax.all_to_all(rows, ('z_lo', 'z_hi'), split_axis=0, concat_axis=0, tiled...  9.6 us
    pallas_call x1, Pallas kernels, prepare(): pl.pallas_call(prepare_kernel, in_specs=[pl.BlockSpec(memory_space=pltpu....  6.08 us
    all_to_all x1, waiting for transfers between devices, on_device(): lax.all_to_all(rows, ('z_lo', 'z_hi'), split_axis=0, concat_axis=0, tiled...  5.58 us
    reshape x1, local copies, waits for them, and re-layouts, on_device(): query_grad = jnp.transpose(dq.reshape(64, 16, QW), (1, 0, 2))  2.66 us
  transfers between devices with their start and end apart: 22, of which 15 were waited for; matrix products, arithmetic and copies ran while one was open for 3% of the time, Pallas kernels for 9%

profile of v5, /device:TPU:40, one launch (start us, length us, event | category | flops | bytes accessed | tf_op | source)
XLA Modules:
  0.0 115.6 jit_solution(2930490947230817207)
XLA Ops:
  0.6 0.0 copy-start.2
  0.6 2.8 %collective-permute-start.1 = (bf16[576,256]{1,0:T(8,128)(2,1)}, bf16[576,256]{1,0:T(8,128)(2,1)S(1)}, u32[]{:S(2)}, u32[]{:S(2)}) collective-permute-start(bf16[576,256]{1,0:T(8,128)(2,1)} %bitcast.9), channel_id=1, source_target_pairs={{0,96},{1,97},{2,98},{3,99},{4,100},{5,101},{6,102},{7,103},{8,104... | collective-permute-start | bytes 884744 | tf_op jit(solution)/shard_map/ppermute | solution.py:277
  3.5 0.0 collective-permute-start
  3.5 0.1 collective-permute-start.2
  3.6 6.1 %shard_map.68 = (bf16[4,256,576]{2,1,0:T(8,128)(2,1)}, bf16[4,256,512]{2,1,0:T(8,128)(2,1)}, bf16[4,512,256]{2,1,0:T(8,128)(2,1)}, bf16[16,128]{1,0:T(8,128)(2,1)}) custom-call(f32[1,256]{1,0:T(1,128)} %bitcast.16, bf16[4,576,256]{2,1,0:T(8,128)(2,1)} %bitcast.13, bf16[256,4,512]{2,1,0:T(4,128)(2,1)} %grad_hbm.1), custom_call_target="tpu_custom_call" | custom-call | tf_op jit(solution)/shard_map/pallas_call | solution.py:66
  9.7 0.4 collective-permute-done.1.refs_1_
  10.1 3.3 %collective-permute-done.refs_0_ = bf16[576,256]{1,0:T(8,128)(2,1)S(1)} collective-permute-done((bf16[576,256]{1,0:T(8,128)(2,1)}, bf16[576,256]{1,0:T(8,128)(2,1)S(1)}, u32[]{:S(2)}, u32[]{:S(2)}) %collective-permute-start) | collective-permute-done | bytes 294944 | tf_op jit(solution)/shard_map/ppermute | solution.py:277
  13.4 0.7 copy-done.3
  14.1 0.2 shard_map.69
  14.2 0.5 collective-permute-start.7
  14.8 0.1 collective-permute-start.5
  14.9 1.9 %collective-permute-start.6 = (bf16[576,256]{1,0:T(8,128)(2,1)S(1)}, bf16[576,256]{1,0:T(8,128)(2,1)S(1)}, u32[]{:S(2)}, u32[]{:S(2)}) collective-permute-start(bf16[576,256]{1,0:T(8,128)(2,1)S(1)} %get-tuple-element.31.refs_2_), channel_id=1, source_target_pairs={{0,128},{1,129},{2,130},{3,131},{4,132},{5,133},{6,134},{7,135},{8... | collective-permute-start | bytes 884744 | tf_op jit(solution)/shard_map/ppermute | solution.py:277
  16.8 1.3 %collective-permute-start.3 = (bf16[576,128]{1,0:T(8,128)(2,1)S(1)}, bf16[576,128]{1,0:T(8,128)(2,1)S(1)}, u32[]{:S(2)}, u32[]{:S(2)}) collective-permute-start(bf16[576,128]{1,0:T(8,128)(2,1)S(1)} %get-tuple-element.32), channel_id=1, source_target_pairs={{0,32},{1,33},{2,34},{3,35},{4,36},{5,37},{6,38},{7,39},{8,40},{9,... | collective-permute-start | bytes 442376 | tf_op jit(solution)/shard_map/ppermute | solution.py:277
  18.1 0.0 collective-permute-done.2.refs_3_
  18.1 5.0 %collective-permute-start.8 = (bf16[576,128]{1,0:T(8,128)(2,1)S(1)}, bf16[576,128]{1,0:T(8,128)(2,1)S(1)}, u32[]{:S(2)}, u32[]{:S(2)}) collective-permute-start(bf16[576,128]{1,0:T(8,128)(2,1)S(1)} %get-tuple-element.33), channel_id=1, source_target_pairs={{0,227},{1,224},{2,225},{3,226},{4,231},{5,228},{6,229},{7,230},{8... | collective-permute-start | bytes 442376 | tf_op jit(solution)/shard_map/ppermute | solution.py:277
  23.1 0.1 collective-permute-done.7.refs_8_
  23.1 0.0 collective-permute-start.4
  23.1 1.4 %collective-permute-done.3.refs_4_ = bf16[576,128]{1,0:T(8,128)(2,1)S(1)} collective-permute-done((bf16[576,128]{1,0:T(8,128)(2,1)S(1)}, bf16[576,128]{1,0:T(8,128)(2,1)S(1)}, u32[]{:S(2)}, u32[]{:S(2)}) %collective-permute-start.3) | collective-permute-done | bytes 147488 | tf_op jit(solution)/shard_map/ppermute | solution.py:277
  24.5 1.9 %collective-permute-done.8.refs_9_ = bf16[576,128]{1,0:T(8,128)(2,1)S(1)} collective-permute-done((bf16[576,128]{1,0:T(8,128)(2,1)S(1)}, bf16[576,128]{1,0:T(8,128)(2,1)S(1)}, u32[]{:S(2)}, u32[]{:S(2)}) %collective-permute-start.8) | collective-permute-done | bytes 147488 | tf_op jit(solution)/shard_map/ppermute | solution.py:277
  26.4 2.2 %collective-permute-done.4.refs_5_ = bf16[576,128]{1,0:T(8,128)(2,1)S(1)} collective-permute-done((bf16[576,128]{1,0:T(8,128)(2,1)S(1)}, bf16[576,128]{1,0:T(8,128)(2,1)S(1)}, u32[]{:S(2)}, u32[]{:S(2)}) %collective-permute-start.4) | collective-permute-done | bytes 147488 | tf_op jit(solution)/shard_map/ppermute | solution.py:277
  28.6 0.0 collective-permute-done.5.refs_6_
  28.6 0.0 collective-permute-done.6.refs_7_
  28.6 0.0 copy-done.2
  28.6 1.1 shard_map.70.rest_0_
  29.7 0.0 copy-start
  29.7 0.3 collective-permute-start.9
  30.0 0.0 copy-done.4
  30.0 0.1 fusion.11
  30.2 0.9 pad_add_fusion.1.info
  31.1 3.6 %collective-permute-done.9.rest_1_ = bf16[16,576,128]{2,1,0:T(8,128)(2,1)} collective-permute-done((bf16[16,576,128]{2,1,0:T(8,128)(2,1)S(1)}, bf16[16,576,128]{2,1,0:T(8,128)(2,1)}, u32[]{:S(2)}, u32[]{:S(2)}) %collective-permute-start.9) | collective-permute-done | bytes 2359328 | tf_op jit(solution)/shard_map/ppermute | solution.py:277
  34.7 0.0 copy-done
  34.7 15.8 %shard_map.71 = (bf16[16,4,16,576]{3,2,1,0:T(8,128)(2,1)}, bf16[16,576,128]{2,1,0:T(8,128)(2,1)}, bf16[16,576,128]{2,1,0:T(8,128)(2,1)}) custom-call(s32[2,27]{1,0:T(2,128)} %pad_add_fusion.1.info, bf16[4,256,576]{2,1,0:T(8,128)(2,1)} %get-tuple-element.26.q_hbm, bf16[4,576,256]{2,1,0:T(8,128)(2,1)} %bitcast.14, ...), custom_call_target="tpu_custom_call" | custom-call | tf_op jit(solution)/shard_map/pallas_call | solution.py:203
  50.5 0.0 copy-start.1
  50.5 0.5 collective-permute-start.10
  51.0 10.4 %all-to-all-start = ((bf16[16,4,16,576]{3,2,1,0:T(8,128)(2,1)}), bf16[16,4,16,576]{3,2,1,0:T(8,128)(2,1)}, u32[]{:S(2)}, u32[]{:S(2)}) async-start(bf16[16,4,16,576]{3,2,1,0:T(8,128)(2,1)} %get-tuple-element.34), calls=%async_computation | async-start | bytes 2621440 | tf_op jit(solution)/shard_map/all_to_all | solution.py:487
  61.4 0.0 collective-permute-done.10.got
  61.4 0.0 copy-done.1
  61.4 2.2 %shard_map.72 = (bf16[2,576,128]{2,1,0:T(8,128)(2,1)S(1)}, bf16[2,576,128]{2,1,0:T(8,128)(2,1)S(1)}, bf16[2,576,128]{2,1,0:T(8,128)(2,1)S(1)}, bf16[2,576,128]{2...) custom-call(bf16[16,576,128]{2,1,0:T(8,128)(2,1)S(1)} %copy-done.1, ...), custom_call_target="tpu_custom_call" | custom-call | tf_op jit(solution)/shard_map/pallas_call | solution.py:373
  63.6 0.7 collective-permute-start.11
  64.3 2.6 %collective-permute-start.12 = (bf16[2,576,128]{2,1,0:T(8,128)(2,1)S(1)}, bf16[2,576,128]{2,1,0:T(8,128)(2,1)S(1)}, u32[]{:S(2)}, u32[]{:S(2)}) collective-permute-start(bf16[2,576,128]{2,1,0:T(8,128)(2,1)S(1)} %get-tuple-element.41), channel_id=1, source_target_pairs={{0,96},{1,97},{2,98},{3,99},{4,100},{5,101},{6,102},{7,103},{8,104... | collective-permute-start | bytes 884744 | tf_op jit(solution)/shard_map/ppermute | solution.py:277
  66.9 0.8 collective-permute-start.14
  67.7 1.2 %collective-permute-start.15 = (bf16[2,576,128]{2,1,0:T(8,128)(2,1)S(1)}, bf16[2,576,128]{2,1,0:T(8,128)(2,1)S(1)}, u32[]{:S(2)}, u32[]{:S(2)}) collective-permute-start(bf16[2,576,128]{2,1,0:T(8,128)(2,1)S(1)} %get-tuple-element.44), channel_id=1, source_target_pairs={{0,32},{1,33},{2,34},{3,35},{4,36},{5,37},{6,38},{7,39},{8,40},{9,... | collective-permute-start | bytes 884744 | tf_op jit(solution)/shard_map/ppermute | solution.py:277
  68.9 5.9 %collective-permute-done.11.from_left = bf16[2,576,128]{2,1,0:T(8,128)(2,1)S(1)} collective-permute-done((bf16[2,576,128]{2,1,0:T(8,128)(2,1)S(1)}, bf16[2,576,128]{2,1,0:T(8,128)(2,1)S(1)}, u32[]{:S(2)}, u32[]{:S(2)}) %collective-permute-start.11) | collective-permute-done | bytes 294944 | tf_op jit(solution)/shard_map/ppermute | solution.py:277
  74.8 0.0 collective-permute-done.12.from_right
  74.8 0.1 shard_map.73
  75.0 0.3 collective-permute-start.13
  75.2 3.1 %collective-permute-start.16 = (bf16[2,576,128]{2,1,0:T(8,128)(2,1)S(1)}, bf16[2,576,128]{2,1,0:T(8,128)(2,1)S(1)}, u32[]{:S(2)}, u32[]{:S(2)}) collective-permute-start(bf16[2,576,128]{2,1,0:T(8,128)(2,1)S(1)} %get-tuple-element.45), channel_id=1, source_target_pairs={{0,96},{1,97},{2,98},{3,99},{4,100},{5,101},{6,102},{7,103},{8,104... | collective-permute-start | bytes 884744 | tf_op jit(solution)/shard_map/ppermute | solution.py:277
  78.4 2.3 %collective-permute-done.14.refs_1_ = bf16[2,576,128]{2,1,0:T(8,128)(2,1)S(1)} collective-permute-done((bf16[2,576,128]{2,1,0:T(8,128)(2,1)S(1)}, bf16[2,576,128]{2,1,0:T(8,128)(2,1)S(1)}, u32[]{:S(2)}, u32[]{:S(2)}) %collective-permute-start.14) | collective-permute-done | bytes 294944 | tf_op jit(solution)/shard_map/ppermute | solution.py:277
  80.7 0.4 collective-permute-done.15.refs_2_
  81.1 4.8 %collective-permute-done.13.refs_0_ = bf16[2,576,128]{2,1,0:T(8,128)(2,1)S(1)} collective-permute-done((bf16[2,576,128]{2,1,0:T(8,128)(2,1)S(1)}, bf16[2,576,128]{2,1,0:T(8,128)(2,1)S(1)}, u32[]{:S(2)}, u32[]{:S(2)}) %collective-permute-start.13) | collective-permute-done | bytes 294944 | tf_op jit(solution)/shard_map/ppermute | solution.py:277
  86.0 0.0 collective-permute-done.16.refs_3_
  86.0 0.5 shard_map.74
  86.5 1.5 %collective-permute-start.17 = (bf16[64,1152]{1,0:T(8,128)(2,1)S(1)}, bf16[64,1152]{1,0:T(8,128)(2,1)S(1)}, u32[]{:S(2)}, u32[]{:S(2)}) collective-permute-start(bf16[64,1152]{1,0:T(8,128)(2,1)S(1)} %get-tuple-element.47), channel_id=1, source_target_pairs={{0,4},{1,5},{2,6},{3,7},{4,8},{5,9},{6,10},{7,11},{8,12},{9,13},{1... | collective-permute-start | bytes 442376 | tf_op jit(solution)/shard_map/ppermute | solution.py:277
  88.0 1.0 collective-permute-start.18
  89.1 2.2 %collective-permute-start.19 = (bf16[64,1152]{1,0:T(8,128)(2,1)S(1)}, bf16[64,1152]{1,0:T(8,128)(2,1)S(1)}, u32[]{:S(2)}, u32[]{:S(2)}) collective-permute-start(bf16[64,1152]{1,0:T(8,128)(2,1)S(1)} %get-tuple-element.49), channel_id=1, source_target_pairs={{0,12},{1,13},{2,14},{3,15},{4,0},{5,1},{6,2},{7,3},{8,4},{9,5},{1... | collective-permute-start | bytes 442376 | tf_op jit(solution)/shard_map/ppermute | solution.py:277
  91.3 2.0 %collective-permute-done.17.refs_1_ = bf16[64,1152]{1,0:T(8,128)(2,1)S(1)} collective-permute-done((bf16[64,1152]{1,0:T(8,128)(2,1)S(1)}, bf16[64,1152]{1,0:T(8,128)(2,1)S(1)}, u32[]{:S(2)}, u32[]{:S(2)}) %collective-permute-start.17) | collective-permute-done | bytes 147488 | tf_op jit(solution)/shard_map/ppermute | solution.py:277
  93.3 2.1 %collective-permute-done.18.refs_2_ = bf16[64,1152]{1,0:T(8,128)(2,1)S(1)} collective-permute-done((bf16[64,1152]{1,0:T(8,128)(2,1)S(1)}, bf16[64,1152]{1,0:T(8,128)(2,1)S(1)}, u32[]{:S(2)}, u32[]{:S(2)}) %collective-permute-start.18) | collective-permute-done | bytes 147488 | tf_op jit(solution)/shard_map/ppermute | solution.py:277
  95.4 1.0 collective-permute-done.19.refs_3_
  96.4 0.8 shard_map.75
  97.1 0.0 all-to-all-done
  97.1 9.6 %all-to-all-start.1 = ((bf16[8,16,576]{2,1,0:T(8,128)(2,1)}), bf16[8,16,576]{2,1,0:T(8,128)(2,1)S(1)}, u32[]{:S(2)}, u32[]{:S(2)}) async-start(bf16[8,16,576]{2,1,0:T(8,128)(2,1)} %bitcast.6), calls=%async_computation.1 | async-start | bytes 327680 | tf_op jit(solution)/shard_map/all_to_all | solution.py:484
  106.7 2.7 %copy.9 = bf16[64,16,576]{2,0,1:T(8,128)(2,1)} copy(bf16[64,16,576]{2,1,0:T(8,128)(2,1)} %bitcast.3) | data formatting | bytes 2359296 | tf_op jit(solution)/shard_map/reshape | solution.py:488
  109.4 5.6 %all-to-all-done.1 = bf16[8,16,576]{2,1,0:T(8,128)(2,1)S(1)} async-done(((bf16[8,16,576]{2,1,0:T(8,128)(2,1)}), bf16[8,16,576]{2,1,0:T(8,128)(2,1)S(1)}, u32[]{:S(2)}, u32[]{:S(2)}) %all-to-all-start.1) | async-done | bytes 147488 | tf_op jit(solution)/shard_map/all_to_all | solution.py:484
  115.0 0.6 convert_reduce_fusion
  (5 shorter events, 0.0 us)
Async XLA Ops:
  0.6 28.0 %copy-start.2 = (bf16[256,576]{0,1:T(8,128)(2,1)S(1)}, bf16[256,576]{0,1:T(8,128)(2,1)}, u32[]{:S(2)}) copy-start(bf16[256,576]{0,1:T(8,128)(2,1)} %param.6) | copy-start | bytes 884740
  0.6 9.4 %collective-permute-start.1 = (bf16[576,256]{1,0:T(8,128)(2,1)}, bf16[576,256]{1,0:T(8,128)(2,1)S(1)}, u32[]{:S(2)}, u32[]{:S(2)}) collective-permute-start(bf16[576,256]{1,0:T(8,128)(2,1)} %bitcast.9), channel_id=1, source_target_pairs={{0,96},{1,97},{2,98},{3,99},{4,100},{5,101},{6,102},{7,103},{8,104... | collective-permute-start | bytes 884744 | tf_op jit(solution)/shard_map/ppermute | solution.py:277
  3.5 9.9 %collective-permute-start = (bf16[576,256]{1,0:T(8,128)(2,1)}, bf16[576,256]{1,0:T(8,128)(2,1)S(1)}, u32[]{:S(2)}, u32[]{:S(2)}) collective-permute-start(bf16[576,256]{1,0:T(8,128)(2,1)} %bitcast.10), channel_id=1, source_target_pairs={{0,32},{1,33},{2,34},{3,35},{4,36},{5,37},{6,38},{7,39},{8,40},{9,... | collective-permute-start | bytes 884744 | tf_op jit(solution)/shard_map/ppermute | solution.py:277
  3.5 14.6 %collective-permute-start.2 = (bf16[576,256]{1,0:T(8,128)(2,1)}, bf16[576,256]{1,0:T(8,128)(2,1)S(1)}, u32[]{:S(2)}, u32[]{:S(2)}) collective-permute-start(bf16[576,256]{1,0:T(8,128)(2,1)} %bitcast.11), channel_id=1, source_target_pairs={{0,128},{1,129},{2,130},{3,131},{4,132},{5,133},{6,134},{7,135},{8... | collective-permute-start | bytes 884744 | tf_op jit(solution)/shard_map/ppermute | solution.py:277
  13.4 0.7 copy-start.3
  14.2 8.9 %collective-permute-start.7 = (bf16[576,128]{1,0:T(8,128)(2,1)S(1)}, bf16[576,128]{1,0:T(8,128)(2,1)S(1)}, u32[]{:S(2)}, u32[]{:S(2)}) collective-permute-start(bf16[576,128]{1,0:T(8,128)(2,1)S(1)} %get-tuple-element.32), channel_id=1, source_target_pairs={{0,160},{1,161},{2,162},{3,163},{4,164},{5,165},{6,166},{7,167},{8... | collective-permute-start | bytes 442376 | tf_op jit(solution)/shard_map/ppermute | solution.py:277
  14.8 13.8 %collective-permute-start.5 = (bf16[576,256]{1,0:T(8,128)(2,1)S(1)}, bf16[576,256]{1,0:T(8,128)(2,1)S(1)}, u32[]{:S(2)}, u32[]{:S(2)}) collective-permute-start(bf16[576,256]{1,0:T(8,128)(2,1)S(1)} %get-tuple-element.30.refs_1_), channel_id=1, source_target_pairs={{0,131},{1,128},{2,129},{3,130},{4,135},{5,132},{6,133},{7,134},{8... | collective-permute-start | bytes 884744 | tf_op jit(solution)/shard_map/ppermute | solution.py:277
  14.9 13.7 %collective-permute-start.6 = (bf16[576,256]{1,0:T(8,128)(2,1)S(1)}, bf16[576,256]{1,0:T(8,128)(2,1)S(1)}, u32[]{:S(2)}, u32[]{:S(2)}) collective-permute-start(bf16[576,256]{1,0:T(8,128)(2,1)S(1)} %get-tuple-element.31.refs_2_), channel_id=1, source_target_pairs={{0,128},{1,129},{2,130},{3,131},{4,132},{5,133},{6,134},{7,135},{8... | collective-permute-start | bytes 884744 | tf_op jit(solution)/shard_map/ppermute | solution.py:277
  16.8 7.7 %collective-permute-start.3 = (bf16[576,128]{1,0:T(8,128)(2,1)S(1)}, bf16[576,128]{1,0:T(8,128)(2,1)S(1)}, u32[]{:S(2)}, u32[]{:S(2)}) collective-permute-start(bf16[576,128]{1,0:T(8,128)(2,1)S(1)} %get-tuple-element.32), channel_id=1, source_target_pairs={{0,32},{1,33},{2,34},{3,35},{4,36},{5,37},{6,38},{7,39},{8,40},{9,... | collective-permute-start | bytes 442376 | tf_op jit(solution)/shard_map/ppermute | solution.py:277
  18.1 11.9 %copy-start.4 = (s32[2,8]{1,0:T(2,128)S(1)}, s32[2,8]{1,0:T(2,128)}, u32[]{:S(2)}) copy-start(s32[2,8]{1,0:T(2,128)} %param.9) | copy-start | bytes 196
  18.1 8.3 %collective-permute-start.8 = (bf16[576,128]{1,0:T(8,128)(2,1)S(1)}, bf16[576,128]{1,0:T(8,128)(2,1)S(1)}, u32[]{:S(2)}, u32[]{:S(2)}) collective-permute-start(bf16[576,128]{1,0:T(8,128)(2,1)S(1)} %get-tuple-element.33), channel_id=1, source_target_pairs={{0,227},{1,224},{2,225},{3,226},{4,231},{5,228},{6,229},{7,230},{8... | collective-permute-start | bytes 442376 | tf_op jit(solution)/shard_map/ppermute | solution.py:277
  23.1 5.5 %collective-permute-start.4 = (bf16[576,128]{1,0:T(8,128)(2,1)S(1)}, bf16[576,128]{1,0:T(8,128)(2,1)S(1)}, u32[]{:S(2)}, u32[]{:S(2)}) collective-permute-start(bf16[576,128]{1,0:T(8,128)(2,1)S(1)} %get-tuple-element.33), channel_id=1, source_target_pairs={{0,96},{1,97},{2,98},{3,99},{4,100},{5,101},{6,102},{7,103},{8,104... | collective-permute-start | bytes 442376 | tf_op jit(solution)/shard_map/ppermute | solution.py:277
  29.7 4.9 %copy-start = (bf16[16,576,128]{2,1,0:T(8,128)(2,1)}, bf16[16,576,128]{2,1,0:T(8,128)(2,1)S(1)}, u32[]{:S(2)}) copy-start(bf16[16,576,128]{2,1,0:T(8,128)(2,1)S(1)} %shard_map.70.rest_0_) | copy-start | bytes 7077892
  29.7 4.9 %collective-permute-start.9 = (bf16[16,576,128]{2,1,0:T(8,128)(2,1)S(1)}, bf16[16,576,128]{2,1,0:T(8,128)(2,1)}, u32[]{:S(2)}, u32[]{:S(2)}) collective-permute-start(bf16[16,576,128]{2,1,0:T(8,128)(2,1)S(1)} %shard_map.70.rest_0_), channel_id=1, source_target_pairs={{0,16},{1,17},{2,18},{3,19},{4,20},{5,21},{6,22},{7,23},{8,24},{9,... | collective-permute-start | bytes 7077896 | tf_op jit(solution)/shard_map/ppermute | solution.py:277
  50.5 10.9 %copy-start.1 = (bf16[16,576,128]{2,1,0:T(8,128)(2,1)S(1)}, bf16[16,576,128]{2,1,0:T(8,128)(2,1)}, u32[]{:S(2)}) copy-start(bf16[16,576,128]{2,1,0:T(8,128)(2,1)} %get-tuple-element.35.keep) | copy-start | bytes 7077892
  50.5 10.9 %collective-permute-start.10 = (bf16[16,576,128]{2,1,0:T(8,128)(2,1)}, bf16[16,576,128]{2,1,0:T(8,128)(2,1)}, u32[]{:S(2)}, u32[]{:S(2)}) collective-permute-start(bf16[16,576,128]{2,1,0:T(8,128)(2,1)} %get-tuple-element.36), channel_id=1, source_target_pairs={{0,16},{1,17},{2,18},{3,19},{4,20},{5,21},{6,22},{7,23},{8,24},{9,... | collective-permute-start | bytes 7077896 | tf_op jit(solution)/shard_map/ppermute | solution.py:277
  51.0 46.2 %all-to-all-start = ((bf16[16,4,16,576]{3,2,1,0:T(8,128)(2,1)}), bf16[16,4,16,576]{3,2,1,0:T(8,128)(2,1)}, u32[]{:S(2)}, u32[]{:S(2)}) async-start(bf16[16,4,16,576]{3,2,1,0:T(8,128)(2,1)} %get-tuple-element.34), calls=%async_computation | async-start | bytes 2621440 | tf_op jit(solution)/shard_map/all_to_all | solution.py:487
  63.6 11.2 %collective-permute-start.11 = (bf16[2,576,128]{2,1,0:T(8,128)(2,1)S(1)}, bf16[2,576,128]{2,1,0:T(8,128)(2,1)S(1)}, u32[]{:S(2)}, u32[]{:S(2)}) collective-permute-start(bf16[2,576,128]{2,1,0:T(8,128)(2,1)S(1)} %get-tuple-element.39), channel_id=1, source_target_pairs={{0,32},{1,33},{2,34},{3,35},{4,36},{5,37},{6,38},{7,39},{8,40},{9,... | collective-permute-start | bytes 884744 | tf_op jit(solution)/shard_map/ppermute | solution.py:277
  64.3 10.5 %collective-permute-start.12 = (bf16[2,576,128]{2,1,0:T(8,128)(2,1)S(1)}, bf16[2,576,128]{2,1,0:T(8,128)(2,1)S(1)}, u32[]{:S(2)}, u32[]{:S(2)}) collective-permute-start(bf16[2,576,128]{2,1,0:T(8,128)(2,1)S(1)} %get-tuple-element.41), channel_id=1, source_target_pairs={{0,96},{1,97},{2,98},{3,99},{4,100},{5,101},{6,102},{7,103},{8,104... | collective-permute-start | bytes 884744 | tf_op jit(solution)/shard_map/ppermute | solution.py:277
  66.9 13.8 %collective-permute-start.14 = (bf16[2,576,128]{2,1,0:T(8,128)(2,1)S(1)}, bf16[2,576,128]{2,1,0:T(8,128)(2,1)S(1)}, u32[]{:S(2)}, u32[]{:S(2)}) collective-permute-start(bf16[2,576,128]{2,1,0:T(8,128)(2,1)S(1)} %get-tuple-element.43), channel_id=1, source_target_pairs={{0,96},{1,97},{2,98},{3,99},{4,100},{5,101},{6,102},{7,103},{8,104... | collective-permute-start | bytes 884744 | tf_op jit(solution)/shard_map/ppermute | solution.py:277
  67.7 13.5 %collective-permute-start.15 = (bf16[2,576,128]{2,1,0:T(8,128)(2,1)S(1)}, bf16[2,576,128]{2,1,0:T(8,128)(2,1)S(1)}, u32[]{:S(2)}, u32[]{:S(2)}) collective-permute-start(bf16[2,576,128]{2,1,0:T(8,128)(2,1)S(1)} %get-tuple-element.44), channel_id=1, source_target_pairs={{0,32},{1,33},{2,34},{3,35},{4,36},{5,37},{6,38},{7,39},{8,40},{9,... | collective-permute-start | bytes 884744 | tf_op jit(solution)/shard_map/ppermute | solution.py:277
  75.0 11.0 %collective-permute-start.13 = (bf16[2,576,128]{2,1,0:T(8,128)(2,1)S(1)}, bf16[2,576,128]{2,1,0:T(8,128)(2,1)S(1)}, u32[]{:S(2)}, u32[]{:S(2)}) collective-permute-start(bf16[2,576,128]{2,1,0:T(8,128)(2,1)S(1)} %get-tuple-element.42), channel_id=1, source_target_pairs={{0,32},{1,33},{2,34},{3,35},{4,36},{5,37},{6,38},{7,39},{8,40},{9,... | collective-permute-start | bytes 884744 | tf_op jit(solution)/shard_map/ppermute | solution.py:277
  75.2 10.8 %collective-permute-start.16 = (bf16[2,576,128]{2,1,0:T(8,128)(2,1)S(1)}, bf16[2,576,128]{2,1,0:T(8,128)(2,1)S(1)}, u32[]{:S(2)}, u32[]{:S(2)}) collective-permute-start(bf16[2,576,128]{2,1,0:T(8,128)(2,1)S(1)} %get-tuple-element.45), channel_id=1, source_target_pairs={{0,96},{1,97},{2,98},{3,99},{4,100},{5,101},{6,102},{7,103},{8,104... | collective-permute-start | bytes 884744 | tf_op jit(solution)/shard_map/ppermute | solution.py:277
  86.5 6.8 %collective-permute-start.17 = (bf16[64,1152]{1,0:T(8,128)(2,1)S(1)}, bf16[64,1152]{1,0:T(8,128)(2,1)S(1)}, u32[]{:S(2)}, u32[]{:S(2)}) collective-permute-start(bf16[64,1152]{1,0:T(8,128)(2,1)S(1)} %get-tuple-element.47), channel_id=1, source_target_pairs={{0,4},{1,5},{2,6},{3,7},{4,8},{5,9},{6,10},{7,11},{8,12},{9,13},{1... | collective-permute-start | bytes 442376 | tf_op jit(solution)/shard_map/ppermute | solution.py:277
  88.0 7.3 %collective-permute-start.18 = (bf16[64,1152]{1,0:T(8,128)(2,1)S(1)}, bf16[64,1152]{1,0:T(8,128)(2,1)S(1)}, u32[]{:S(2)}, u32[]{:S(2)}) collective-permute-start(bf16[64,1152]{1,0:T(8,128)(2,1)S(1)} %get-tuple-element.48), channel_id=1, source_target_pairs={{0,8},{1,9},{2,10},{3,11},{4,12},{5,13},{6,14},{7,15},{8,0},{9,1},... | collective-permute-start | bytes 442376 | tf_op jit(solution)/shard_map/ppermute | solution.py:277
  89.1 7.3 %collective-permute-start.19 = (bf16[64,1152]{1,0:T(8,128)(2,1)S(1)}, bf16[64,1152]{1,0:T(8,128)(2,1)S(1)}, u32[]{:S(2)}, u32[]{:S(2)}) collective-permute-start(bf16[64,1152]{1,0:T(8,128)(2,1)S(1)} %get-tuple-element.49), channel_id=1, source_target_pairs={{0,12},{1,13},{2,14},{3,15},{4,0},{5,1},{6,2},{7,3},{8,4},{9,5},{1... | collective-permute-start | bytes 442376 | tf_op jit(solution)/shard_map/ppermute | solution.py:277
  97.1 17.8 %all-to-all-start.1 = ((bf16[8,16,576]{2,1,0:T(8,128)(2,1)}), bf16[8,16,576]{2,1,0:T(8,128)(2,1)S(1)}, u32[]{:S(2)}, u32[]{:S(2)}) async-start(bf16[8,16,576]{2,1,0:T(8,128)(2,1)} %bitcast.6), calls=%async_computation.1 | async-start | bytes 327680 | tf_op jit(solution)/shard_map/all_to_all | solution.py:484
